TPU v7x, 32 devices: a whole 2x2x4 slice. The times are simulated.
32 devices in a mesh: outer: 4 (over z), inner: 8 (over y, x, core).
Axes of the slice: x: 2, y: 2, z: 4, core: 2. Of those that a mesh axis runs over, the one named last changes fastest.
Arguments:
- target: bfloat16 [32768, 1024], P(('outer', 'inner')), may hold values from -6 to 6
- memory: bfloat16 [16384, 1024], P(('outer', 'inner')), may hold values from -6 to 6
- cotangent: bfloat16 [32768, 1024], P(('outer', 'inner')), may hold values from -6 to 6
- segment_ids: int32 [32, 1024], P(('outer', 'inner')), may hold values from 0 to 7, never falling along the last dimension, each value on 1 to 256 neighbouring positions
- memory_segments: int32 [32, 512], P(('outer', 'inner')), may hold values from 0 to 7, never falling along the last dimension, each value on 1 to 128 neighbouring positions
- directions: int32 [32, 8], P(('outer', 'inner')), may hold values from 0 to 15
- lang_table: bfloat16 [1024, 16], P(('outer', 'inner')), may hold values from -3 to 3
- self_qkv: bfloat16 [1024, 3072], P('inner', 'outer'), may hold values from -0.1875 to 0.1875
- self_out: bfloat16 [1024, 1024], P('inner', 'outer'), may hold values from -1.5 to 1.5
- cross_q: bfloat16 [1024, 1024], P('inner', 'outer'), may hold values from -0.1875 to 0.1875
- cross_kv: bfloat16 [1024, 2048], P('inner', 'outer'), may hold values from -0.1875 to 0.1875
- cross_out: bfloat16 [1024, 1024], P('inner', 'outer'), may hold values from -1.5 to 1.5
- ffn_in: bfloat16 [1024, 4096], P('inner', 'outer'), may hold values from -0.1875 to 0.1875
- ffn_in_bias: bfloat16 [4096], P(('outer', 'inner')), may hold values from -2 to 2
- ffn_out: bfloat16 [4096, 1024], P(('outer', 'inner')), may hold values from -0.09375 to 0.09375
- ffn_out_bias: bfloat16 [1024], P(('outer', 'inner')), may hold values from -2 to 2
- norm_gains: bfloat16 [1024, 3], P(('outer', 'inner')), may hold values from 0.5 to 1.5
- norm_biases: bfloat16 [1024, 3], P(('outer', 'inner')), may hold values from -2 to 2
Outputs:
- layer_output: bfloat16 [32768, 1024], P(('outer', 'inner'))
- target_grad: float32 [32768, 1024], P(('outer', 'inner'))
- memory_grad: float32 [16384, 1024], P(('outer', 'inner'))
- lang_table_grad: float32 [1024, 16], P(('outer', 'inner'))
- self_qkv_grad: float32 [1024, 3072], P('inner', 'outer')
- self_out_grad: float32 [1024, 1024], P('inner', 'outer')
- cross_q_grad: float32 [1024, 1024], P('inner', 'outer')
- cross_kv_grad: float32 [1024, 2048], P('inner', 'outer')
- cross_out_grad: float32 [1024, 1024], P('inner', 'outer')
- ffn_in_grad: float32 [1024, 4096], P('inner', 'outer')
- ffn_in_bias_grad: float32 [4096], P(('outer', 'inner'))
- ffn_out_grad: float32 [4096, 1024], P(('outer', 'inner'))
- ffn_out_bias_grad: float32 [1024], P(('outer', 'inner'))
- norm_gains_grad: float32 [1024, 3], P(('outer', 'inner'))
- norm_biases_grad: float32 [1024, 3], P(('outer', 'inner'))
Inputs may be any that keep to these rules, and one draw needn't show every extreme that they name: `segment_ids`: along each row the ids never fall and every id of 0 to 7 occurs, at most 1024 / 4 times, exactly that often for one of them. `memory_segments`: along each row the ids never fall and every id of 0 to 7 occurs, at most 512 / 4 times, exactly that often for one of them.
All inputs are finite; a program needn't handle non-finite values.
Results may differ from a plain program's by a relative error of at most 0.017.
The roundings to bfloat16 on the way count: a program that leaves them out, or rounds other values in their place, can miss the bound.
Values may be sent and summed in bfloat16 or wider, within the bound.
No kernel may reach another device: no remote copies, remote signals or barrier semaphores. Data moves between devices by JAX's collectives and lax.ppermute only.
A program may use at most 256 MiB of HBM per device.

v0:
```python
import jax
import jax.numpy as jnp
from jax import lax
from jax.sharding import PartitionSpec as P

HEADS = 16
HEAD_DIM = 64


epsilon = 1e-05
residual_scale = 2.0
masked_score = -1000000000.0
highest = lax.Precision.HIGHEST
split_both = (False, True, True, True, True, True, True, False, False, False, False, False)


def layer_norm(matrix, gain_vec, shift_vec):
    row_mean = jnp.mean(matrix, axis=-1, keepdims=True)
    centred = matrix - row_mean
    row_var = jnp.mean(centred * centred, axis=-1, keepdims=True)
    return centred * lax.rsqrt(row_var + epsilon) * gain_vec + shift_vec


def norm_section(residual, branch, gain_vec, shift_vec):
    return layer_norm(residual_scale * residual + branch, gain_vec, shift_vec)


def smooth(hidden_pre):
    return jax.nn.gelu(hidden_pre, approximate=False)


def project(left_side, right_side):
    return jnp.dot(left_side, right_side, preferred_element_type=jnp.float32)


def transposed_left(left_side, right_side):
    return lax.dot_general(
        left_side, right_side, (((0,), (0,)), ((), ())), preferred_element_type=jnp.float32
    )


def transposed_right(left_side, right_side):
    return lax.dot_general(
        left_side, right_side, (((1,), (1,)), ((), ())), preferred_element_type=jnp.float32
    )


def split_heads(matrix, row_count):
    length = matrix.shape[0] // row_count
    head_count = matrix.shape[1] // HEAD_DIM
    shaped = matrix.reshape(row_count, length, head_count, HEAD_DIM).transpose(0, 2, 1, 3)
    return shaped.reshape(row_count * head_count, length, HEAD_DIM)


def join_heads(stacked, row_count):
    item_count, length, head_width = stacked.shape
    head_count = item_count // row_count
    shaped = stacked.reshape(row_count, head_count, length, head_width).transpose(0, 2, 1, 3)
    return shaped.reshape(row_count * length, head_count * head_width)


def masked_scores(query_block, key_block, own_ids, other_ids, causal):
    raw_scores = transposed_right(query_block, key_block) * HEAD_DIM ** (-0.5)
    allowed = own_ids[:, None] == other_ids[None, :]
    if causal:
        positions = jnp.arange(query_block.shape[0])
        allowed = allowed & (positions[:, None] >= positions[None, :])
    return jnp.where(allowed, raw_scores, masked_score)


def attention_forward(queries, keys_all, values_all, own_ids, other_ids, causal):

    def one_item(item_tuple):
        query_block, key_block, value_block, mine_ids, their_ids = item_tuple
        scores = masked_scores(query_block, key_block, mine_ids, their_ids, causal)
        row_max = jnp.max(scores, axis=-1, keepdims=True)
        exps = jnp.exp(scores - row_max)
        row_total = jnp.sum(exps, axis=-1, keepdims=True)
        attn_probs = (exps / row_total).astype(jnp.bfloat16)
        return (project(attn_probs, value_block), (row_max + jnp.log(row_total))[:, 0])

    return lax.map(one_item, (queries, keys_all, values_all, own_ids, other_ids))


def attention_backward(
    queries, keys_all, values_all, own_ids, other_ids, causal, levels, grads_mix
):

    def one_item(item_tuple):
        query_block, key_block, value_block, mine_ids, their_ids, row_level, grad_block = item_tuple
        scores = masked_scores(query_block, key_block, mine_ids, their_ids, causal)
        attn_probs = jnp.exp(scores - row_level[:, None])
        rounded = attn_probs.astype(jnp.bfloat16)
        grad_probs = transposed_right(grad_block, value_block)
        grad_value = transposed_left(rounded, grad_block)
        row_inner = jnp.sum(attn_probs * grad_probs, axis=-1, keepdims=True)
        grad_scores = (attn_probs * (grad_probs - row_inner)).astype(jnp.bfloat16)
        scaled = grad_scores * HEAD_DIM ** (-0.5)
        grad_query = project(scaled, key_block)
        grad_key = transposed_left(scaled, query_block)
        return (grad_query, grad_key, grad_value)

    return lax.map(one_item, (queries, keys_all, values_all, own_ids, other_ids, levels, grads_mix))


def flat_restore(stacked, outer_count):
    total_rows, piece_cols = stacked.shape
    shaped = stacked.reshape(outer_count, total_rows // outer_count, piece_cols)
    return shaped.transpose(1, 0, 2).reshape(total_rows // outer_count, outer_count * piece_cols)


def flat_arrange(grad_full, outer_count, inner_count):
    full_rows, full_cols = grad_full.shape
    piece_rows = full_rows // inner_count
    piece_cols = full_cols // outer_count
    shaped = grad_full.reshape(inner_count, piece_rows, outer_count, piece_cols).transpose(
        2, 0, 1, 3
    )
    return shaped.reshape(outer_count * inner_count * piece_rows, piece_cols)


def restore_all(gathered, outer_count):
    return tuple(
        (
            flat_restore(item, outer_count) if flag else item
            for item, flag in zip(gathered, split_both)
        )
    )


def per_device(
    target,
    memory,
    cotangent,
    segment_ids,
    memory_segments,
    directions,
    lang_table,
    self_qkv,
    self_out,
    cross_q,
    cross_kv,
    cross_out,
    ffn_in,
    ffn_in_bias,
    ffn_out,
    ffn_out_bias,
    norm_gains,
    norm_biases,
):
    outer_count = lax.axis_size("outer")
    inner_count = lax.axis_size("inner")
    gathered = restore_all(
        (
            lax.all_gather(lang_table, ("outer", "inner"), axis=0, tiled=True),
            lax.all_gather(self_qkv, ("outer", "inner"), axis=0, tiled=True),
            lax.all_gather(self_out, ("outer", "inner"), axis=0, tiled=True),
            lax.all_gather(cross_q, ("outer", "inner"), axis=0, tiled=True),
            lax.all_gather(cross_kv, ("outer", "inner"), axis=0, tiled=True),
            lax.all_gather(cross_out, ("outer", "inner"), axis=0, tiled=True),
            lax.all_gather(ffn_in, ("outer", "inner"), axis=0, tiled=True),
            lax.all_gather(ffn_in_bias, ("outer", "inner"), axis=0, tiled=True),
            lax.all_gather(ffn_out, ("outer", "inner"), axis=0, tiled=True),
            lax.all_gather(ffn_out_bias, ("outer", "inner"), axis=0, tiled=True),
            lax.all_gather(norm_gains, ("outer", "inner"), axis=0, tiled=True),
            lax.all_gather(norm_biases, ("outer", "inner"), axis=0, tiled=True),
        ),
        outer_count,
    )
    (
        lang_full,
        triple_full,
        merge_full,
        cross_query,
        cross_pair,
        cross_merge,
        expand_full,
        expand_bias,
        shrink_full,
        shrink_bias,
        gain_full,
        shift_full,
    ) = gathered
    row_count = segment_ids.shape[0]
    model_width = target.shape[1]
    gains = gain_full.astype(jnp.float32)
    shifts = shift_full.astype(jnp.float32)
    selector = segment_ids[:, :, None] == jnp.arange(directions.shape[1])[None, None, :]
    token_dir = jnp.sum(jnp.where(selector, directions[:, None, :], 0), axis=-1).reshape(-1)
    lang_hot = (token_dir[:, None] == jnp.arange(lang_full.shape[1])[None, :]).astype(jnp.float32)
    start = target.astype(jnp.float32) + lax.dot_general(
        lang_hot, lang_full.astype(jnp.float32), (((1,), (1,)), ((), ())), precision=highest
    )
    own_rep = jnp.repeat(segment_ids, HEADS, axis=0)
    memory_rep = jnp.repeat(memory_segments, HEADS, axis=0)
    self_entry = start.astype(jnp.bfloat16)
    triple = project(self_entry, triple_full).astype(jnp.bfloat16)
    self_queries = split_heads(triple[:, :model_width], row_count)
    self_keys = split_heads(triple[:, model_width : 2 * model_width], row_count)
    self_values = split_heads(triple[:, 2 * model_width :], row_count)
    self_heads, self_levels = attention_forward(
        self_queries, self_keys, self_values, own_rep, own_rep, True
    )
    self_mix = join_heads(self_heads, row_count).astype(jnp.bfloat16)
    self_branch = project(self_mix, merge_full)
    first = norm_section(start, self_branch, gains[:, 0], shifts[:, 0])
    cross_entry = first.astype(jnp.bfloat16)
    cross_queries = project(cross_entry, cross_query).astype(jnp.bfloat16)
    cross_pairs = project(memory, cross_pair).astype(jnp.bfloat16)
    cross_heads_q = split_heads(cross_queries, row_count)
    cross_keys = split_heads(cross_pairs[:, :model_width], row_count)
    cross_values = split_heads(cross_pairs[:, model_width:], row_count)
    cross_heads, cross_levels = attention_forward(
        cross_heads_q, cross_keys, cross_values, own_rep, memory_rep, False
    )
    cross_mix = join_heads(cross_heads, row_count).astype(jnp.bfloat16)
    cross_branch = project(cross_mix, cross_merge)
    second = norm_section(first, cross_branch, gains[:, 1], shifts[:, 1])
    ffn_entry = second.astype(jnp.bfloat16)
    hidden_pre = project(ffn_entry, expand_full) + expand_bias.astype(jnp.float32)
    hidden_act = smooth(hidden_pre).astype(jnp.bfloat16)
    ffn_branch = project(hidden_act, shrink_full) + shrink_bias.astype(jnp.float32)
    final = norm_section(second, ffn_branch, gains[:, 2], shifts[:, 2])
    refetched = restore_all(
        (
            lax.all_gather(lang_table, ("outer", "inner"), axis=0, tiled=True),
            lax.all_gather(self_qkv, ("outer", "inner"), axis=0, tiled=True),
            lax.all_gather(self_out, ("outer", "inner"), axis=0, tiled=True),
            lax.all_gather(cross_q, ("outer", "inner"), axis=0, tiled=True),
            lax.all_gather(cross_kv, ("outer", "inner"), axis=0, tiled=True),
            lax.all_gather(cross_out, ("outer", "inner"), axis=0, tiled=True),
            lax.all_gather(ffn_in, ("outer", "inner"), axis=0, tiled=True),
            lax.all_gather(ffn_in_bias, ("outer", "inner"), axis=0, tiled=True),
            lax.all_gather(ffn_out, ("outer", "inner"), axis=0, tiled=True),
            lax.all_gather(ffn_out_bias, ("outer", "inner"), axis=0, tiled=True),
            lax.all_gather(norm_gains, ("outer", "inner"), axis=0, tiled=True),
            lax.all_gather(norm_biases, ("outer", "inner"), axis=0, tiled=True),
        ),
        outer_count,
    )
    triple_back = refetched[1]
    merge_back = refetched[2]
    query_back = refetched[3]
    pair_back = refetched[4]
    cross_merge_back = refetched[5]
    expand_back = refetched[6]
    shrink_back = refetched[8]
    gains_back = refetched[10].astype(jnp.float32)
    grad_final = cotangent.astype(jnp.float32)
    _, pull_last = jax.vjp(norm_section, second, ffn_branch, gains_back[:, 2], shifts[:, 2])
    back_second, back_ffn, gain_last, shift_last = pull_last(grad_final)
    back_ffn = back_ffn.astype(jnp.bfloat16)
    grad_shrink = transposed_left(hidden_act, back_ffn)
    grad_shrink_bias = jnp.sum(back_ffn.astype(jnp.float32), axis=0)
    back_act = transposed_right(back_ffn, shrink_back)
    _, pull_smooth = jax.vjp(smooth, hidden_pre)
    back_pre = pull_smooth(back_act)[0].astype(jnp.bfloat16)
    grad_expand = transposed_left(ffn_entry, back_pre)
    grad_expand_bias = jnp.sum(back_pre.astype(jnp.float32), axis=0)
    back_second = back_second + transposed_right(back_pre, expand_back)
    _, pull_cross = jax.vjp(norm_section, first, cross_branch, gains_back[:, 1], shifts[:, 1])
    back_first, back_cross, gain_cross, shift_cross = pull_cross(back_second)
    back_cross = back_cross.astype(jnp.bfloat16)
    grad_cross_merge = transposed_left(cross_mix, back_cross)
    back_cross_mix = transposed_right(back_cross, cross_merge_back).astype(jnp.bfloat16)
    cross_dq, cross_dk, cross_dv = attention_backward(
        cross_heads_q,
        cross_keys,
        cross_values,
        own_rep,
        memory_rep,
        False,
        cross_levels,
        split_heads(back_cross_mix, row_count),
    )
    back_cross_q = join_heads(cross_dq, row_count).astype(jnp.bfloat16)
    back_pairs = jnp.concatenate(
        [join_heads(cross_dk, row_count), join_heads(cross_dv, row_count)], axis=1
    ).astype(jnp.bfloat16)
    grad_cross_query = transposed_left(cross_entry, back_cross_q)
    grad_cross_pair = transposed_left(memory, back_pairs)
    back_memory = transposed_right(back_pairs, pair_back)
    back_first = back_first + transposed_right(back_cross_q, query_back)
    _, pull_self = jax.vjp(norm_section, start, self_branch, gains_back[:, 0], shifts[:, 0])
    back_start, back_self, gain_self, shift_self = pull_self(back_first)
    back_self = back_self.astype(jnp.bfloat16)
    grad_merge = transposed_left(self_mix, back_self)
    back_self_mix = transposed_right(back_self, merge_back).astype(jnp.bfloat16)
    self_dq, self_dk, self_dv = attention_backward(
        self_queries,
        self_keys,
        self_values,
        own_rep,
        own_rep,
        True,
        self_levels,
        split_heads(back_self_mix, row_count),
    )
    back_triple = jnp.concatenate(
        [
            join_heads(self_dq, row_count),
            join_heads(self_dk, row_count),
            join_heads(self_dv, row_count),
        ],
        axis=1,
    ).astype(jnp.bfloat16)
    grad_triple = transposed_left(self_entry, back_triple)
    back_start = back_start + transposed_right(back_triple, triple_back)
    grad_lang = lax.dot_general(back_start, lang_hot, (((0,), (0,)), ((), ())), precision=highest)
    grad_gains = jnp.stack([gain_self, gain_cross, gain_last], axis=1)
    grad_shifts = jnp.stack([shift_self, shift_cross, shift_last], axis=1)
    grad_list = (
        grad_lang,
        grad_triple,
        grad_merge,
        grad_cross_query,
        grad_cross_pair,
        grad_cross_merge,
        grad_expand,
        grad_expand_bias,
        grad_shrink,
        grad_shrink_bias,
        grad_gains,
        grad_shifts,
    )
    arranged = [
        flat_arrange(grad_item, outer_count, inner_count) if flag else grad_item
        for grad_item, flag in zip(grad_list, split_both)
    ]
    summed = (
        lax.psum_scatter(arranged[0], ("outer", "inner"), scatter_dimension=0, tiled=True),
        lax.psum_scatter(arranged[1], ("outer", "inner"), scatter_dimension=0, tiled=True),
        lax.psum_scatter(arranged[2], ("outer", "inner"), scatter_dimension=0, tiled=True),
        lax.psum_scatter(arranged[3], ("outer", "inner"), scatter_dimension=0, tiled=True),
        lax.psum_scatter(arranged[4], ("outer", "inner"), scatter_dimension=0, tiled=True),
        lax.psum_scatter(arranged[5], ("outer", "inner"), scatter_dimension=0, tiled=True),
        lax.psum_scatter(arranged[6], ("outer", "inner"), scatter_dimension=0, tiled=True),
        lax.psum_scatter(arranged[7], ("outer", "inner"), scatter_dimension=0, tiled=True),
        lax.psum_scatter(arranged[8], ("outer", "inner"), scatter_dimension=0, tiled=True),
        lax.psum_scatter(arranged[9], ("outer", "inner"), scatter_dimension=0, tiled=True),
        lax.psum_scatter(arranged[10], ("outer", "inner"), scatter_dimension=0, tiled=True),
        lax.psum_scatter(arranged[11], ("outer", "inner"), scatter_dimension=0, tiled=True),
    )
    return (
        final.astype(jnp.bfloat16),
        back_start,
        back_memory,
        summed[0],
        summed[1],
        summed[2],
        summed[3],
        summed[4],
        summed[5],
        summed[6],
        summed[7],
        summed[8],
        summed[9],
        summed[10],
        summed[11],
    )


def solution(mesh):
    placed = (
        P(("outer", "inner"), None),
        P(("outer", "inner"), None),
        P(("outer", "inner"), None),
        P(("outer", "inner"), None),
        P(("outer", "inner"), None),
        P(("outer", "inner"), None),
        P(("outer", "inner"), None),
        P("inner", "outer"),
        P("inner", "outer"),
        P("inner", "outer"),
        P("inner", "outer"),
        P("inner", "outer"),
        P("inner", "outer"),
        P(("outer", "inner")),
        P(("outer", "inner"), None),
        P(("outer", "inner")),
        P(("outer", "inner"), None),
        P(("outer", "inner"), None),
    )
    return jax.shard_map(
        per_device,
        mesh=mesh,
        in_specs=placed,
        out_specs=(
            P(("outer", "inner"), None),
            P(("outer", "inner"), None),
            P(("outer", "inner"), None),
            P(("outer", "inner"), None),
            P("inner", "outer"),
            P("inner", "outer"),
            P("inner", "outer"),
            P("inner", "outer"),
            P("inner", "outer"),
            P("inner", "outer"),
            P(("outer", "inner")),
            P(("outer", "inner"), None),
            P(("outer", "inner")),
            P(("outer", "inner"), None),
            P(("outer", "inner"), None),
        ),
        check_vma=False,
    )
```

profile of v0, /device:TPU:0, one launch (start us, length us, event | category | flops | bytes accessed | tf_op | source)
XLA Modules:
  0.0 2521.0 jit_solution(4844705448704641207)
XLA Ops:
  12.0 43.9 %all-gather = bf16[32,32,16]{1,2,0:T(8,128)(2,1)S(1)} all-gather(bf16[1,32,16]{1,2,0:T(8,128)(2,1)} %bitcast.516), channel_id=1, replica_groups=mesh['outer'=4,'inner'=8] {'outer','inner'}, dimensions={0}, use_global_device_ids=true | all-gather | bytes 33792 | tf_op jit(solution)/shard_map/all_gather | solution.py:155
  56.1 4.0 copy.195
  60.1 36.7 %all-gather.1 = bf16[32,32,3]{1,2,0:T(4,128)(2,1)S(1)} all-gather(bf16[1,32,3]{1,2,0:T(4,128)(2,1)S(1)} %bitcast.522), channel_id=1, replica_groups=mesh['outer'=4,'inner'=8] {'outer','inner'}, dimensions={0}, use_global_device_ids=true | all-gather | bytes 6336 | tf_op jit(solution)/shard_map/all_gather | solution.py:165
  97.5 38.1 %all-gather.2 = bf16[32,32,3]{1,2,0:T(4,128)(2,1)S(1)} all-gather(bf16[1,32,3]{1,2,0:T(4,128)(2,1)S(1)} %bitcast.523), channel_id=1, replica_groups=mesh['outer'=4,'inner'=8] {'outer','inner'}, dimensions={0}, use_global_device_ids=true | all-gather | bytes 6336 | tf_op jit(solution)/shard_map/all_gather | solution.py:166
  136.4 36.4 %all-gather.3 = bf16[32,1,128]{2,1,0:T(2,128)(2,1)S(1)} all-gather(bf16[1,1,128]{2,1,0:T(2,128)(2,1)S(1)} %bitcast.524), channel_id=1, replica_groups=mesh['outer'=4,'inner'=8] {'outer','inner'}, dimensions={0}, use_global_device_ids=true | all-gather | bytes 8448 | tf_op jit(solution)/shard_map/all_gather | solution.py:162
  173.1 37.4 %all-reduce = bf16[1024]{0:T(1024)(128)(2,1)S(1)} all-reduce(bf16[1024]{0:T(1024)(128)(2,1)S(1)} %dynamic-update-slice), channel_id=1, replica_groups=mesh['outer'=4,'inner'=8] {'outer','inner'}, use_global_device_ids=true, to_apply=%add | all-reduce | flops 1024 | bytes 4096
  216.6 4.0 copy.204
  220.5 4.0 copy.207
  224.5 3.9 copy.214
  228.4 22.3 all-gather.18.cloned.1.call-done
  250.7 6.3 copy.209
  257.0 4.6 convolution_convert_fusion.1
  268.4 53.2 %all-gather.12.cloned.1.call-done = bf16[4096,768]{1,0:T(8,128)(2,1)} async-done(((bf16[128,768]{1,0:T(8,128)(2,1)}), bf16[4096,768]{1,0:T(8,128)(2,1)}) %all-gather.12.cloned.1.call-update) | async-done | bytes 6291472 | tf_op jit(solution)/shard_map/all_gather | solution.py:156
  321.5 8.9 copy.197
  330.4 10.3 convolution_convert_fusion
  346.4 3.2 copy.201
  352.4 3.6 copy.202
  358.9 3.2 copy.203
  362.4 126.4 %while.52 = (s32[]{:T(128)}, bf16[16,1024,64]{1,2,0:T(8,128)(2,1)S(1)}, f32[16,1024]{1,0:T(8,128)S(1)}, s32[16,1024]{1,0:T(8,128)S(1)}, bf16[16,1024,64]{2,1,0:T...) while((s32[]{:T(128)}, ...), condition=%wide.region_4.5_spmd, body=%wide.region_1.4_spmd.sunk | while | flops 279968768 | bytes 30468224 | solution.py:82
  375.2 3.1 fusion.207
  438.2 3.1 fusion.207
  488.8 6.7 fusion.124
  501.0 3.1 copy.208
  505.8 64.0 %while.53 = (s32[]{:T(128)}, bf16[16,1024,64]{1,2,0:T(8,128)(2,1)}, f32[16,1024]{1,0:T(8,128)S(1)}, s32[16,1024]{1,0:T(8,128)S(1)}, s32[16,512]{1,0:T(8,128)S(1)...) while((s32[]{:T(128)}, bf16[16,1024,64]{1,2,0:T(8,128)(2,1)}, ...), condition=%wide.region_10.11_spmd, body=%wide.region_7.10_spmd.sunk | while | flops 138935296 | bytes 7139441 | solution.py:82
  569.9 6.3 fusion.125
  578.8 11.4 copy.215
  590.2 48.0 %multiply_convert_fusion.2 = (bf16[1024,4096]{1,0:T(8,128)(2,1)}, f32[1024,4096]{1,0:T(8,128)}, f32[1024,4096]{1,0:T(8,128)}) fusion(f32[4096]{0:T(1024)S(1)} %bitcast.513, bf16[1024,4096]{0,1:T(8,128)(2,1)} %bitcast.446, bf16[1024,1024]{0,1:T(8,128)(2,1)S(1)} %fusion.113.clone.4), kind=kOutput, calls=%fused_computation.111 | convolution fusion | flops 8866758656 | bytes 52445184 | tf_op jit(solution)/shard_map/dot_general | solution.py:33
  638.2 16.7 fusion.126
  655.0 3.7 fusion.89
  661.8 3.8 convert_reduce_fusion.2
  665.7 24.8 convert_reduce_fusion
  690.4 19.1 multiply_reduce_fusion.2
  709.6 4.5 fusion.116
  719.7 3.2 copy.217
  723.2 180.4 %while.54 = (s32[]{:T(128)}, bf16[16,1024,64]{1,2,0:T(8,128)(2,1)S(1)}, bf16[16,512,64]{1,2,0:T(8,128)(2,1)}, bf16[16,512,64]{1,2,0:T(8,128)(2,1)}, s32[16,1024]...) while((s32[]{:T(128)}, ...), condition=%wide.region_21.22_spmd, body=%wide.region_19.21_spmd.sunk | while | flops 341310464 | bytes 17738880 | solution.py:103
  903.6 8.9 multiply_reduce_fusion.3
  913.9 4.5 fusion.115
  924.0 3.2 copy.220
  930.5 219.6 %while.55 = (s32[]{:T(128)}, bf16[16,1024,64]{1,2,0:T(8,128)(2,1)S(1)}, bf16[16,1024,64]{1,2,0:T(8,128)(2,1)}, bf16[16,1024,64]{1,2,0:T(8,128)(2,1)}, s32[16,102...) while((s32[]{:T(128)}, ...), condition=%wide.region_26.27_spmd, body=%wide.region_24.26_spmd.sunk | while | flops 684719104 | bytes 34120820 | solution.py:103
  1151.8 11.0 multiply_add_fusion
  1168.0 4.6 convolution_bitcast_fusion.7
  1176.5 4.0 convolution_bitcast_fusion.9
  1184.5 4.0 convolution_bitcast_fusion.8
  1192.0 3.7 convolution_bitcast_fusion.6
  1195.7 5.3 copy.243
  1201.0 9.9 copy.228
  1212.6 13.5 fusion.94
  1226.1 15.9 reshape.505
  1241.9 11.5 copy.225
  1254.1 16.6 fusion.110
  1270.7 20.4 reshape.512
  1291.2 17.7 copy.230
  1310.5 14.6 fusion.127
  1325.2 5.5 copy.232
  1333.3 39.5 %all-reduce.3 = (f32[4096]{0:T(1024)S(1)}, f32[1024]{0:T(1024)S(1)}) all-reduce(f32[4096]{0:T(1024)S(1)} %copy-done.54, f32[1024]{0:T(1024)S(1)} %copy-done.49), channel_id=9, replica_groups=mesh['outer'=4,'inner'=8] {'outer','inner'}, use_global_device_ids=true, to_apply=%region_35.36.clone | all-reduce | flops 5120 | bytes 40960
  1374.0 6.5 fusion.96
  1383.3 33.2 %reduce-scatter.31.cloned.1.call-done = f32[32,16]{1,0:T(8,128)} async-done(((f32[1024,16]{1,0:T(8,128)}), f32[32,16]{1,0:T(8,128)}) %reduce-scatter.31.cloned.1.call-update) | async-done | bytes 2064
  1417.9 138.4 %reduce-scatter.25.cloned.1.call-done = f32[128,256]{1,0:T(8,128)} async-done(((f32[4096,256]{1,0:T(8,128)}), f32[128,256]{1,0:T(8,128)}) %reduce-scatter.25.cloned.1.call-update) | async-done | bytes 131088 | tf_op jit(solution)/shard_map/reduce_scatter | solution.py:336
  1556.3 139.7 %reduce-scatter.19.cloned.1.call-done = f32[128,256]{1,0:T(8,128)} async-done(((f32[4096,256]{1,0:T(8,128)}), f32[128,256]{1,0:T(8,128)}) %reduce-scatter.19.cloned.1.call-update) | async-done | bytes 131088 | tf_op jit(solution)/shard_map/reduce_scatter | solution.py:333
  1696.0 139.5 %reduce-scatter.21.cloned.1.call-done = f32[128,256]{1,0:T(8,128)} async-done(((f32[4096,256]{1,0:T(8,128)}), f32[128,256]{1,0:T(8,128)}) %reduce-scatter.21.cloned.1.call-update) | async-done | bytes 131088 | tf_op jit(solution)/shard_map/reduce_scatter | solution.py:334
  1835.5 147.8 %reduce-scatter.23.cloned.1.call-done = f32[128,512]{1,0:T(8,128)} async-done(((f32[4096,512]{1,0:T(8,128)}), f32[128,512]{1,0:T(8,128)}) %reduce-scatter.23.cloned.1.call-update) | async-done | bytes 262160 | tf_op jit(solution)/shard_map/reduce_scatter | solution.py:335
  1983.4 158.8 %reduce-scatter.17.cloned.1.call-done = f32[128,768]{1,0:T(8,128)} async-done(((f32[4096,768]{1,0:T(8,128)}), f32[128,768]{1,0:T(8,128)}) %reduce-scatter.17.cloned.1.call-update) | async-done | bytes 393232 | tf_op jit(solution)/shard_map/reduce_scatter | solution.py:332
  2142.1 184.8 %reduce-scatter.27.cloned.1.call-done = f32[128,1024]{1,0:T(8,128)} async-done(((f32[4096,1024]{1,0:T(8,128)}), f32[128,1024]{1,0:T(8,128)}) %reduce-scatter.27.cloned.1.call-update) | async-done | bytes 524304 | tf_op jit(solution)/shard_map/reduce_scatter | solution.py:337
  2326.9 187.3 %reduce-scatter.29.cloned.1.call-done = f32[128,1024]{1,0:T(8,128)} async-done(((f32[4096,1024]{1,0:T(8,128)}), f32[128,1024]{1,0:T(8,128)}) %reduce-scatter.29.cloned.1.call-update) | async-done | bytes 524304 | tf_op jit(solution)/shard_map/reduce_scatter | solution.py:339
  (748 shorter events, 671.8 us)
Async XLA Ops:
  7.2 249.9 %copy-start = (bf16[512,1024]{1,0:T(8,128)(2,1)S(1)}, bf16[512,1024]{1,0:T(8,128)(2,1)}, u32[]{:S(2)}) copy-start(bf16[512,1024]{1,0:T(8,128)(2,1)} %param.27) | copy-start | bytes 3145732
  7.2 52.9 %copy-start.58 = (bf16[32,3]{0,1:T(4,128)(2,1)S(1)}, bf16[32,3]{0,1:T(4,128)(2,1)}, u32[]{:S(2)}) copy-start(bf16[32,3]{0,1:T(4,128)(2,1)} %param.42) | copy-start | bytes 580
  7.2 90.3 %copy-start.59 = (bf16[32,3]{0,1:T(4,128)(2,1)S(1)}, bf16[32,3]{0,1:T(4,128)(2,1)}, u32[]{:S(2)}) copy-start(bf16[32,3]{0,1:T(4,128)(2,1)} %param.43) | copy-start | bytes 580
  7.2 129.2 %copy-start.60 = (bf16[128]{0:T(256)(128)(2,1)S(1)}, bf16[128]{0:T(256)(128)(2,1)}, u32[]{:S(2)}) copy-start(bf16[128]{0:T(256)(128)(2,1)} %param.39) | copy-start | bytes 772
  7.2 165.6 %copy-start.63 = (bf16[32]{0:T(256)(128)(2,1)S(1)}, bf16[32]{0:T(256)(128)(2,1)}, u32[]{:S(2)}) copy-start(bf16[32]{0:T(256)(128)(2,1)} %param.41) | copy-start | bytes 196
  7.2 203.8 %copy-start.17 = (bf16[1024,1024]{1,0:T(8,128)(2,1)S(1)}, bf16[1024,1024]{1,0:T(8,128)(2,1)}, u32[]{:S(2)}) copy-start(bf16[1024,1024]{1,0:T(8,128)(2,1)} %param.28) | copy-start | bytes 6291460
  7.2 209.3 %all-gather.14.cloned.1.call-start = ((), (), s32[]{:S(2)}) async-start(), calls=%async_computation.11 | async-start | bytes 2162688 | tf_op jit(solution)/shard_map/all_gather | solution.py:157
  8.0 212.6 %all-gather.16.cloned.1.call-start = ((), (), s32[]{:S(2)}) async-start(), calls=%async_computation.12 | async-start | bytes 2162688 | tf_op jit(solution)/shard_map/all_gather | solution.py:158
  8.7 215.8 %all-gather.20.cloned.1.call-start = ((), (), s32[]{:S(2)}) async-start(), calls=%async_computation.14 | async-start | bytes 2162688 | tf_op jit(solution)/shard_map/all_gather | solution.py:160
  9.5 241.3 %all-gather.18.cloned.1.call-start = ((), (), s32[]{:S(2)}) async-start(), calls=%async_computation.13 | async-start | bytes 4325376 | tf_op jit(solution)/shard_map/all_gather | solution.py:159
  10.0 311.5 %all-gather.12.cloned.1.call-start = ((), (), s32[]{:S(2)}) async-start(), calls=%async_computation.10 | async-start | bytes 6488064 | tf_op jit(solution)/shard_map/all_gather | solution.py:156
  10.6 568.2 %all-gather.22.cloned.1.call-start = ((), (), s32[]{:S(2)}) async-start(), calls=%async_computation.15 | async-start | bytes 8650752 | tf_op jit(solution)/shard_map/all_gather | solution.py:161
  11.2 627.0 %all-gather.24.cloned.1.call-start = ((), (), s32[]{:S(2)}) async-start(), calls=%async_computation.16 | async-start | bytes 8650752 | tf_op jit(solution)/shard_map/all_gather | solution.py:163
  12.0 1368.6 %reduce-scatter.35.cloned.1.call-start = ((), (), s32[]{:S(2)}) async-start(), calls=%async_computation.26 | async-start | bytes 540672
  56.1 157.5 %copy-start.55 = (s32[1,1024]{1,0:T(1,128)S(1)}, s32[1,1024]{1,0:T(1,128)}, u32[]{:S(2)}) copy-start(s32[1,1024]{1,0:T(1,128)} %param.29) | copy-start | bytes 12292
  56.1 157.5 %copy-start.61 = (s32[1,8]{1,0:T(1,128)S(1)}, s32[1,8]{1,0:T(1,128)}, u32[]{:S(2)}) copy-start(s32[1,8]{1,0:T(1,128)} %param.31) | copy-start | bytes 100
  97.5 472.3 %copy-start.41 = (f32[1024,1]{0,1:T(1,128)}, f32[1024,1]{0,1:T(1,128)S(1)}, u32[]{:S(2)}) copy-start(f32[1024,1]{0,1:T(1,128)S(1)} %get-tuple-element.600) | copy-start | bytes 12292
  97.5 612.1 %copy-start.39 = (f32[1024,1]{0,1:T(1,128)}, f32[1024,1]{0,1:T(1,128)S(1)}, u32[]{:S(2)}) copy-start(f32[1024,1]{0,1:T(1,128)S(1)} %get-tuple-element.599) | copy-start | bytes 12292
  136.4 501.8 %copy-start.51 = (f32[1024,1]{0,1:T(1,128)}, f32[1024,1]{0,1:T(1,128)S(1)}, u32[]{:S(2)}) copy-start(f32[1024,1]{0,1:T(1,128)S(1)} %get-tuple-element.602) | copy-start | bytes 12292
  213.7 6.9 copy-start.43
  321.5 8.9 copy-start.18
  488.8 6.7 copy-start.15
  488.8 6.7 copy-start.27
  495.5 74.3 %copy-start.32 = (f32[1024]{0:T(1024)}, f32[1024]{0:T(1024)S(1)}, u32[]{:S(2)}) copy-start(f32[1024]{0:T(1024)S(1)} %broadcast_multiply_fusion.2) | copy-start | bytes 12292
  496.0 4.9 copy-start.45
  496.1 73.8 %copy-start.37 = (f32[1024]{0:T(1024)}, f32[1024]{0:T(1024)S(1)}, u32[]{:S(2)}) copy-start(f32[1024]{0:T(1024)S(1)} %fusion.101) | copy-start | bytes 12292
  497.6 3.3 copy-start.10
  501.0 3.2 copy-start.57
  569.8 6.3 copy-start.26
  569.8 6.3 copy-start.28
  569.8 6.3 copy-start.29
  576.2 133.4 %copy-start.30 = (f32[1024]{0:T(1024)}, f32[1024]{0:T(1024)S(1)}, u32[]{:S(2)}) copy-start(f32[1024]{0:T(1024)S(1)} %broadcast_multiply_fusion.1) | copy-start | bytes 12292
  576.7 13.5 copy-start.47
  576.7 133.0 %copy-start.35 = (f32[1024]{0:T(1024)}, f32[1024]{0:T(1024)S(1)}, u32[]{:S(2)}) copy-start(f32[1024]{0:T(1024)S(1)} %fusion.102) | copy-start | bytes 12292
  590.2 48.0 %copy-start.56 = (f32[1024]{0:T(1024)S(1)}, f32[1024]{0:T(1024)}, u32[]{:S(2)}) copy-start(f32[1024]{0:T(1024)} %convert_element_type.153) | copy-start | bytes 12292
  638.2 16.7 copy-start.5
  638.2 16.7 copy-start.34
  655.0 3.8 copy-start.4
  658.7 3.1 copy-start.53
  665.7 24.8 copy-start.22
  690.4 19.2 copy-start.48
  714.2 5.5 copy-start.7
  714.2 3.1 copy-start.21
  723.1 180.5 %copy-start.33 = (f32[1024]{0:T(1024)S(1)}, f32[1024]{0:T(1024)}, u32[]{:S(2)}) copy-start(f32[1024]{0:T(1024)} %copy-done.32) | copy-start | bytes 12292
  723.1 180.4 %copy-start.38 = (f32[1024]{0:T(1024)S(1)}, f32[1024]{0:T(1024)}, u32[]{:S(2)}) copy-start(f32[1024]{0:T(1024)} %copy-done.37) | copy-start | bytes 12292
  723.1 180.4 %copy-start.42 = (f32[1024,1]{0,1:T(1,128)S(1)}, f32[1024,1]{0,1:T(1,128)}, u32[]{:S(2)}) copy-start(f32[1024,1]{0,1:T(1,128)} %copy-done.41) | copy-start | bytes 12292
  903.6 9.0 copy-start.14
  903.6 10.3 copy-start.46
  913.6 468.3 %reduce-scatter.33.cloned.1.call-start = ((), (), s32[]{:S(2)}) async-start(), calls=%async_computation.25 | async-start | bytes 540672
  918.4 5.5 copy-start.6
  918.4 3.1 copy-start.19
  930.5 219.6 %copy-start.50 = (f32[1024]{0:T(1024)S(1)}, f32[1024]{0:T(1024)}, u32[]{:S(2)}) copy-start(f32[1024]{0:T(1024)} %get-tuple-element.493) | copy-start | bytes 12292
  1150.2 12.7 copy-start.12
  1151.5 265.0 %reduce-scatter.31.cloned.1.call-start = ((), (), s32[]{:S(2)}) async-start(), calls=%async_computation.24 | async-start | bytes 540672
  1151.8 13.2 copy-start.44
  1168.0 388.3 %reduce-scatter.25.cloned.1.call-start = ((), (), s32[]{:S(2)}) async-start(), calls=%async_computation.21 | async-start | bytes 4325376 | tf_op jit(solution)/shard_map/reduce_scatter | solution.py:336
  1175.0 521.0 %reduce-scatter.19.cloned.1.call-start = ((), (), s32[]{:S(2)}) async-start(), calls=%async_computation.18 | async-start | bytes 4325376 | tf_op jit(solution)/shard_map/reduce_scatter | solution.py:333
  1182.9 652.6 %reduce-scatter.21.cloned.1.call-start = ((), (), s32[]{:S(2)}) async-start(), calls=%async_computation.19 | async-start | bytes 4325376 | tf_op jit(solution)/shard_map/reduce_scatter | solution.py:334
  1190.8 792.6 %reduce-scatter.23.cloned.1.call-start = ((), (), s32[]{:S(2)}) async-start(), calls=%async_computation.20 | async-start | bytes 8650752 | tf_op jit(solution)/shard_map/reduce_scatter | solution.py:335
  1211.0 931.1 %reduce-scatter.17.cloned.1.call-start = ((), (), s32[]{:S(2)}) async-start(), calls=%async_computation.17 | async-start | bytes 12976128 | tf_op jit(solution)/shard_map/reduce_scatter | solution.py:332
  1253.4 1073.5 %reduce-scatter.27.cloned.1.call-start = ((), (), s32[]{:S(2)}) async-start(), calls=%async_computation.22 | async-start | bytes 17301504 | tf_op jit(solution)/shard_map/reduce_scatter | solution.py:337
  1308.9 1205.3 %reduce-scatter.29.cloned.1.call-start = ((), (), s32[]{:S(2)}) async-start(), calls=%async_computation.23 | async-start | bytes 17301504 | tf_op jit(solution)/shard_map/reduce_scatter | solution.py:339
  1325.2 5.6 copy-start.9
  1330.7 2.6 copy-start.54
  (32 other events, 58.0 us)
Sparse Core Ops, SparseCore 0:
  10.9 59.1 all-gather.13
  73.0 55.2 all-gather.15
  131.2 55.7 all-gather.19
  189.6 61.0 all-gather.17
  253.4 68.0 all-gather.11
  324.3 75.9 all-gather.21
  403.1 76.0 all-gather.23
  913.7 132.6 reduce-scatter.34
  1151.6 132.7 reduce-scatter.32
  1286.5 129.9 reduce-scatter.30
  1419.5 136.7 reduce-scatter.24
  1559.1 136.8 reduce-scatter.18
  1698.9 136.5 reduce-scatter.20
  1838.4 144.9 reduce-scatter.22
  1990.9 151.2 reduce-scatter.16
  2144.9 182.0 reduce-scatter.26
  2329.7 184.5 reduce-scatter.28
where the time goes:
time: 2540 us; the launch traced here: 2520 us
  waiting for transfers between devices  1210 us (48%)
  matrix products  687 us (27%)
  local copies, waits for them, and re-layouts  307 us (12%)
  blocking collectives  232 us (9%)
  other arithmetic  65.9 us (3%)
    dot_general x103, matrix products, transposed_right(): lax.dot_general(left_side, right_side, (((1,), (1,)), ((), ())), preferre...  258 us
    dot_general x71, matrix products, project(): return jnp.dot(left_side, right_side, preferred_element_type=jnp.float32)  221 us
    dot_general x71, matrix products, transposed_left(): lax.dot_general(left_side, right_side, (((0,), (0,)), ((), ())), preferre...  202 us
    reduce_scatter x1, waiting for transfers between devices, per_device(): lax.psum_scatter(arranged[8], ('outer', 'inner'), scatter_dimension=0, ti...  187 us
    reduce_scatter x1, waiting for transfers between devices, per_device(): lax.psum_scatter(arranged[6], ('outer', 'inner'), scatter_dimension=0, ti...  185 us
    reduce_scatter x1, waiting for transfers between devices, per_device(): lax.psum_scatter(arranged[1], ('outer', 'inner'), scatter_dimension=0, ti...  159 us
    reduce_scatter x1, waiting for transfers between devices, per_device(): lax.psum_scatter(arranged[4], ('outer', 'inner'), scatter_dimension=0, ti...  148 us
    reduce_scatter x1, waiting for transfers between devices, per_device(): lax.psum_scatter(arranged[2], ('outer', 'inner'), scatter_dimension=0, ti...  140 us
  transfers between devices with their start and end apart: 17, of which 10 were waited for; matrix products, arithmetic and copies ran while one was open for 29% of the time, Pallas kernels for 0%

commit v1 on v0

v1 whole, which is shorter than its diff:
```python
import functools

import jax
import jax.numpy as jnp
from jax import lax
from jax.experimental import pallas as pl
from jax.experimental.pallas import tpu as pltpu
from jax.sharding import PartitionSpec as P

HEADS = 16
HEAD_DIM = 64
GROUP = 4
BLOCK = 256
WINDOW = 512

epsilon = 1e-05
masked_score = -1000000000.0
bf16 = jnp.bfloat16
f32 = jnp.float32
both = ("outer", "inner")
MIB = 1 << 20


def mm(left, right):
    return lax.dot_general(left, right, (((1,), (0,)), ((), ())), preferred_element_type=f32)


def mm_nt(left, right):
    return lax.dot_general(left, right, (((1,), (1,)), ((), ())), preferred_element_type=f32)


def params():
    return pltpu.CompilerParams(vmem_limit_bytes=60 * MIB)


def cost(flops, moved, trans=0):
    share = 64
    return pl.CostEstimate(
        flops=int(flops) // share, bytes_accessed=int(moved) // share, transcendentals=int(trans) // share
    )


def whole(shape):
    return pl.BlockSpec(shape, lambda *_: (0,) * len(shape), pipeline_mode=pl.Buffered(1))


def weight_step(model, width, at):
    return pl.BlockSpec((1, model, width), lambda o, *_: (o, 0, at))


def weight_block(packed, width, at):
    outer, model, _ = packed.shape
    return pl.BlockSpec(
        (outer, model, width), lambda *_: (0, 0, at), pipeline_mode=pl.Buffered(1)
    )


def normalise(matrix):
    centred = matrix - jnp.mean(matrix, axis=-1, keepdims=True)
    rstd = lax.rsqrt(jnp.mean(centred * centred, axis=-1, keepdims=True) + epsilon)
    return centred * rstd, rstd


def norm_back(grad, gain, normed, rstd):
    scaled = grad * gain
    mean_scaled = jnp.mean(scaled, axis=-1, keepdims=True)
    mean_product = jnp.mean(scaled * normed, axis=-1, keepdims=True)
    return (scaled - mean_scaled - normed * mean_product) * rstd


def column_sum(matrix):
    return jnp.sum(matrix, axis=0, keepdims=True)


def triple_kernel(target_ref, token_ref, lang_ref, weight_ref, out_ref):
    start = target_ref[...].astype(f32) + mm(token_ref[...], lang_ref[...])
    out_ref[...] = mm(start.astype(bf16), weight_ref[0]).astype(bf16)


def triple_call(target, token_hot, lang_rows, packed, width, at):
    tokens, model = target.shape
    outer = packed.shape[0]
    step = tokens // 2
    return pl.pallas_call(
        triple_kernel,
        grid=(outer, 2),
        in_specs=[
            pl.BlockSpec((step, model), lambda o, r: (r, 0)),
            pl.BlockSpec((step, 128), lambda o, r: (r, 0)),
            pl.BlockSpec((128, model), lambda o, r: (0, 0)),
            weight_step(model, width, at),
        ],
        out_specs=pl.BlockSpec((step, width), lambda o, r: (r, o)),
        out_shape=jax.ShapeDtypeStruct((tokens, outer * width), bf16),
        compiler_params=params(),
        cost_estimate=cost(2 * tokens * model * outer * width, 16 * MIB),
        name="triple",
    )(target, token_hot, lang_rows, packed)


def pairs_kernel(memory_ref, weight_ref, out_ref):
    out_ref[...] = mm(memory_ref[...], weight_ref[0]).astype(bf16)


def pairs_call(memory, packed, width, at):
    tokens, model = memory.shape
    outer = packed.shape[0]
    return pl.pallas_call(
        pairs_kernel,
        grid=(outer,),
        in_specs=[
            pl.BlockSpec((tokens, model), lambda o: (0, 0)),
            weight_step(model, width, at),
        ],
        out_specs=pl.BlockSpec((tokens, width), lambda o: (0, o)),
        out_shape=jax.ShapeDtypeStruct((tokens, outer * width), bf16),
        compiler_params=params(),
        cost_estimate=cost(2 * tokens * model * outer * width, 8 * MIB),
        name="pairs",
    )(memory, packed)


def mask_bias(own_ref, other_ref, start, window, causal):
    block = own_ref.shape[0]
    allowed = own_ref[...] == other_ref[:, pl.ds(start, window)]
    if causal:
        own_at = pl.program_id(0) * block + lax.broadcasted_iota(jnp.int32, (block, window), 0)
        other_at = start + lax.broadcasted_iota(jnp.int32, (block, window), 1)
        allowed = allowed & (own_at >= other_at)
    return jnp.where(allowed, 0.0, masked_score).astype(f32)


def window_start(block_index, causal):
    if not causal:
        return 0
    return pl.multiple_of(jnp.maximum(block_index - 1, 0) * BLOCK, BLOCK)


def attend_kernel(causal, window, q_ref, k_ref, v_ref, own_ref, other_ref, mix_ref, level_ref, bias_ref):
    start = window_start(pl.program_id(0), causal)
    group = pl.program_id(1)

    @pl.when(group == 0)
    def _():
        bias_ref[...] = mask_bias(own_ref, other_ref, start, window, causal)
        level_ref[...] = jnp.zeros_like(level_ref)

    width = q_ref.shape[1]
    owner = lax.broadcasted_iota(jnp.int32, (1, width), 1) // HEAD_DIM
    lane = lax.broadcasted_iota(jnp.int32, (1, 128), 1)
    queries = q_ref[...] * bf16(HEAD_DIM ** -0.5)
    keys = k_ref[pl.ds(start, window), :]
    values = v_ref[pl.ds(start, window), :]
    mix = jnp.zeros(q_ref.shape, f32)
    levels = level_ref[...]
    for head in range(GROUP):
        chosen = owner == head
        scores = mm_nt(queries * chosen.astype(bf16), keys) + bias_ref[...]
        row_max = jnp.max(scores, axis=-1, keepdims=True)
        exps = jnp.exp(scores - row_max)
        total = jnp.sum(exps, axis=-1, keepdims=True)
        probs = (exps * (1.0 / total)).astype(bf16)
        mix = jnp.where(chosen, mm(probs, values), mix)
        levels = jnp.where(lane == group * GROUP + head, row_max + jnp.log(total), levels)
    mix_ref[...] = mix.astype(bf16)
    level_ref[...] = levels


def attend_call(q_array, q_at, k_array, k_at, v_array, v_at, own_column, other_row, causal):
    tokens, others = q_array.shape[0], k_array.shape[0]
    width = GROUP * HEAD_DIM
    model = HEADS * HEAD_DIM
    return pl.pallas_call(
        functools.partial(attend_kernel, causal, WINDOW),
        grid=(tokens // BLOCK, HEADS // GROUP),
        in_specs=[
            pl.BlockSpec((BLOCK, width), lambda b, g: (b, q_at + g)),
            pl.BlockSpec((others, width), lambda b, g: (0, k_at + g)),
            pl.BlockSpec((others, width), lambda b, g: (0, v_at + g)),
            pl.BlockSpec((BLOCK, 1), lambda b, g: (b, 0)),
            pl.BlockSpec((1, others), lambda b, g: (0, 0)),
        ],
        out_specs=[
            pl.BlockSpec((BLOCK, width), lambda b, g: (b, g)),
            pl.BlockSpec((BLOCK, 128), lambda b, g: (b, 0)),
        ],
        out_shape=[
            jax.ShapeDtypeStruct((tokens, model), bf16),
            jax.ShapeDtypeStruct((tokens, 128), f32),
        ],
        scratch_shapes=[pltpu.VMEM((BLOCK, WINDOW), f32)],
        compiler_params=params(),
        cost_estimate=cost(16e9, 12 * MIB, HEADS * tokens * WINDOW),
        name="attend",
    )(q_array, k_array, v_array, own_column, other_row)


def attend_back_kernel(
    causal, joined, q_ref, k_ref, v_ref, grad_ref, level_ref, own_ref, other_ref, *rest
):
    if joined:
        out_ref, keys_t, values_t = rest
    else:
        out_ref, pair_ref, keys_t, values_t = rest
    block_index = pl.program_id(0)
    group = pl.program_id(1)
    blocks = pl.num_programs(0)
    start = window_start(block_index, causal)
    window = WINDOW
    width = q_ref.shape[1]
    model = HEADS * HEAD_DIM
    rows = pl.ds(pl.multiple_of(group * width, width), width)

    @pl.when(block_index == 0)
    def _():
        keys_t[rows, :] = jnp.zeros((width, keys_t.shape[1]), f32)
        values_t[rows, :] = jnp.zeros((width, keys_t.shape[1]), f32)

    bias = mask_bias(own_ref, other_ref, start, window, causal)
    owner = lax.broadcasted_iota(jnp.int32, (1, width), 1) // HEAD_DIM
    lane = lax.broadcasted_iota(jnp.int32, (1, 128), 1)
    queries = q_ref[...] * bf16(HEAD_DIM ** -0.5)
    grads = grad_ref[...]
    queries_t = queries.T
    grads_t = grads.T
    keys = k_ref[pl.ds(start, window), :]
    values = v_ref[pl.ds(start, window), :]
    levels = level_ref[...]
    grad_q = jnp.zeros(q_ref.shape, f32)
    spot = pl.ds(start, window)
    for head in range(GROUP):
        chosen = owner == head
        picked = chosen.astype(bf16)
        scores = mm_nt(queries * picked, keys) + bias
        level = jnp.sum(
            jnp.where(lane == group * GROUP + head, levels, 0.0), axis=-1, keepdims=True
        )
        probs = jnp.exp(scores - level)
        grad_probs = mm_nt(grads * picked, values)
        inner = jnp.sum(probs * grad_probs, axis=-1, keepdims=True)
        grad_scores = (probs * (grad_probs - inner)).astype(bf16)
        band = slice(head * HEAD_DIM, (head + 1) * HEAD_DIM)
        target_rows = pl.ds(pl.multiple_of(group * width + head * HEAD_DIM, HEAD_DIM), HEAD_DIM)
        values_t[target_rows, spot] += mm(grads_t[band, :], probs.astype(bf16))
        keys_t[target_rows, spot] += mm(queries_t[band, :], grad_scores)
        grad_q = jnp.where(chosen, mm(grad_scores, keys), grad_q)
    grad_q = (grad_q * HEAD_DIM ** -0.5).astype(bf16)
    own_rows = pl.ds(pl.multiple_of(block_index * BLOCK, BLOCK), BLOCK)
    columns = pl.multiple_of(group * width, width)
    out_ref[own_rows, pl.ds(columns, width)] = grad_q
    other_ref_out, shift = (out_ref, model) if joined else (pair_ref, 0)

    @pl.when(block_index == blocks - 1)
    def _():
        other_ref_out[:, pl.ds(columns + shift, width)] = keys_t[rows, :].T.astype(bf16)
        other_ref_out[:, pl.ds(columns + shift + model, width)] = values_t[rows, :].T.astype(bf16)


def attend_back_call(
    q_array, q_at, k_array, k_at, v_array, v_at, grad_mix, levels, own_column, other_row, causal
):
    tokens, others = q_array.shape[0], k_array.shape[0]
    width = GROUP * HEAD_DIM
    model = HEADS * HEAD_DIM
    if causal:
        out_shape = [jax.ShapeDtypeStruct((tokens, 3 * model), bf16)]
    else:
        out_shape = [
            jax.ShapeDtypeStruct((tokens, model), bf16),
            jax.ShapeDtypeStruct((others, 2 * model), bf16),
        ]
    return pl.pallas_call(
        functools.partial(attend_back_kernel, causal, causal),
        grid=(tokens // BLOCK, HEADS // GROUP),
        in_specs=[
            pl.BlockSpec((BLOCK, width), lambda b, g: (b, q_at + g)),
            pl.BlockSpec((others, width), lambda b, g: (0, k_at + g)),
            pl.BlockSpec((others, width), lambda b, g: (0, v_at + g)),
            pl.BlockSpec((BLOCK, width), lambda b, g: (b, g)),
            pl.BlockSpec((BLOCK, 128), lambda b, g: (b, 0)),
            pl.BlockSpec((BLOCK, 1), lambda b, g: (b, 0)),
            pl.BlockSpec((1, others), lambda b, g: (0, 0)),
        ],
        out_specs=[whole(item.shape) for item in out_shape],
        out_shape=out_shape,
        scratch_shapes=[pltpu.VMEM((model, others), f32), pltpu.VMEM((model, others), f32)],
        compiler_params=params(),
        cost_estimate=cost(40e9, 16 * MIB, HEADS * tokens * WINDOW),
        name="attend_back",
    )(q_array, k_array, v_array, grad_mix, levels, own_column, other_row)


def middle_kernel(
    mix_ref, target_ref, token_ref, lang_ref, vec_ref, out_weight_ref, query_weight_ref,
    normed_ref, rstd_ref, entry_ref, queries_ref,
):
    outer, _, width = out_weight_ref.shape
    start = target_ref[...].astype(f32) + mm(token_ref[...], lang_ref[...])
    mix = mix_ref[...]
    branch = jnp.concatenate([mm(mix, out_weight_ref[o]) for o in range(outer)], axis=1)
    normed, rstd = normalise(2.0 * start + branch)
    normed_ref[...] = normed
    rstd_ref[...] = rstd
    entry = (normed * vec_ref[0:1, :] + vec_ref[3:4, :]).astype(bf16)
    entry_ref[...] = entry
    for o in range(outer):
        queries_ref[:, o * width:(o + 1) * width] = mm(entry, query_weight_ref[o]).astype(bf16)


def middle_call(mix, target, token_hot, lang_rows, vec, packed, at_self, at_cross, width):
    tokens, model = target.shape
    row = lambda r: (r, 0)
    return pl.pallas_call(
        middle_kernel,
        grid=(tokens // BLOCK,),
        in_specs=[
            pl.BlockSpec((BLOCK, model), row),
            pl.BlockSpec((BLOCK, model), row),
            pl.BlockSpec((BLOCK, 128), row),
            whole(lang_rows.shape),
            whole(vec.shape),
            weight_block(packed, width, at_self),
            weight_block(packed, width, at_cross),
        ],
        out_specs=[
            pl.BlockSpec((BLOCK, model), row),
            pl.BlockSpec((BLOCK, 1), row),
            pl.BlockSpec((BLOCK, model), row),
            pl.BlockSpec((BLOCK, model), row),
        ],
        out_shape=[
            jax.ShapeDtypeStruct((tokens, model), f32),
            jax.ShapeDtypeStruct((tokens, 1), f32),
            jax.ShapeDtypeStruct((tokens, model), bf16),
            jax.ShapeDtypeStruct((tokens, model), bf16),
        ],
        compiler_params=params(),
        cost_estimate=cost(4 * tokens * model * model, 16 * MIB),
        name="middle",
    )(mix, target, token_hot, lang_rows, vec, packed, packed)


def feed_kernel(
    at_cross, at_in, at_out,
    mix_ref, normed_ref, cot_ref, vec_ref, bias_ref, cross_hbm, in_hbm, out_hbm,
    layer_ref, entry_ref, act_ref, branch_grad_ref, pre_grad_ref, residual_ref, cross_grad_ref,
    mix_grad_ref, sums_ref, bias_sum_ref,
    cross_weight, in_weight, out_weight, slope, sems,
):
    outer, _, width = cross_weight.shape
    chunk = in_weight.shape[2]
    step = pl.program_id(0)

    def cross_copy():
        return pltpu.make_async_copy(
            cross_hbm.at[:, :, pl.ds(at_cross, width)], cross_weight, sems.at[0]
        )

    def in_copy(o):
        return pltpu.make_async_copy(
            in_hbm.at[o, :, pl.ds(at_in, chunk)], in_weight.at[o], sems.at[1 + o]
        )

    def out_copy(o):
        return pltpu.make_async_copy(
            out_hbm.at[o, :, pl.ds(at_out, out_weight.shape[2])], out_weight.at[o],
            sems.at[1 + outer + o],
        )


    @pl.when(step == 0)
    def _():
        cross_copy().start()
        for o in range(outer):
            in_copy(o).start()
            out_copy(o).start()
        sums_ref[...] = jnp.zeros_like(sums_ref)
        bias_sum_ref[...] = jnp.zeros_like(bias_sum_ref)
        cross_copy().wait()

    gain0, gain1, gain2 = vec_ref[0:1, :], vec_ref[1:2, :], vec_ref[2:3, :]
    shift0, shift1, shift2 = vec_ref[3:4, :], vec_ref[4:5, :], vec_ref[5:6, :]
    first = normed_ref[...] * gain0 + shift0
    mix = mix_ref[...]
    branch = jnp.concatenate([mm(mix, cross_weight[o]) for o in range(outer)], axis=1)
    normed1, rstd1 = normalise(2.0 * first + branch)
    second = normed1 * gain1 + shift1
    entry = second.astype(bf16)
    entry_ref[...] = entry
    total = 2.0 * second + vec_ref[6:7, :]
    for o in range(outer):
        @pl.when(step == 0)
        def _():
            in_copy(o).wait()
            out_copy(o).wait()

        span = slice(o * chunk, (o + 1) * chunk)
        pre = mm(entry, in_weight[o]) + bias_ref[:, span]
        half = 0.5 + 0.5 * lax.erf(pre * (0.5 ** 0.5))
        slope[:, span] = half + pre * (jnp.exp(-0.5 * pre * pre) * 0.3989422804014327)
        act = (pre * half).astype(bf16)
        act_ref[:, span] = act
        total = total + mm(act, out_weight[o])
    normed2, rstd2 = normalise(total)
    layer_ref[...] = (normed2 * gain2 + shift2).astype(bf16)
    cot = cot_ref[...].astype(f32)
    sums_ref[0:1, :] += column_sum(cot * normed2)
    sums_ref[1:2, :] += column_sum(cot)
    back2 = norm_back(cot, gain2, normed2, rstd2)
    branch_grad = back2.astype(bf16)
    branch_grad_ref[...] = branch_grad
    sums_ref[2:3, :] += column_sum(branch_grad.astype(f32))
    grad_second = 2.0 * back2
    for o in range(outer):
        span = slice(o * chunk, (o + 1) * chunk)
        pre_grad = (mm_nt(branch_grad, out_weight[o]) * slope[:, span]).astype(bf16)
        pre_grad_ref[:, span] = pre_grad
        bias_sum_ref[:, span] += column_sum(pre_grad.astype(f32))
        grad_second = grad_second + mm_nt(pre_grad, in_weight[o])
    sums_ref[3:4, :] += column_sum(grad_second * normed1)
    sums_ref[4:5, :] += column_sum(grad_second)
    back1 = norm_back(grad_second, gain1, normed1, rstd1)
    residual_ref[...] = back1
    cross_grad = back1.astype(bf16)
    cross_grad_ref[...] = cross_grad
    mix_grad = mm_nt(cross_grad[:, 0:width], cross_weight[0])
    for o in range(1, outer):
        mix_grad = mix_grad + mm_nt(
            cross_grad[:, o * width:(o + 1) * width], cross_weight[o]
        )
    mix_grad_ref[...] = mix_grad.astype(bf16)


def feed_call(mix, normed, cot, vec, bias, packed_cross, at_cross, packed_in, at_in, packed_out, at_out, width):
    tokens, model = mix.shape
    hidden = bias.shape[1]
    outer = packed_cross.shape[0]
    chunk = hidden // outer
    row = lambda r: (r, 0)
    blocked = lambda cols: pl.BlockSpec((BLOCK, cols), row)
    anywhere = pl.BlockSpec(memory_space=pl.ANY)
    out = lambda cols, kind: jax.ShapeDtypeStruct((tokens, cols), kind)
    return pl.pallas_call(
        functools.partial(feed_kernel, at_cross, at_in, at_out),
        grid=(tokens // BLOCK,),
        in_specs=[
            blocked(model), blocked(model), blocked(model),
            whole(vec.shape), whole(bias.shape), anywhere, anywhere, anywhere,
        ],
        out_specs=[
            blocked(model), blocked(model), blocked(hidden), blocked(model), blocked(hidden),
            blocked(model), blocked(model), blocked(model),
            pl.BlockSpec((8, model), lambda r: (0, 0)),
            pl.BlockSpec((1, hidden), lambda r: (0, 0)),
        ],
        out_shape=[
            out(model, bf16), out(model, bf16), out(hidden, bf16), out(model, bf16),
            out(hidden, bf16), out(model, f32), out(model, bf16), out(model, bf16),
            jax.ShapeDtypeStruct((8, model), f32),
            jax.ShapeDtypeStruct((1, hidden), f32),
        ],
        scratch_shapes=[
            pltpu.VMEM((outer, model, width), bf16),
            pltpu.VMEM((outer, model, chunk), bf16),
            pltpu.VMEM((outer, chunk, model), bf16),
            pltpu.VMEM((BLOCK, hidden), f32),
            pltpu.SemaphoreType.DMA((1 + 2 * outer,)),
        ],
        compiler_params=params(),
        cost_estimate=cost(36 * tokens * model * model, 60 * MIB, tokens * hidden * 2),
        name="feed",
    )(mix, normed, cot, vec, bias, packed_cross, packed_in, packed_out)


def middle_back_kernel(
    residual_ref, queries_grad_ref, normed_ref, rstd_ref, vec_ref, query_weight_ref, out_weight_ref,
    start_ref, branch_grad_ref, mix_grad_ref, sums_ref,
):
    outer, _, width = out_weight_ref.shape

    @pl.when(pl.program_id(0) == 0)
    def _():
        sums_ref[...] = jnp.zeros_like(sums_ref)

    grad_first = 2.0 * residual_ref[...]
    for o in range(outer):
        grad_first = grad_first + mm_nt(
            queries_grad_ref[:, o * width:(o + 1) * width], query_weight_ref[o]
        )
    normed = normed_ref[...]
    sums_ref[0:1, :] += column_sum(grad_first * normed)
    sums_ref[1:2, :] += column_sum(grad_first)
    back = norm_back(grad_first, vec_ref[0:1, :], normed, rstd_ref[...])
    start_ref[...] = back
    branch_grad = back.astype(bf16)
    branch_grad_ref[...] = branch_grad
    mix_grad = mm_nt(branch_grad[:, 0:width], out_weight_ref[0])
    for o in range(1, outer):
        mix_grad = mix_grad + mm_nt(
            branch_grad[:, o * width:(o + 1) * width], out_weight_ref[o]
        )
    mix_grad_ref[...] = mix_grad.astype(bf16)


def middle_back_call(residual, queries_grad, normed, rstd, vec, packed, at_cross, at_self, width):
    tokens, model = residual.shape
    row = lambda r: (r, 0)
    blocked = pl.BlockSpec((BLOCK, model), row)
    return pl.pallas_call(
        middle_back_kernel,
        grid=(tokens // BLOCK,),
        in_specs=[
            blocked, blocked, blocked,
            pl.BlockSpec((BLOCK, 1), row),
            whole(vec.shape),
            weight_block(packed, width, at_cross),
            weight_block(packed, width, at_self),
        ],
        out_specs=[blocked, blocked, blocked, pl.BlockSpec((8, model), lambda r: (0, 0))],
        out_shape=[
            jax.ShapeDtypeStruct((tokens, model), f32),
            jax.ShapeDtypeStruct((tokens, model), bf16),
            jax.ShapeDtypeStruct((tokens, model), bf16),
            jax.ShapeDtypeStruct((8, model), f32),
        ],
        compiler_params=params(),
        cost_estimate=cost(4 * tokens * model * model, 22 * MIB),
        name="middle_back",
    )(residual, queries_grad, normed, rstd, vec, packed, packed)


def fill_product(table_ref, left_t, right_ref, lo, hi, out_refs):
    piece, width = out_refs[0].shape[2:]
    inner = left_t.shape[0] // piece
    part = inner // len(out_refs)
    count = min(BLOCK // piece, part)
    for at, out_ref in enumerate(out_refs):
        @pl.loop(0, part // count)
        def _(m):
            blocks = [
                left_t[pl.ds(pl.multiple_of(table_ref[at * part + m * count + k] * piece, piece), piece), :]
                for k in range(count)
            ]
            product = mm(jnp.concatenate(blocks, axis=0), right_ref[:, lo:hi]).astype(bf16)
            out_ref[pl.ds(m * count, count), 0] = product.reshape(count, piece, width)


def split_refs(rest, outputs):
    return rest[-outputs - 1:-1], rest[-1]


def weight_kernel(outputs, lo, hi, table_ref, left_ref, right_ref, *rest):
    out_refs, left_t = split_refs(rest, outputs)

    @pl.when(pl.program_id(0) == 0)
    def _():
        left_t[...] = left_ref[...].T

    fill_product(table_ref, left_t, right_ref, lo, hi, out_refs)


def entry_weight_kernel(outputs, lo, hi, table_ref, target_ref, token_ref, lang_ref, right_ref, *rest):
    out_refs, left_t = split_refs(rest, outputs)

    @pl.when(pl.program_id(0) == 0)
    def _():
        start = target_ref[...].astype(f32) + mm(token_ref[...], lang_ref[...])
        left_t[...] = start.astype(bf16).T

    fill_product(table_ref, left_t, right_ref, lo, hi, out_refs)


def rows_weight_kernel(outputs, lo, hi, table_ref, left_ref, right_ref, *rest):
    out_refs, left_t = split_refs(rest, outputs)
    left_t[...] = left_ref[...].T
    fill_product(table_ref, left_t, right_ref, lo, hi, out_refs)


def weight_call(
    kernel, table, lefts, left_specs, right, right_spec, inner, model, lo, hi, at, total, outputs, held
):
    tokens = right.shape[0]
    outer = table.shape[0] - inner
    width = hi - lo
    operands = list(lefts) + [right]
    specs = list(left_specs) + [right_spec]
    aliases = {}
    for index, item in enumerate(held or ()):
        aliases[1 + len(operands)] = index
        operands.append(item)
        specs.append(pl.BlockSpec(memory_space=pl.ANY))
    part = inner // outputs
    return pl.pallas_call(
        functools.partial(kernel, outputs, lo, hi),
        grid_spec=pltpu.PrefetchScalarGridSpec(
            num_scalar_prefetch=1,
            grid=(outer,),
            in_specs=specs,
            out_specs=[
                pl.BlockSpec(
                    (part, 1, model // inner, width), lambda o, table: (0, table[inner + o], 0, at)
                )
            ] * outputs,
            scratch_shapes=[pltpu.VMEM((model, tokens), bf16)],
        ),
        out_shape=[jax.ShapeDtypeStruct((part, outer, model // inner, total), bf16)] * outputs,
        input_output_aliases=aliases,
        compiler_params=params(),
        cost_estimate=cost(2 * tokens * model * outer * width, 4 * MIB + 4 * model * outer * width),
        name="weight_grad",
    )(table, *operands)


def column_weight_grad(table, left, right, inner, width, at, total, outputs, held=None):
    tokens, model = left.shape
    return weight_call(
        weight_kernel, table, [left], [whole(left.shape)], right,
        pl.BlockSpec((tokens, width), lambda o, table: (0, o)), inner, model, 0, width, at, total,
        outputs, held,
    )


def row_weight_grad(table, left, right, inner, at, total, held=None):
    tokens, width = right.shape
    rows = left.shape[1] // (table.shape[0] - inner)
    return weight_call(
        rows_weight_kernel, table, [left], [pl.BlockSpec((tokens, rows), lambda o, table: (0, o))],
        right, whole(right.shape), inner, rows, 0, width, at, total, 1, held,
    )


def target_back_kernel(start_ref, triple_ref, weight_ref, token_t_ref, out_ref, lang_ref):
    outer, _, width = weight_ref.shape

    @pl.when(pl.program_id(0) == 0)
    def _():
        lang_ref[...] = jnp.zeros_like(lang_ref)

    grad = 2.0 * start_ref[...]
    for o in range(outer):
        grad = grad + mm_nt(
            triple_ref[:, o * width:(o + 1) * width], weight_ref[o]
        )
    out_ref[...] = grad
    high = grad.astype(bf16)
    rest = grad - high.astype(f32)
    mid = rest.astype(bf16)
    low = (rest - mid.astype(f32)).astype(bf16)
    token_t = token_t_ref[...]
    lang_ref[...] += mm(token_t, high) + mm(token_t, mid) + mm(token_t, low)


def target_back_call(start_grad, triple_grad, packed, width, at, token_t):
    tokens, model = start_grad.shape
    outer = packed.shape[0]
    row = lambda r: (r, 0)
    return pl.pallas_call(
        target_back_kernel,
        grid=(tokens // BLOCK,),
        in_specs=[
            pl.BlockSpec((BLOCK, model), row),
            pl.BlockSpec((BLOCK, outer * width), row),
            weight_block(packed, width, at),
            pl.BlockSpec((token_t.shape[0], BLOCK), lambda r: (0, r)),
        ],
        out_specs=[
            pl.BlockSpec((BLOCK, model), row),
            pl.BlockSpec((token_t.shape[0], model), lambda r: (0, 0)),
        ],
        out_shape=[
            jax.ShapeDtypeStruct((tokens, model), f32),
            jax.ShapeDtypeStruct((token_t.shape[0], model), f32),
        ],
        compiler_params=params(),
        cost_estimate=cost(2 * tokens * model * outer * width, 20 * MIB),
        name="target_back",
    )(start_grad, triple_grad, packed, token_t)


def memory_back_kernel(pairs_ref, weight_ref, out_ref):
    outer, _, width = weight_ref.shape
    grad = mm_nt(pairs_ref[:, 0:width], weight_ref[0])
    for o in range(1, outer):
        grad = grad + mm_nt(
            pairs_ref[:, o * width:(o + 1) * width], weight_ref[o]
        )
    out_ref[...] = grad


def memory_back_call(pairs_grad, packed, width, at):
    tokens = pairs_grad.shape[0]
    outer, model, _ = packed.shape
    row = lambda r: (r, 0)
    return pl.pallas_call(
        memory_back_kernel,
        grid=(tokens // BLOCK,),
        in_specs=[
            pl.BlockSpec((BLOCK, outer * width), row),
            weight_block(packed, width, at),
        ],
        out_specs=pl.BlockSpec((BLOCK, model), row),
        out_shape=jax.ShapeDtypeStruct((tokens, model), f32),
        compiler_params=params(),
        cost_estimate=cost(2 * tokens * model * outer * width, 8 * MIB),
        name="memory_back",
    )(pairs_grad, packed)


def gather(shard, outer):
    full = lax.all_gather(shard, both, axis=0, tiled=True)
    return full.reshape(outer, full.shape[0] // outer, full.shape[1])


def bits_of(count):
    return count.bit_length() - 1


def reverse_bits(number, order):
    last = len(order) - 1
    return sum(((number >> bit) & 1) << (last - at) for at, bit in enumerate(order))


def place_orders(outer, inner, swapped):
    inner_order = list(range(bits_of(inner)))
    if swapped and len(inner_order) > 2:
        inner_order[1], inner_order[2] = inner_order[2], inner_order[1]
    return inner_order, list(range(bits_of(outer)))


def inner_places(inner, order):
    places = [0] * inner
    for number in range(inner):
        places[reverse_bits(number, order)] = number
    return jnp.array(places, jnp.int32)


def together_with(value, *others):
    return lax.optimization_barrier((value,) + others)


def chain_step(state, devices):
    keep, send, bits = state
    moved = lax.ppermute(send, both, [(d, d ^ (1 << bits[0])) for d in range(devices)])
    if len(bits) == 1:
        return (keep.astype(f32) + moved.astype(f32))[0], None, ()
    half = keep.shape[0] // 2
    send = (keep[half:].astype(f32) + moved[half:].astype(f32)).astype(send.dtype)
    keep = (keep[:half].astype(f32) + moved[:half].astype(f32)).astype(send.dtype)
    return keep, send, bits[1:]


def chain_start(halves, orders, inner):
    inner_order, outer_order = orders
    keep, send = [item.reshape((-1,) + item.shape[2:]) for item in halves]
    return keep, send, tuple(inner_order + [bits_of(inner) + bit for bit in outer_order])


def chain_end(state, devices):
    while state[2]:
        state = chain_step(state, devices)
    return state[0]


def hold(value, *states):
    value, parts = lax.optimization_barrier((value, [state[:2] for state in states]))
    return value, *[(*part, state[2]) for part, state in zip(parts, states)]


def inner_scatter(packed):
    inner, outer, rows, columns = packed.shape
    flat = packed.reshape(inner * outer * rows, columns)
    part = lax.psum_scatter(flat, "inner", scatter_dimension=0, tiled=True)
    part = part.reshape(outer, rows, columns)
    bits = tuple(bits_of(inner) + bit for bit in range(bits_of(outer)))
    return part[:outer // 2], part[outer // 2:], bits


def per_device(
    target, memory, cotangent, segment_ids, memory_segments, directions, lang_table,
    self_qkv, self_out, cross_q, cross_kv, cross_out, ffn_in, ffn_in_bias, ffn_out, ffn_out_bias,
    norm_gains, norm_biases,
):
    outer = lax.axis_size("outer")
    inner = lax.axis_size("inner")
    devices = outer * inner
    tokens, model = target.shape
    hidden = devices * ffn_in_bias.shape[0]
    langs = lang_table.shape[1]
    piece = model // devices
    rows = model // inner
    w3, w1, w2, w4 = 3 * model // outer, model // outer, 2 * model // outer, hidden // outer
    ratio = hidden // model
    together = ffn_out.shape[0] == rows and model == w4

    small = jnp.concatenate(
        [
            lang_table.T, norm_gains.T, norm_biases.T,
            ffn_out_bias.reshape(1, piece), ffn_in_bias.reshape(ratio, piece),
        ],
        axis=0,
    )
    n_small = small.shape[0]
    small = jnp.pad(small, ((0, rows - n_small), (0, 128 - piece)))
    shards = [self_qkv, self_out, cross_kv, cross_q, cross_out, small]
    weights = gather(jnp.concatenate(shards, axis=1), outer)
    at_small = w3 + 2 * w1 + w2 + w1
    if together:
        shard, weights = lax.optimization_barrier((jnp.concatenate([ffn_in, ffn_out], axis=1), weights))
        g_in = gather(shard, outer)
        g_out, at_out = g_in, w4
    else:
        g_in = gather(ffn_in, outer)
        g_out, at_out = gather(ffn_out, outer), 0

    my_inner, my_outer = lax.axis_index("inner"), lax.axis_index("outer")
    straight = place_orders(outer, inner, False)
    crossed = place_orders(outer, inner, True)
    outer_order = straight[1]
    outer_places = jnp.array([reverse_bits(o, outer_order) for o in range(outer)], jnp.int32)
    outer_places = outer_places ^ reverse_bits(my_outer, outer_order)
    table_plain = jnp.concatenate([jnp.arange(inner, dtype=jnp.int32), outer_places])
    table_a = jnp.concatenate([inner_places(inner, straight[0]) ^ my_inner, outer_places])
    table_b = jnp.concatenate([inner_places(inner, crossed[0]) ^ my_inner, outer_places])

    seg = segment_ids.reshape(-1)
    hot_seg = seg[:, None] == jnp.arange(directions.shape[1])[None, :]
    token_dir = jnp.sum(jnp.where(hot_seg, directions.reshape(1, -1), 0), axis=-1)
    token_hot = (token_dir[:, None] == jnp.arange(128)[None, :]).astype(bf16)
    token_t = (jnp.arange(langs)[:, None] == token_dir[None, :]).astype(bf16)
    own_column = seg[:, None]

    smalls = weights[:, :, at_small:at_small + piece].reshape(devices, rows, piece)[:, :n_small]
    smalls = smalls.transpose(1, 0, 2)
    lang_rows = jnp.pad(smalls[:langs].reshape(langs, model), ((0, 128 - langs), (0, 0)))
    vec = jnp.pad(smalls[langs:langs + 7].reshape(7, model).astype(f32), ((0, 1), (0, 0)))
    in_bias = smalls[langs + 7:].transpose(1, 0, 2).reshape(1, hidden).astype(f32)

    triple = triple_call(target, token_hot, lang_rows, weights, w3, 0)
    hg = HEADS // GROUP
    self_mix, self_levels = attend_call(
        triple, 0, triple, hg, triple, 2 * hg, own_column, segment_ids, True
    )
    pairs = pairs_call(memory, weights, w2, 2)
    normed0, rstd0, cross_entry, queries = middle_call(
        self_mix, target, token_hot, lang_rows, vec, weights, 3, 6, w1
    )
    cross_mix, cross_levels = attend_call(
        queries, 0, pairs, 0, pairs, hg, own_column, memory_segments, False
    )
    (
        layer_output, ffn_entry, act, branch_grad, pre_grad, residual1, cross_grad, cross_mix_grad,
        sums, bias_sum,
    ) = feed_call(
        cross_mix, normed0, cotangent, vec, in_bias, weights, w3 + 2 * w1 + w2, g_in, 0, g_out, at_out, w1
    )

    if together:
        ffn_grads = row_weight_grad(table_plain, act, branch_grad, inner, 1, 2 * w4)
        ffn_grads = column_weight_grad(
            table_plain, ffn_entry, pre_grad, inner, w4, 0, 2 * w4, 1, ffn_grads
        )
        ffn_states = [inner_scatter(ffn_grads[0])]
    else:
        ffn_grads = column_weight_grad(table_plain, ffn_entry, pre_grad, inner, w4, 0, w4, 1)
        ffn_grads += row_weight_grad(table_plain, act, branch_grad, inner, 0, model)
        ffn_states = [inner_scatter(item) for item in ffn_grads]

    cross_mix_grad, _ = lax.optimization_barrier((cross_mix_grad, ffn_grads))
    queries_grad, pairs_grad = attend_back_call(
        queries, 0, pairs, 0, pairs, hg, cross_mix_grad, cross_levels, own_column, memory_segments, False
    )
    start_grad, self_grad, self_mix_grad, sums0 = middle_back_call(
        residual1, queries_grad, normed0, rstd0, vec, weights, 6, 3, w1
    )
    grads_a = column_weight_grad(table_a, memory, pairs_grad, inner, w2, 0, w2 + w1, 2)
    grads_a = column_weight_grad(table_a, self_mix, self_grad, inner, w1, 2, w2 + w1, 2, grads_a)
    state_a = chain_start(grads_a, straight, inner)
    queries_grad, state_a = hold(queries_grad, state_a)
    grads_b = column_weight_grad(table_b, cross_entry, queries_grad, inner, w1, 0, 2 * w1, 2)
    grads_b = column_weight_grad(table_b, cross_mix, cross_grad, inner, w1, 1, 2 * w1, 2, grads_b)
    state_b = chain_start(grads_b, crossed, inner)
    state_a = chain_step(state_a, devices)
    self_mix_grad, state_a, state_b = hold(self_mix_grad, state_a, state_b)
    (triple_grad,) = attend_back_call(
        triple, 0, triple, hg, triple, 2 * hg, self_mix_grad, self_levels, own_column, segment_ids, True
    )
    state_a, state_b = chain_step(state_a, devices), chain_step(state_b, devices)
    triple_grad, state_a, state_b, *ffn_states = hold(triple_grad, state_a, state_b, *ffn_states)
    middle = (w3 + 255) // 256 * 128

    def triple_weight_grad(table, right, lo, hi):
        return weight_call(
            entry_weight_kernel, table, [target, token_hot, lang_rows],
            [whole(target.shape), whole(token_hot.shape), whole(lang_rows.shape)],
            right, pl.BlockSpec((tokens, w3), lambda o, table: (0, o)), inner, model, lo, hi, 0,
            hi - lo, 2, None,
        )

    state_c = chain_start(triple_weight_grad(table_a, triple_grad, 0, middle), straight, inner)
    triple_grad, state_c = hold(triple_grad, state_c)
    state_d = chain_start(triple_weight_grad(table_b, triple_grad, middle, w3), crossed, inner)
    state_a, state_b = chain_step(state_a, devices), chain_step(state_b, devices)
    state_c = chain_step(state_c, devices)
    triple_grad, state_a, state_b, state_c, state_d = hold(
        triple_grad, state_a, state_b, state_c, state_d
    )
    target_grad, lang_sum = target_back_call(start_grad, triple_grad, weights, w3, 0, token_t)
    state_c, state_d = chain_step(state_c, devices), chain_step(state_d, devices)
    lang_sum, state_c, state_d = hold(lang_sum, state_c, state_d)

    stacked = jnp.concatenate(
        [lang_sum, sums0[0:1], sums[3:4], sums[0:1], sums0[1:2], sums[4:5], sums[1:2], sums[2:3]], axis=0
    )
    stacked = stacked.reshape(langs + 7, devices, piece).transpose(1, 0, 2)
    stacked = jnp.concatenate([stacked, bias_sum.reshape(devices, ratio, piece)], axis=1)
    order = table_a[:inner, None] + inner * (inner_places(outer, outer_order) ^ my_outer)[None, :]
    stacked = jnp.take(stacked, order.reshape(-1), axis=0, mode="clip")
    half = devices // 2
    state_e = chain_start(
        [stacked[:half].reshape(inner // 2, outer, n_small, piece),
         stacked[half:].reshape(inner // 2, outer, n_small, piece)], straight, inner,
    )
    pairs_grad, state_e = hold(pairs_grad, state_e)
    memory_grad = memory_back_call(pairs_grad, weights, w2, 2)

    done_a, done_b, done_c, done_d, extra = [
        chain_end(state, devices) for state in (state_a, state_b, state_c, state_d, state_e)
    ]
    ffn_done = [chain_end(state, devices) for state in ffn_states]
    if together:
        ffn_in_grad, ffn_out_grad = ffn_done[0][:, :w4], ffn_done[0][:, w4:]
    else:
        ffn_in_grad, ffn_out_grad = ffn_done
    return (
        layer_output,
        target_grad,
        memory_grad,
        extra[:langs].T,
        jnp.concatenate([done_c, done_d], axis=1),
        done_a[:, w2:],
        done_b[:, :w1],
        done_a[:, :w2],
        done_b[:, w1:],
        ffn_in_grad,
        extra[langs + 7:].reshape(-1),
        ffn_out_grad,
        extra[langs + 6],
        extra[langs:langs + 3].T,
        extra[langs + 3:langs + 6].T,
    )


def solution(mesh):
    rows, cols, line = P(both, None), P("inner", "outer"), P(both)
    return jax.shard_map(
        per_device,
        mesh=mesh,
        in_specs=(
            rows, rows, rows, rows, rows, rows, rows, cols, cols, cols, cols, cols, cols, line, rows,
            line, rows, rows,
        ),
        out_specs=(
            rows, rows, rows, rows, cols, cols, cols, cols, cols, cols, line, rows, line, rows, rows,
        ),
        check_vma=False,
    )
```

time: 2540 us -> 670 us (0.26)
  waiting for transfers between devices: 1210 us -> 199 us
  matrix products: 687 us -> 0 us
  Pallas kernels: 0 us -> 357 us
  local copies, waits for them, and re-layouts: 307 us -> 25.2 us
  blocking collectives: 232 us -> 0 us
  other arithmetic: 65.9 us -> 35.6 us
  starting transfers between devices: 2.24 us -> 31.8 us
    reduce_scatter x7 -> x1, waiting for transfers between devices: 1100 us -> 0.01 us  [inner_scatter(): part = lax.psum_scatter(flat, 'inner', scatter_dimension=0, tiled=True)]
    dot_general x246 -> x0, matrix products: 684 us -> none  [the longest x103 258 us: transposed_right(): lax.dot_general(left_side, right_side, (((1,), (1,)), ((), ())), preferre...]
    pallas_call x0 -> x19, Pallas kernels: none -> 357 us  [the longest x8 94.5 us: weight_call(): pl.pallas_call(functools.partial(kernel, outputs, lo, hi), grid_spec=pltp...]
    all_gather x4 -> x0, blocking collectives: 155 us -> none  [the longest x1 43.9 us: per_device(): lax.all_gather(lang_table, ('outer', 'inner'), axis=0, tiled=True)]
    transpose x12 -> x3, local copies, waits for them, and re-layouts: 84.6 us -> 1.2 us  [the longest x1 0.6 us: per_device(): extra[:langs]]
    unnamed x2 -> x0, blocking collectives: 76.9 us -> none
    all_gather x7 -> x2, waiting for transfers between devices: 75.5 us -> 144 us  [gather(): full = lax.all_gather(shard, both, axis=0, tiled=True)]
    dynamic_slice x128 -> x0, local copies, waits for them, and re-layouts: 61.1 us -> none  [the longest x96 36.4 us: attention_forward(): lax.map(one_item, (queries, keys_all, values_all, own_ids, other_ids))]
  transfers between devices with their start and end apart: 17 -> 30, of which waited for: 10 -> 15; matrix products, arithmetic and copies ran while one was open for 29% -> 8% of each run, Pallas kernels for 0% -> 40%
where the time goes in v1:
time: 670 us; the launch traced here: 663 us
  Pallas kernels  357 us (53%)
  waiting for transfers between devices  199 us (30%)
  other arithmetic  35.6 us (5%)
  starting transfers between devices  31.8 us (5%)
  local copies, waits for them, and re-layouts  25.2 us (4%)
  between operations  14.5 us (2%)
    all_gather x2, waiting for transfers between devices, gather(): full = lax.all_gather(shard, both, axis=0, tiled=True)  144 us
    pallas_call x8, Pallas kernels, weight_call(): pl.pallas_call(functools.partial(kernel, outputs, lo, hi), grid_spec=pltp...  94.5 us
    pallas_call x2, Pallas kernels, attend_back_call(): pl.pallas_call(functools.partial(attend_back_kernel, causal, causal), gri...  87.1 us
    pallas_call x1, Pallas kernels, feed_call(): pl.pallas_call(functools.partial(feed_kernel, at_cross, at_in, at_out), g...  57.7 us
    ppermute x27, waiting for transfers between devices, chain_step(): lax.ppermute(send, both, [(d, d ^ 1 << bits[0]) for d in range(devices)])  54.6 us
    pallas_call x2, Pallas kernels, attend_call(): pl.pallas_call(functools.partial(attend_kernel, causal, WINDOW), grid=(to...  53.4 us
    ppermute x27, starting transfers between devices, chain_step(): lax.ppermute(send, both, [(d, d ^ 1 << bits[0]) for d in range(devices)])  31.7 us
    convert_element_type x13, other arithmetic, chain_step(): (keep[half:].astype(f32) + moved[half:].astype(f32)).astype(send.dtype)  24.6 us
  transfers between devices with their start and end apart: 30, of which 15 were waited for; matrix products, arithmetic and copies ran while one was open for 8% of the time, Pallas kernels for 40%

profile of v1, /device:TPU:0, one launch (start us, length us, event | category | flops | bytes accessed | tf_op | source)
XLA Modules:
  0.0 663.1 jit_solution(5108280600927675564)
XLA Ops:
  12.4 1.5 concatenate.29
  14.8 1.9 pad_maximum_fusion
  16.7 120.8 %all-gather.3.cloned.1.call-done = bf16[4096,2176]{1,0:T(8,128)(2,1)} async-done(((bf16[128,2176]{1,0:T(8,128)(2,1)}), bf16[4096,2176]{1,0:T(8,128)(2,1)}) %all-gather.3.cloned.1.call-update) | async-done | bytes 17825808 | tf_op jit(solution)/shard_map/all_gather | solution.py:710
  140.2 1.3 slice.349
  143.4 6.2 pairs.1.k_ref.v_ref
  149.6 16.3 %triple.1.q_ref.k_ref.v_ref = bf16[1024,3072]{1,0:T(8,128)(2,1)} custom-call(bf16[1024,1024]{1,0:T(8,128)(2,1)} %target_ref.7, bf16[1024,128]{1,0:T(8,128)(2,1)} %fusion.token_ref, bf16[128,1024]{1,0:T(8,128)(2,1)} %pad.15.lang_ref, bf16[4,1024,2176]{2,1,0:T(8,128)(2,1)} %bitcast.54), custom_call_target="tpu_custom_call" | custom-call | flops 100663296 | bytes 262144 | tf_op jit(solution)/shard_map/triple/pallas_call | solution.py:84
  165.9 26.8 %attend.2 = (bf16[1024,1024]{1,0:T(8,128)(2,1)}, f32[1024,128]{1,0:T(8,128)}) custom-call(bf16[1024,3072]{1,0:T(8,128)(2,1)} %triple.1.q_ref.k_ref.v_ref, bf16[1024,3072]{1,0:T(8,128)(2,1)} %triple.1.q_ref.k_ref.v_ref, bf16[1024,3072]{1,0:T(8,128)(2,1)} %triple.1.q_ref.k_ref.v_ref, s32[1024,1]{1,0:T(8,128)} %copy.53.own_ref, s32[1,1024]{1,0:T(1,128)} %other_ref.7), custom_call_target="tpu_custom_call" | custom-call | flops 250000000 | bytes 196608 | tf_op jit(solution)/shard_map/attend/pallas_call | solution.py:173
  193.2 10.8 %middle.1 = (f32[1024,1024]{1,0:T(8,128)}, f32[1024,1]{1,0:T(8,128)}, bf16[1024,1024]{1,0:T(8,128)(2,1)}, bf16[1024,1024]{1,0:T(8,128)(2,1)}) custom-call(bf16[1024,1024]{1,0:T(8,128)(2,1)} %get-tuple-element.92.mix_ref.left_ref, bf16[1024,1024]{1,0:T(8,128)(2,1)} %target_ref.7, bf16[1024,128]{1,0:T(8,128)(2,1)} %fusion.token_ref, ...), custom_call_target="tpu_custom_call" | custom-call | flops 67108864 | bytes 262144 | tf_op jit(solution)/shard_map/middle/pallas_call | solution.py:313
  204.0 26.6 %attend.3 = (bf16[1024,1024]{1,0:T(8,128)(2,1)}, f32[1024,128]{1,0:T(8,128)}) custom-call(bf16[1024,1024]{1,0:T(8,128)(2,1)} %get-tuple-element.93.q_ref, bf16[512,2048]{1,0:T(8,128)(2,1)} %pairs.1.k_ref.v_ref, bf16[512,2048]{1,0:T(8,128)(2,1)} %pairs.1.k_ref.v_ref, s32[1024,1]{1,0:T(8,128)} %copy.53.own_ref, s32[1,512]{1,0:T(1,128)} %other_ref.6), custom_call_target="tpu_custom_call" | custom-call | flops 250000000 | bytes 196608 | tf_op jit(solution)/shard_map/attend/pallas_call | solution.py:173
  230.7 23.3 %all-gather.5.cloned.1.call-done = bf16[4096,2048]{1,0:T(8,128)(2,1)} async-done(((bf16[128,2048]{1,0:T(8,128)(2,1)}), bf16[4096,2048]{1,0:T(8,128)(2,1)}) %all-gather.5.cloned.1.call-update) | async-done | bytes 16777232 | tf_op jit(solution)/shard_map/all_gather | solution.py:710
  254.0 57.7 %feed.1 = (bf16[1024,1024]{1,0:T(8,128)(2,1)}, bf16[1024,1024]{1,0:T(8,128)(2,1)}, bf16[1024,4096]{1,0:T(8,128)(2,1)}, bf16[1024,1024]{1,0:T(8,128)(2,1)}, bf16[...) custom-call(bf16[1024,1024]{1,0:T(8,128)(2,1)} %get-tuple-element.94, ...), custom_call_target="tpu_custom_call" | custom-call | flops 603979776 | bytes 983040 | tf_op jit(solution)/shard_map/feed/pallas_call | solution.py:443
  311.7 18.6 %weight_grad.8.rest_0_ = bf16[8,4,128,2048]{3,2,1,0:T(8,128)(2,1)} custom-call(s32[12]{0:T(128)} %get-tuple-element.216.table_ref, bf16[1024,4096]{1,0:T(8,128)(2,1)} %get-tuple-element.102.left_ref, bf16[1024,1024]{1,0:T(8,128)(2,1)} %get-tuple-element.103.right_ref), custom_call_target="tpu_custom_call" | custom-call | flops 134217728 | bytes 327680 | tf_op jit(solution)/shard_map/weight_grad/pallas_call | solution.py:593
  330.3 16.4 %weight_grad.9 = bf16[8,4,128,2048]{3,2,1,0:T(8,128)(2,1)} custom-call(s32[12]{0:T(128)} %get-tuple-element.216.table_ref, bf16[1024,1024]{1,0:T(8,128)(2,1)} %get-tuple-element.100.left_ref, bf16[1024,4096]{1,0:T(8,128)(2,1)} %get-tuple-element.101.right_ref, bf16[8,4,128,2048]{3,2,1,0:T(8,128)(2,1)} %weight_grad.8.rest_0_), custom_call_target="tpu_custom_call", output_to_operand_aliasing={{}: (3, {})} | custom-call | flops 134217728 | bytes 327680 | tf_op jit(solution)/shard_map/weight_grad/pallas_call | solution.py:593
  346.7 42.2 %attend_back.2 = (bf16[1024,1024]{1,0:T(8,128)(2,1)}, bf16[512,2048]{1,0:T(8,128)(2,1)}) custom-call(bf16[1024,1024]{1,0:T(8,128)(2,1)} %get-tuple-element.93.q_ref, bf16[512,2048]{1,0:T(8,128)(2,1)} %pairs.1.k_ref.v_ref, bf16[512,2048]{1,0:T(8,128)(2,1)} %pairs.1.k_ref.v_ref, bf16[1024,1024]{1,0:T(8,128)(2,1)} %get-tuple-element.104.grad_ref, ...), custom_call_target="tpu_custom_call" | custom-call | flops 625000000 | bytes 262144 | tf_op jit(solution)/shard_map/attend_back/pallas_call | solution.py:272
  389.0 8.8 %weight_grad.10 = (bf16[4,4,128,768]{3,2,1,0:T(8,128)(2,1)}, bf16[4,4,128,768]{3,2,1,0:T(8,128)(2,1)}) custom-call(s32[12]{0:T(128)} %get-tuple-element.215.table_ref, bf16[512,1024]{1,0:T(8,128)(2,1)} %left_ref.1, bf16[512,2048]{1,0:T(8,128)(2,1)} %get-tuple-element.154.right_ref.pairs_ref), custom_call_target="tpu_custom_call" | custom-call | flops 33554432 | bytes 196608 | tf_op jit(solution)/shard_map/weight_grad/pallas_call | solution.py:593
  397.8 11.7 %middle_back.1 = (f32[1024,1024]{1,0:T(8,128)}, bf16[1024,1024]{1,0:T(8,128)(2,1)}, bf16[1024,1024]{1,0:T(8,128)(2,1)}, f32[8,1024]{1,0:T(8,128)}) custom-call(f32[1024,1024]{1,0:T(8,128)} %get-tuple-element.98.residual_ref, bf16[1024,1024]{1,0:T(8,128)(2,1)} %get-tuple-element.120.queries_grad_ref.right_ref, f32[1024,1024]{1,0:T(8,128)} %get-tuple-element.95.normed_ref, ...), custom_call_target="tpu_custom_call" | custom-call | flops 67108864 | bytes 360448 | tf_op jit(solution)/shard_map/middle_back/pallas_call | solution.py:509
  409.5 9.1 %weight_grad.11 = (bf16[4,4,128,768]{3,2,1,0:T(8,128)(2,1)}, bf16[4,4,128,768]{3,2,1,0:T(8,128)(2,1)}) custom-call(s32[12]{0:T(128)} %get-tuple-element.215.table_ref, bf16[1024,1024]{1,0:T(8,128)(2,1)} %get-tuple-element.92.mix_ref.left_ref, bf16[1024,1024]{1,0:T(8,128)(2,1)} %get-tuple-element.110.right_ref, ...), custom_call_target="tpu_custom_call", output_to_operand_aliasing={{0}: (3, {}), {1}: (4, {})} | custom-call | flops 33554432 | bytes 131072 | tf_op jit(solution)/shard_map/weight_grad/pallas_call | solution.py:593
  418.7 9.0 %weight_grad.12 = (bf16[4,4,128,512]{3,2,1,0:T(8,128)(2,1)}, bf16[4,4,128,512]{3,2,1,0:T(8,128)(2,1)}) custom-call(s32[12]{0:T(128)} %get-tuple-element.214.table_ref, bf16[1024,1024]{1,0:T(8,128)(2,1)} %get-tuple-element.119.left_ref, bf16[1024,1024]{1,0:T(8,128)(2,1)} %get-tuple-element.120.queries_grad_ref.right_ref), custom_call_target="tpu_custom_call" | custom-call | flops 33554432 | bytes 131072 | tf_op jit(solution)/shard_map/weight_grad/pallas_call | solution.py:593
  427.7 9.3 %weight_grad.13 = (bf16[4,4,128,512]{3,2,1,0:T(8,128)(2,1)}, bf16[4,4,128,512]{3,2,1,0:T(8,128)(2,1)}) custom-call(s32[12]{0:T(128)} %get-tuple-element.214.table_ref, bf16[1024,1024]{1,0:T(8,128)(2,1)} %get-tuple-element.94.mix_ref.left_ref, bf16[1024,1024]{1,0:T(8,128)(2,1)} %get-tuple-element.118.right_ref, ...), custom_call_target="tpu_custom_call", output_to_operand_aliasing={{0}: (3, {}), {1}: (4, {})} | custom-call | flops 33554432 | bytes 131072 | tf_op jit(solution)/shard_map/weight_grad/pallas_call | solution.py:593
  437.0 4.5 add_convert_fusion
  441.9 1.3 collective-permute-start.1
  443.2 44.8 %attend_back.3.right_ref.triple_ref = bf16[1024,3072]{1,0:T(8,128)(2,1)} custom-call(bf16[1024,3072]{1,0:T(8,128)(2,1)} %triple.1.q_ref.k_ref.v_ref, bf16[1024,3072]{1,0:T(8,128)(2,1)} %triple.1.q_ref.k_ref.v_ref, bf16[1024,3072]{1,0:T(8,128)(2,1)} %triple.1.q_ref.k_ref.v_ref, bf16[1024,1024]{1,0:T(8,128)(2,1)} %get-tuple-element.125.grad_ref, ...), custom_call_target="tpu_custom_call" | custom-call | flops 625000000 | bytes 262144 | tf_op jit(solution)/shard_map/attend_back/pallas_call | solution.py:272
  488.1 5.3 collective-permute-done.1
  493.4 2.7 add_convert_fusion.8
  496.0 3.2 add_convert_fusion.2
  499.2 2.7 fusion.3
  501.9 1.4 collective-permute-start.3
  503.4 1.5 collective-permute-start.25
  504.9 11.7 %weight_grad.14 = (bf16[4,4,128,384]{3,2,1,0:T(8,128)(2,1)}, bf16[4,4,128,384]{3,2,1,0:T(8,128)(2,1)}) custom-call(s32[12]{0:T(128)} %get-tuple-element.215.table_ref, bf16[1024,1024]{1,0:T(8,128)(2,1)} %target_ref.7, bf16[1024,128]{1,0:T(8,128)(2,1)} %fusion.token_ref, bf16[128,1024]{1,0:T(8,128)(2,1)} %pad.15.lang_ref, ...), custom_call_target="tpu_custom_call" | custom-call | flops 50331648 | bytes 163840 | tf_op jit(solution)/shard_map/weight_grad/pallas_call | solution.py:593
  518.5 11.7 %weight_grad.15 = (bf16[4,4,128,384]{3,2,1,0:T(8,128)(2,1)}, bf16[4,4,128,384]{3,2,1,0:T(8,128)(2,1)}) custom-call(s32[12]{0:T(128)} %get-tuple-element.214.table_ref, bf16[1024,1024]{1,0:T(8,128)(2,1)} %target_ref.7, bf16[1024,128]{1,0:T(8,128)(2,1)} %fusion.token_ref, bf16[128,1024]{1,0:T(8,128)(2,1)} %pad.15.lang_ref, ...), custom_call_target="tpu_custom_call" | custom-call | flops 50331648 | bytes 163840 | tf_op jit(solution)/shard_map/weight_grad/pallas_call | solution.py:593
  530.2 2.2 add_convert_fusion.18
  532.4 1.3 add_convert_fusion.10
  533.7 2.5 collective-permute-start.26
  536.2 7.8 %collective-permute-done.4 = bf16[8,128,512]{2,1,0:T(8,128)(2,1)} collective-permute-done((bf16[8,128,512]{2,1,0:T(8,128)(2,1)}, bf16[8,128,512]{2,1,0:T(8,128)(2,1)}, u32[]{:S(2)}, u32[]{:S(2)}) %collective-permute-start.4) | collective-permute-done | bytes 1048608 | tf_op jit(solution)/shard_map/ppermute | solution.py:743
  544.0 2.3 add_convert_fusion.12
  546.3 2.7 add_convert_fusion.6
  552.8 1.8 collective-permute-start.20
  554.6 1.4 collective-permute-start.6
  556.0 4.1 collective-permute-done.26
  560.1 1.4 add_bitcast_fusion
  561.6 13.4 %target_back.1 = (f32[1024,1024]{1,0:T(8,128)}, f32[16,1024]{1,0:T(8,128)}) custom-call(f32[1024,1024]{1,0:T(8,128)} %get-tuple-element.108.start_ref, bf16[1024,3072]{1,0:T(8,128)(2,1)} %attend_back.3.right_ref.triple_ref, bf16[4,1024,2176]{2,1,0:T(8,128)(2,1)} %bitcast.60, bf16[16,1024]{1,0:T(8,128)(2,1)} %fusion.1.token_t_ref), custom_call_target="tpu_custom_call" | custom-call | flops 100663296 | bytes 327680 | tf_op jit(solution)/shard_map/target_back/pallas_call | solution.py:657
  575.0 1.0 fusion.4
  576.9 7.0 %collective-permute-done.6 = bf16[8,128,384]{2,1,0:T(8,128)(2,1)} collective-permute-done((bf16[8,128,384]{2,1,0:T(8,128)(2,1)}, bf16[8,128,384]{2,1,0:T(8,128)(2,1)}, u32[]{:S(2)}, u32[]{:S(2)}) %collective-permute-start.6) | collective-permute-done | bytes 786464 | tf_op jit(solution)/shard_map/ppermute | solution.py:743
  583.9 2.1 add_convert_fusion.16
  586.0 2.8 add_convert_fusion.4
  590.4 1.2 add_convert_fusion.21
  591.5 1.6 collective-permute-start.23
  596.3 2.6 collective-permute-done.9
  598.9 1.5 collective-permute-start.10
  600.4 2.6 collective-permute-start.24
  603.2 1.3 collective-permute-start.11
  604.5 4.7 collective-permute-done.24
  609.3 1.5 collective-permute-start.16
  612.2 6.2 memory_back.1
  618.9 1.3 reshape.159
  621.4 8.4 %collective-permute-done.16 = bf16[8,128,384]{2,1,0:T(8,128)(2,1)S(1)} collective-permute-done((bf16[8,128,384]{2,1,0:T(8,128)(2,1)S(1)}, bf16[8,128,384]{2,1,0:T(8,128)(2,1)S(1)}, u32[]{:S(2)}, u32[]{:S(2)}) %collective-permute-start.16) | collective-permute-done | bytes 786464 | tf_op jit(solution)/shard_map/ppermute | solution.py:743
  631.1 5.1 collective-permute-done.13
  636.3 1.5 collective-permute-start.14
  638.0 1.9 collective-permute-start.18
  639.9 4.3 collective-permute-done.14
  644.3 2.9 collective-permute-start.15
  647.4 3.4 collective-permute-start.19
  650.9 2.4 collective-permute-done.15
  653.3 2.3 collective-permute-done.19
  (148 shorter events, 28.9 us)
Async XLA Ops:
  7.2 131.4 %copy-start.23 = (s32[4]{0:T(128)S(1)}, s32[4]{0:T(128)}, u32[]{:S(2)}) copy-start(s32[4]{0:T(128)} %constant.24.clone) | copy-start | bytes 52
  7.2 131.4 %copy-start.21 = (s32[8]{0:T(128)S(1)}, s32[8]{0:T(128)}, u32[]{:S(2)}) copy-start(s32[8]{0:T(128)} %constant.25.clone) | copy-start | bytes 100
  7.2 131.4 %copy-start.22 = (s32[8]{0:T(128)S(1)}, s32[8]{0:T(128)}, u32[]{:S(2)}) copy-start(s32[8]{0:T(128)} %constant.26.clone) | copy-start | bytes 100
  7.2 130.3 %copy-start.14 = (s32[1,1024]{1,0:T(1,128)S(1)}, s32[1,1024]{1,0:T(1,128)}, u32[]{:S(2)}) copy-start(s32[1,1024]{1,0:T(1,128)} %other_ref.7) | copy-start | bytes 12292
  7.2 132.0 %copy-start.20 = (s32[1,8]{1,0:T(1,128)S(1)}, s32[1,8]{1,0:T(1,128)}, u32[]{:S(2)}) copy-start(s32[1,8]{1,0:T(1,128)} %param.27) | copy-start | bytes 100
  7.2 130.2 %all-gather.3.cloned.1.call-start = ((), (), s32[]{:S(2)}) async-start(), calls=%async_computation.1 | async-start | bytes 18382848 | tf_op jit(solution)/shard_map/all_gather | solution.py:710
  14.0 0.8 copy-start.7
  14.8 239.2 %all-gather.5.cloned.1.call-start = ((), (), s32[]{:S(2)}) async-start(), calls=%async_computation.2 | async-start | bytes 17301504 | tf_op jit(solution)/shard_map/all_gather | solution.py:710
  137.5 361.8 %reduce-scatter.2.cloned.1.call-start = ((), (), s32[]{:S(2)}) async-start(), calls=%async_computation.3 | async-start | bytes 18874368 | tf_op jit(solution)/shard_map/reduce_scatter | solution.py:772
  418.6 18.4 %collective-permute-start = (bf16[16,128,768]{2,1,0:T(8,128)(2,1)}, bf16[16,128,768]{2,1,0:T(8,128)(2,1)}, u32[]{:S(2)}, u32[]{:S(2)}) collective-permute-start(bf16[16,128,768]{2,1,0:T(8,128)(2,1)} %bitcast.69), channel_id=1, source_target_pairs={{0,1},{1,0},{2,3},{3,2},{4,5},{5,4},{6,7},{7,6},{8,9},{9,8},{10,11... | collective-permute-start | bytes 9437192 | tf_op jit(solution)/shard_map/ppermute | solution.py:743
  427.7 9.3 %copy-start = (bf16[4,4,128,768]{3,2,1,0:T(8,128)(2,1)S(1)}, bf16[4,4,128,768]{3,2,1,0:T(8,128)(2,1)}, u32[]{:S(2)}) copy-start(bf16[4,4,128,768]{3,2,1,0:T(8,128)(2,1)} %get-tuple-element.114) | copy-start | bytes 9437188
  441.5 54.6 %collective-permute-start.2 = (bf16[16,128,512]{2,1,0:T(8,128)(2,1)}, bf16[16,128,512]{2,1,0:T(8,128)(2,1)}, u32[]{:S(2)}, u32[]{:S(2)}) collective-permute-start(bf16[16,128,512]{2,1,0:T(8,128)(2,1)} %bitcast.15), channel_id=1, source_target_pairs={{0,1},{1,0},{2,3},{3,2},{4,5},{5,4},{6,7},{7,6},{8,9},{9,8},{10,11... | collective-permute-start | bytes 6291464 | tf_op jit(solution)/shard_map/ppermute | solution.py:743
  441.9 51.4 %collective-permute-start.1 = (bf16[8,128,768]{2,1,0:T(8,128)(2,1)}, bf16[8,128,768]{2,1,0:T(8,128)(2,1)}, u32[]{:S(2)}, u32[]{:S(2)}) collective-permute-start(bf16[8,128,768]{2,1,0:T(8,128)(2,1)} %get-tuple-element.128), channel_id=1, source_target_pairs={{0,2},{1,3},{2,0},{3,1},{4,6},{5,7},{6,4},{7,5},{8,10},{9,11},{10,... | collective-permute-start | bytes 4718600 | tf_op jit(solution)/shard_map/ppermute | solution.py:743
  443.2 50.2 %copy-start.2 = (bf16[8,128,768]{2,1,0:T(8,128)(2,1)S(1)}, bf16[8,128,768]{2,1,0:T(8,128)(2,1)}, u32[]{:S(2)}) copy-start(bf16[8,128,768]{2,1,0:T(8,128)(2,1)} %get-tuple-element.127) | copy-start | bytes 4718596
  488.0 8.0 %copy-start.1 = (bf16[4,4,128,512]{3,2,1,0:T(8,128)(2,1)S(1)}, bf16[4,4,128,512]{3,2,1,0:T(8,128)(2,1)}, u32[]{:S(2)}) copy-start(bf16[4,4,128,512]{3,2,1,0:T(8,128)(2,1)} %get-tuple-element.123) | copy-start | bytes 6291460
  501.9 28.3 %collective-permute-start.3 = (bf16[4,128,768]{2,1,0:T(8,128)(2,1)}, bf16[4,128,768]{2,1,0:T(8,128)(2,1)}, u32[]{:S(2)}, u32[]{:S(2)}) collective-permute-start(bf16[4,128,768]{2,1,0:T(8,128)(2,1)} %get-tuple-element.136), channel_id=1, source_target_pairs={{0,4},{1,5},{2,6},{3,7},{4,0},{5,1},{6,2},{7,3},{8,12},{9,13},{10,... | collective-permute-start | bytes 2359304 | tf_op jit(solution)/shard_map/ppermute | solution.py:743
  503.4 29.0 %collective-permute-start.25 = (bf16[2,128,2048]{2,1,0:T(8,128)(2,1)}, bf16[2,128,2048]{2,1,0:T(8,128)(2,1)}, u32[]{:S(2)}, u32[]{:S(2)}) collective-permute-start(bf16[2,128,2048]{2,1,0:T(8,128)(2,1)} %bitcast.18), channel_id=1, source_target_pairs={{0,8},{1,9},{2,10},{3,11},{4,12},{5,13},{6,14},{7,15},{8,0},{9,1},... | collective-permute-start | bytes 3145736 | tf_op jit(solution)/shard_map/ppermute | solution.py:743
  516.6 29.7 %collective-permute-start.5 = (bf16[16,128,384]{2,1,0:T(8,128)(2,1)}, bf16[16,128,384]{2,1,0:T(8,128)(2,1)}, u32[]{:S(2)}, u32[]{:S(2)}) collective-permute-start(bf16[16,128,384]{2,1,0:T(8,128)(2,1)} %bitcast.81), channel_id=1, source_target_pairs={{0,1},{1,0},{2,3},{3,2},{4,5},{5,4},{6,7},{7,6},{8,9},{9,8},{10,11... | collective-permute-start | bytes 4718600 | tf_op jit(solution)/shard_map/ppermute | solution.py:743
  516.8 27.2 %collective-permute-start.4 = (bf16[8,128,512]{2,1,0:T(8,128)(2,1)}, bf16[8,128,512]{2,1,0:T(8,128)(2,1)}, u32[]{:S(2)}, u32[]{:S(2)}) collective-permute-start(bf16[8,128,512]{2,1,0:T(8,128)(2,1)} %get-tuple-element.138), channel_id=1, source_target_pairs={{0,4},{1,5},{2,6},{3,7},{4,0},{5,1},{6,2},{7,3},{8,12},{9,13},{10,... | collective-permute-start | bytes 3145736 | tf_op jit(solution)/shard_map/ppermute | solution.py:743
  532.4 13.9 %copy-start.6 = (bf16[4,4,128,384]{3,2,1,0:T(8,128)(2,1)S(1)}, bf16[4,4,128,384]{3,2,1,0:T(8,128)(2,1)}, u32[]{:S(2)}) copy-start(bf16[4,4,128,384]{3,2,1,0:T(8,128)(2,1)} %get-tuple-element.132) | copy-start | bytes 4718596
  533.7 26.4 %collective-permute-start.26 = (bf16[1,128,2048]{2,1,0:T(8,128)(2,1)S(1)}, bf16[1,128,2048]{2,1,0:T(8,128)(2,1)}, u32[]{:S(2)}, u32[]{:S(2)}) collective-permute-start(bf16[1,128,2048]{2,1,0:T(8,128)(2,1)S(1)} %add_convert_fusion.10), channel_id=1, source_target_pairs={{0,16},{1,17},{2,18},{3,19},{4,20},{5,21},{6,22},{7,23},{8,24},{9,... | collective-permute-start | bytes 1572872 | tf_op jit(solution)/shard_map/ppermute | solution.py:743
  546.3 3.6 copy-start.19
  546.3 4.1 copy-start.15
  549.0 37.0 %collective-permute-start.7 = (bf16[16,128,384]{2,1,0:T(8,128)(2,1)}, bf16[16,128,384]{2,1,0:T(8,128)(2,1)}, u32[]{:S(2)}, u32[]{:S(2)}) collective-permute-start(bf16[16,128,384]{2,1,0:T(8,128)(2,1)} %bitcast.22), channel_id=1, source_target_pairs={{0,1},{1,0},{2,3},{3,2},{4,5},{5,4},{6,7},{7,6},{8,9},{9,8},{10,11... | collective-permute-start | bytes 4718600 | tf_op jit(solution)/shard_map/ppermute | solution.py:743
  552.4 37.9 %collective-permute-start.22 = (bf16[4,128,512]{2,1,0:T(8,128)(2,1)}, bf16[4,128,512]{2,1,0:T(8,128)(2,1)}, u32[]{:S(2)}, u32[]{:S(2)}) collective-permute-start(bf16[4,128,512]{2,1,0:T(8,128)(2,1)} %get-tuple-element.164), channel_id=1, source_target_pairs={{0,2},{1,3},{2,0},{3,1},{4,6},{5,7},{6,4},{7,5},{8,10},{9,11},{10,... | collective-permute-start | bytes 1572872 | tf_op jit(solution)/shard_map/ppermute | solution.py:743
  552.8 23.3 %collective-permute-start.20 = (bf16[2,128,768]{2,1,0:T(8,128)(2,1)}, bf16[2,128,768]{2,1,0:T(8,128)(2,1)S(1)}, u32[]{:S(2)}, u32[]{:S(2)}) collective-permute-start(bf16[2,128,768]{2,1,0:T(8,128)(2,1)} %get-tuple-element.162), channel_id=1, source_target_pairs={{0,8},{1,9},{2,10},{3,11},{4,12},{5,13},{6,14},{7,15},{8,0},{9,1},... | collective-permute-start | bytes 1179656 | tf_op jit(solution)/shard_map/ppermute | solution.py:743
  554.6 29.4 %collective-permute-start.6 = (bf16[8,128,384]{2,1,0:T(8,128)(2,1)}, bf16[8,128,384]{2,1,0:T(8,128)(2,1)}, u32[]{:S(2)}, u32[]{:S(2)}) collective-permute-start(bf16[8,128,384]{2,1,0:T(8,128)(2,1)} %get-tuple-element.147), channel_id=1, source_target_pairs={{0,2},{1,3},{2,0},{3,1},{4,6},{5,7},{6,4},{7,5},{8,10},{9,11},{10,... | collective-permute-start | bytes 2359304 | tf_op jit(solution)/shard_map/ppermute | solution.py:743
  575.0 1.1 copy-start.3
  575.0 11.0 %copy-start.5 = (bf16[4,4,128,384]{3,2,1,0:T(8,128)(2,1)S(1)}, bf16[4,4,128,384]{3,2,1,0:T(8,128)(2,1)}, u32[]{:S(2)}) copy-start(bf16[4,4,128,384]{3,2,1,0:T(8,128)(2,1)} %get-tuple-element.141) | copy-start | bytes 4718596
  576.1 12.7 %copy-start.10 = (bf16[2,128,768]{2,1,0:T(8,128)(2,1)}, bf16[2,128,768]{2,1,0:T(8,128)(2,1)S(1)}, u32[]{:S(2)}) copy-start(bf16[2,128,768]{2,1,0:T(8,128)(2,1)S(1)} %collective-permute-done.20) | copy-start | bytes 1179652
  576.9 17.0 %collective-permute-start.21 = (bf16[1,128,768]{2,1,0:T(8,128)(2,1)}, bf16[1,128,768]{2,1,0:T(8,128)(2,1)}, u32[]{:S(2)}, u32[]{:S(2)}) collective-permute-start(bf16[1,128,768]{2,1,0:T(8,128)(2,1)} %add_convert_fusion.22), channel_id=1, source_target_pairs={{0,16},{1,17},{2,18},{3,19},{4,20},{5,21},{6,22},{7,23},{8,24},{9,... | collective-permute-start | bytes 589832 | tf_op jit(solution)/shard_map/ppermute | solution.py:743
  586.0 2.8 copy-start.13
  586.0 2.8 copy-start.16
  586.0 2.8 copy-start.17
  586.0 2.8 copy-start.18
  586.0 3.3 copy-start.12
  589.4 4.5 copy-start.4
  590.2 3.7 copy-start.11
  590.3 2.9 collective-permute-start.8
  591.5 17.8 %copy-start.8 = (bf16[8,128,384]{2,1,0:T(8,128)(2,1)S(1)}, bf16[8,128,384]{2,1,0:T(8,128)(2,1)}, u32[]{:S(2)}) copy-start(bf16[8,128,384]{2,1,0:T(8,128)(2,1)} %get-tuple-element.160) | copy-start | bytes 2359300
  591.5 8.9 %collective-permute-start.23 = (bf16[2,128,512]{2,1,0:T(8,128)(2,1)S(1)}, bf16[2,128,512]{2,1,0:T(8,128)(2,1)S(1)}, u32[]{:S(2)}, u32[]{:S(2)}) collective-permute-start(bf16[2,128,512]{2,1,0:T(8,128)(2,1)S(1)} %get-tuple-element.190), channel_id=1, source_target_pairs={{0,8},{1,9},{2,10},{3,11},{4,12},{5,13},{6,14},{7,15},{8,0},{9,1},... | collective-permute-start | bytes 786440 | tf_op jit(solution)/shard_map/ppermute | solution.py:743
  593.2 18.4 %copy-start.9 = (bf16[4,128,384]{2,1,0:T(8,128)(2,1)S(1)}, bf16[4,128,384]{2,1,0:T(8,128)(2,1)}, u32[]{:S(2)}) copy-start(bf16[4,128,384]{2,1,0:T(8,128)(2,1)} %get-tuple-element.158) | copy-start | bytes 1179652
  593.2 5.7 collective-permute-start.9
  598.9 4.3 collective-permute-start.10
  600.4 8.8 %collective-permute-start.24 = (bf16[1,128,512]{2,1,0:T(8,128)(2,1)S(1)}, bf16[1,128,512]{2,1,0:T(8,128)(2,1)S(1)}, u32[]{:S(2)}, u32[]{:S(2)}) collective-permute-start(bf16[1,128,512]{2,1,0:T(8,128)(2,1)S(1)} %add_convert_fusion.28), channel_id=1, source_target_pairs={{0,16},{1,17},{2,18},{3,19},{4,20},{5,21},{6,22},{7,23},{8,24},{9,... | collective-permute-start | bytes 393224 | tf_op jit(solution)/shard_map/ppermute | solution.py:743
  603.2 7.6 %collective-permute-start.11 = (f32[2,27,32]{2,1,0:T(8,128)S(1)}, f32[2,27,32]{2,1,0:T(8,128)S(1)}, u32[]{:S(2)}, u32[]{:S(2)}) collective-permute-start(f32[2,27,32]{2,1,0:T(8,128)S(1)} %get-tuple-element.204), channel_id=1, source_target_pairs={{0,8},{1,9},{2,10},{3,11},{4,12},{5,13},{6,14},{7,15},{8,0},{9,1},... | collective-permute-start | bytes 20744 | tf_op jit(solution)/shard_map/ppermute | solution.py:743
  609.3 20.5 %collective-permute-start.16 = (bf16[8,128,384]{2,1,0:T(8,128)(2,1)S(1)}, bf16[8,128,384]{2,1,0:T(8,128)(2,1)S(1)}, u32[]{:S(2)}, u32[]{:S(2)}) collective-permute-start(bf16[8,128,384]{2,1,0:T(8,128)(2,1)S(1)} %copy-done.8), channel_id=1, source_target_pairs={{0,4},{1,5},{2,6},{3,7},{4,0},{5,1},{6,2},{7,3},{8,12},{9,13},{10,... | collective-permute-start | bytes 2359304 | tf_op jit(solution)/shard_map/ppermute | solution.py:743
  610.8 7.6 %collective-permute-start.12 = (f32[1,27,32]{2,1,0:T(8,128)S(1)}, f32[1,27,32]{2,1,0:T(8,128)S(1)}, u32[]{:S(2)}, u32[]{:S(2)}) collective-permute-start(f32[1,27,32]{2,1,0:T(8,128)S(1)} %slice_add_fusion.6), channel_id=1, source_target_pairs={{0,16},{1,17},{2,18},{3,19},{4,20},{5,21},{6,22},{7,23},{8,24},{9,... | collective-permute-start | bytes 10376 | tf_op jit(solution)/shard_map/ppermute | solution.py:743
  611.6 24.6 %collective-permute-start.13 = (bf16[4,128,384]{2,1,0:T(8,128)(2,1)S(1)}, bf16[4,128,384]{2,1,0:T(8,128)(2,1)S(1)}, u32[]{:S(2)}, u32[]{:S(2)}) collective-permute-start(bf16[4,128,384]{2,1,0:T(8,128)(2,1)S(1)} %copy-done.9), channel_id=1, source_target_pairs={{0,4},{1,5},{2,6},{3,7},{4,0},{5,1},{6,2},{7,3},{8,12},{9,13},{10,... | collective-permute-start | bytes 1179656 | tf_op jit(solution)/shard_map/ppermute | solution.py:743
  630.0 7.8 %collective-permute-start.17 = (bf16[4,128,384]{2,1,0:T(8,128)(2,1)S(1)}, bf16[4,128,384]{2,1,0:T(8,128)(2,1)S(1)}, u32[]{:S(2)}, u32[]{:S(2)}) collective-permute-start(bf16[4,128,384]{2,1,0:T(8,128)(2,1)S(1)} %get-tuple-element.182), channel_id=1, source_target_pairs={{0,2},{1,3},{2,0},{3,1},{4,6},{5,7},{6,4},{7,5},{8,10},{9,11},{10,... | collective-permute-start | bytes 1179656 | tf_op jit(solution)/shard_map/ppermute | solution.py:743
  636.3 7.9 %collective-permute-start.14 = (bf16[2,128,384]{2,1,0:T(8,128)(2,1)S(1)}, bf16[2,128,384]{2,1,0:T(8,128)(2,1)S(1)}, u32[]{:S(2)}, u32[]{:S(2)}) collective-permute-start(bf16[2,128,384]{2,1,0:T(8,128)(2,1)S(1)} %get-tuple-element.192), channel_id=1, source_target_pairs={{0,8},{1,9},{2,10},{3,11},{4,12},{5,13},{6,14},{7,15},{8,0},{9,1},... | collective-permute-start | bytes 589832 | tf_op jit(solution)/shard_map/ppermute | solution.py:743
  638.0 9.4 %collective-permute-start.18 = (bf16[2,128,384]{2,1,0:T(8,128)(2,1)S(1)}, bf16[2,128,384]{2,1,0:T(8,128)(2,1)S(1)}, u32[]{:S(2)}, u32[]{:S(2)}) collective-permute-start(bf16[2,128,384]{2,1,0:T(8,128)(2,1)S(1)} %get-tuple-element.194), channel_id=1, source_target_pairs={{0,8},{1,9},{2,10},{3,11},{4,12},{5,13},{6,14},{7,15},{8,0},{9,1},... | collective-permute-start | bytes 589832 | tf_op jit(solution)/shard_map/ppermute | solution.py:743
  644.3 9.0 %collective-permute-start.15 = (bf16[1,128,384]{2,1,0:T(8,128)(2,1)S(1)}, bf16[1,128,384]{2,1,0:T(8,128)(2,1)S(1)}, u32[]{:S(2)}, u32[]{:S(2)}) collective-permute-start(bf16[1,128,384]{2,1,0:T(8,128)(2,1)S(1)} %add_convert_fusion.32), channel_id=1, source_target_pairs={{0,16},{1,17},{2,18},{3,19},{4,20},{5,21},{6,22},{7,23},{8,24},{9,... | collective-permute-start | bytes 294920 | tf_op jit(solution)/shard_map/ppermute | solution.py:743
  647.4 8.1 %collective-permute-start.19 = (bf16[1,128,384]{2,1,0:T(8,128)(2,1)S(1)}, bf16[1,128,384]{2,1,0:T(8,128)(2,1)S(1)}, u32[]{:S(2)}, u32[]{:S(2)}) collective-permute-start(bf16[1,128,384]{2,1,0:T(8,128)(2,1)S(1)} %add_convert_fusion.30), channel_id=1, source_target_pairs={{0,16},{1,17},{2,18},{3,19},{4,20},{5,21},{6,22},{7,23},{8,24},{9,... | collective-permute-start | bytes 294920 | tf_op jit(solution)/shard_map/ppermute | solution.py:743
Sparse Core Ops, SparseCore 0:
  14.9 122.4 all-gather.2
  140.9 113.0 all-gather.4
  346.9 128.7 reduce-scatter.1

commit v2 on v1

--- a/solution.py
+++ b/solution.py
@@ -72,33 +72,43 @@
     return jnp.sum(matrix, axis=0, keepdims=True)
 
 
-def triple_kernel(target_ref, token_ref, lang_ref, weight_ref, out_ref):
-    start = target_ref[...].astype(f32) + mm(token_ref[...], lang_ref[...])
-    out_ref[...] = mm(start.astype(bf16), weight_ref[0]).astype(bf16)
+def triple_kernel(target_ref, token_ref, lang_ref, weight_ref, out_ref, entry_t_ref, entry_ref):
+    @pl.when(pl.program_id(0) == 0)
+    def _():
+        start = target_ref[...].astype(f32) + mm(token_ref[...], lang_ref[...])
+        entry_ref[...] = start.astype(bf16)
+        entry_t_ref[...] = entry_ref[...].T
+
+    out_ref[...] = mm(entry_ref[...], weight_ref[0]).astype(bf16)
 
 
 def triple_call(target, token_hot, lang_rows, packed, width, at):
     tokens, model = target.shape
     outer = packed.shape[0]
-    step = tokens // 2
     return pl.pallas_call(
         triple_kernel,
-        grid=(outer, 2),
+        grid=(outer,),
         in_specs=[
-            pl.BlockSpec((step, model), lambda o, r: (r, 0)),
-            pl.BlockSpec((step, 128), lambda o, r: (r, 0)),
-            pl.BlockSpec((128, model), lambda o, r: (0, 0)),
+            whole(target.shape), whole(token_hot.shape), whole(lang_rows.shape),
             weight_step(model, width, at),
         ],
-        out_specs=pl.BlockSpec((step, width), lambda o, r: (r, o)),
-        out_shape=jax.ShapeDtypeStruct((tokens, outer * width), bf16),
+        out_specs=[pl.BlockSpec((tokens, width), lambda o: (0, o)), whole((model, tokens))],
+        out_shape=[
+            jax.ShapeDtypeStruct((tokens, outer * width), bf16),
+            jax.ShapeDtypeStruct((model, tokens), bf16),
+        ],
+        scratch_shapes=[pltpu.VMEM((tokens, model), bf16)],
         compiler_params=params(),
         cost_estimate=cost(2 * tokens * model * outer * width, 16 * MIB),
         name="triple",
     )(target, token_hot, lang_rows, packed)
 
 
-def pairs_kernel(memory_ref, weight_ref, out_ref):
+def pairs_kernel(memory_ref, weight_ref, out_ref, memory_t_ref):
+    @pl.when(pl.program_id(0) == 0)
+    def _():
+        memory_t_ref[...] = memory_ref[...].T
+
     out_ref[...] = mm(memory_ref[...], weight_ref[0]).astype(bf16)
 
 
@@ -108,12 +118,12 @@
     return pl.pallas_call(
         pairs_kernel,
         grid=(outer,),
-        in_specs=[
-            pl.BlockSpec((tokens, model), lambda o: (0, 0)),
-            weight_step(model, width, at),
-        ],
-        out_specs=pl.BlockSpec((tokens, width), lambda o: (0, o)),
-        out_shape=jax.ShapeDtypeStruct((tokens, outer * width), bf16),
+        in_specs=[whole(memory.shape), weight_step(model, width, at)],
+        out_specs=[pl.BlockSpec((tokens, width), lambda o: (0, o)), whole((model, tokens))],
+        out_shape=[
+            jax.ShapeDtypeStruct((tokens, outer * width), bf16),
+            jax.ShapeDtypeStruct((model, tokens), bf16),
+        ],
         compiler_params=params(),
         cost_estimate=cost(2 * tokens * model * outer * width, 8 * MIB),
         name="pairs",
@@ -136,7 +146,7 @@
     return pl.multiple_of(jnp.maximum(block_index - 1, 0) * BLOCK, BLOCK)
 
 
-def attend_kernel(causal, window, q_ref, k_ref, v_ref, own_ref, other_ref, mix_ref, level_ref, bias_ref):
+def attend_kernel(causal, window, q_ref, k_ref, v_ref, own_ref, other_ref, mix_ref, mix_t_ref, level_ref, bias_ref):
     start = window_start(pl.program_id(0), causal)
     group = pl.program_id(1)
 
@@ -162,7 +172,9 @@
         probs = (exps * (1.0 / total)).astype(bf16)
         mix = jnp.where(chosen, mm(probs, values), mix)
         levels = jnp.where(lane == group * GROUP + head, row_max + jnp.log(total), levels)
-    mix_ref[...] = mix.astype(bf16)
+    mix = mix.astype(bf16)
+    mix_ref[...] = mix
+    mix_t_ref[...] = mix.T
     level_ref[...] = levels
 
 
@@ -182,10 +194,12 @@
         ],
         out_specs=[
             pl.BlockSpec((BLOCK, width), lambda b, g: (b, g)),
+            pl.BlockSpec((width, BLOCK), lambda b, g: (g, b)),
             pl.BlockSpec((BLOCK, 128), lambda b, g: (b, 0)),
         ],
         out_shape=[
             jax.ShapeDtypeStruct((tokens, model), bf16),
+            jax.ShapeDtypeStruct((model, tokens), bf16),
             jax.ShapeDtypeStruct((tokens, 128), f32),
         ],
         scratch_shapes=[pltpu.VMEM((BLOCK, WINDOW), f32)],
@@ -252,8 +266,8 @@
 
     @pl.when(block_index == blocks - 1)
     def _():
-        other_ref_out[:, pl.ds(columns + shift, width)] = keys_t[rows, :].T.astype(bf16)
-        other_ref_out[:, pl.ds(columns + shift + model, width)] = values_t[rows, :].T.astype(bf16)
+        other_ref_out[:, pl.ds(columns + shift, width)] = keys_t[rows, :].astype(bf16).T
+        other_ref_out[:, pl.ds(columns + shift + model, width)] = values_t[rows, :].astype(bf16).T
 
 
 def attend_back_call(
@@ -292,7 +306,7 @@
 
 def middle_kernel(
     mix_ref, target_ref, token_ref, lang_ref, vec_ref, out_weight_ref, query_weight_ref,
-    normed_ref, rstd_ref, entry_ref, queries_ref,
+    normed_ref, rstd_ref, entry_t_ref, queries_ref,
 ):
     outer, _, width = out_weight_ref.shape
     start = target_ref[...].astype(f32) + mm(token_ref[...], lang_ref[...])
@@ -302,7 +316,7 @@
     normed_ref[...] = normed
     rstd_ref[...] = rstd
     entry = (normed * vec_ref[0:1, :] + vec_ref[3:4, :]).astype(bf16)
-    entry_ref[...] = entry
+    entry_t_ref[...] = entry.T
     for o in range(outer):
         queries_ref[:, o * width:(o + 1) * width] = mm(entry, query_weight_ref[o]).astype(bf16)
 
@@ -325,13 +339,13 @@
         out_specs=[
             pl.BlockSpec((BLOCK, model), row),
             pl.BlockSpec((BLOCK, 1), row),
-            pl.BlockSpec((BLOCK, model), row),
+            pl.BlockSpec((model, BLOCK), lambda r: (0, r)),
             pl.BlockSpec((BLOCK, model), row),
         ],
         out_shape=[
             jax.ShapeDtypeStruct((tokens, model), f32),
             jax.ShapeDtypeStruct((tokens, 1), f32),
-            jax.ShapeDtypeStruct((tokens, model), bf16),
+            jax.ShapeDtypeStruct((model, tokens), bf16),
             jax.ShapeDtypeStruct((tokens, model), bf16),
         ],
         compiler_params=params(),
@@ -343,7 +357,7 @@
 def feed_kernel(
     at_cross, at_in, at_out,
     mix_ref, normed_ref, cot_ref, vec_ref, bias_ref, cross_hbm, in_hbm, out_hbm,
-    layer_ref, entry_ref, act_ref, branch_grad_ref, pre_grad_ref, residual_ref, cross_grad_ref,
+    layer_ref, entry_t_ref, act_ref, branch_grad_t_ref, pre_grad_ref, residual_ref, cross_grad_ref,
     mix_grad_ref, sums_ref, bias_sum_ref,
     cross_weight, in_weight, out_weight, slope, sems,
 ):
@@ -386,7 +400,7 @@
     normed1, rstd1 = normalise(2.0 * first + branch)
     second = normed1 * gain1 + shift1
     entry = second.astype(bf16)
-    entry_ref[...] = entry
+    entry_t_ref[...] = entry.T
     total = 2.0 * second + vec_ref[6:7, :]
     for o in range(outer):
         @pl.when(step == 0)
@@ -408,7 +422,7 @@
     sums_ref[1:2, :] += column_sum(cot)
     back2 = norm_back(cot, gain2, normed2, rstd2)
     branch_grad = back2.astype(bf16)
-    branch_grad_ref[...] = branch_grad
+    branch_grad_t_ref[...] = branch_grad.T
     sums_ref[2:3, :] += column_sum(branch_grad.astype(f32))
     grad_second = 2.0 * back2
     for o in range(outer):
@@ -439,6 +453,8 @@
     row = lambda r: (r, 0)
     blocked = lambda cols: pl.BlockSpec((BLOCK, cols), row)
     anywhere = pl.BlockSpec(memory_space=pl.ANY)
+    turned = pl.BlockSpec((model, BLOCK), lambda r: (0, r))
+    turned_shape = jax.ShapeDtypeStruct((model, tokens), bf16)
     out = lambda cols, kind: jax.ShapeDtypeStruct((tokens, cols), kind)
     return pl.pallas_call(
         functools.partial(feed_kernel, at_cross, at_in, at_out),
@@ -448,13 +464,13 @@
             whole(vec.shape), whole(bias.shape), anywhere, anywhere, anywhere,
         ],
         out_specs=[
-            blocked(model), blocked(model), blocked(hidden), blocked(model), blocked(hidden),
+            blocked(model), turned, blocked(hidden), turned, blocked(hidden),
             blocked(model), blocked(model), blocked(model),
             pl.BlockSpec((8, model), lambda r: (0, 0)),
             pl.BlockSpec((1, hidden), lambda r: (0, 0)),
         ],
         out_shape=[
-            out(model, bf16), out(model, bf16), out(hidden, bf16), out(model, bf16),
+            out(model, bf16), turned_shape, out(hidden, bf16), turned_shape,
             out(hidden, bf16), out(model, f32), out(model, bf16), out(model, bf16),
             jax.ShapeDtypeStruct((8, model), f32),
             jax.ShapeDtypeStruct((1, hidden), f32),
@@ -529,108 +545,118 @@
     )(residual, queries_grad, normed, rstd, vec, packed, packed)
 
 
-def fill_product(table_ref, left_t, right_ref, lo, hi, out_refs):
-    piece, width = out_refs[0].shape[2:]
-    inner = left_t.shape[0] // piece
-    part = inner // len(out_refs)
-    count = min(BLOCK // piece, part)
-    for at, out_ref in enumerate(out_refs):
-        @pl.loop(0, part // count)
-        def _(m):
-            blocks = [
-                left_t[pl.ds(pl.multiple_of(table_ref[at * part + m * count + k] * piece, piece), piece), :]
-                for k in range(count)
+def half_kernel(count, first, table_ref, *refs):
+    lefts, rights = refs[:count], refs[count:2 * count]
+    out_ref, held, sems = refs[2 * count], refs[2 * count + 1:-1], refs[-1]
+    part, _, piece, _ = out_ref.shape
+    step = pl.program_id(0)
+
+    def copy(at, row):
+        source = pl.multiple_of(table_ref[first + row] * piece, piece)
+        return pltpu.make_async_copy(
+            lefts[at].at[pl.ds(source, piece), :], held[at].at[pl.ds(row * piece, piece), :],
+            sems.at[at, row],
+        )
+
+    @pl.when(step == 0)
+    def _():
+        for at in range(count):
+            for row in range(part):
+                copy(at, row).start()
+
+    lo = 0
+    for at in range(count):
+        @pl.when(step == 0)
+        def _():
+            for row in range(part):
+                copy(at, row).wait()
+
+        width = rights[at].shape[1]
+        product = mm(held[at][...], rights[at][...]).astype(bf16)
+        out_ref[:, 0, :, lo:lo + width] = product.reshape(part, piece, width)
+        lo += width
+
+
+def half_weight_grads(table, lefts, rights, inner, first):
+    outer = table.shape[0] - inner
+    part, piece = inner // 2, lefts[0].shape[0] // inner
+    widths = [right.shape[1] // outer for right in rights]
+    flops = sum(right.size for right in rights) * part * piece * 2
+    return pl.pallas_call(
+        functools.partial(half_kernel, len(lefts), first),
+        grid_spec=pltpu.PrefetchScalarGridSpec(
+            num_scalar_prefetch=1,
+            grid=(outer,),
+            in_specs=[pl.BlockSpec(memory_space=pl.ANY)] * len(lefts) + [
+                pl.BlockSpec((right.shape[0], width), lambda o, table: (0, o))
+                for right, width in zip(rights, widths)
+            ],
+            out_specs=pl.BlockSpec(
+                (part, 1, piece, sum(widths)), lambda o, table: (0, table[inner + o], 0, 0)
+            ),
+            scratch_shapes=[pltpu.VMEM((part * piece, left.shape[1]), bf16) for left in lefts]
+            + [pltpu.SemaphoreType.DMA((len(lefts), part))],
+        ),
+        out_shape=jax.ShapeDtypeStruct((part, outer, piece, sum(widths)), bf16),
+        compiler_params=params(),
+        cost_estimate=cost(flops, 12 * MIB),
+        name="half_weight_grads",
+    )(table, *lefts, *rights)
+
+
+def feed_in_kernel(table_ref, left_ref, right_ref, *rest):
+    out_ref = rest[-1]
+    inner, _, piece, width = out_ref.shape
+    product = mm(left_ref[...], right_ref[...]).astype(bf16)
+    out_ref[:, 0] = product.reshape(inner, piece, width)
+
+
+def feed_out_kernel(table_ref, left_ref, right_ref, out_ref):
+    inner, _, piece, width = out_ref.shape
+    product = mm(left_ref[...], right_ref[...]).astype(bf16)
+    for i in range(inner):
+        for b in range(width // piece):
+            out_ref[i, 0, :, b * piece:(b + 1) * piece] = product[
+                b * piece:(b + 1) * piece, i * piece:(i + 1) * piece
             ]
-            product = mm(jnp.concatenate(blocks, axis=0), right_ref[:, lo:hi]).astype(bf16)
-            out_ref[pl.ds(m * count, count), 0] = product.reshape(count, piece, width)
-
-
-def split_refs(rest, outputs):
-    return rest[-outputs - 1:-1], rest[-1]
-
-
-def weight_kernel(outputs, lo, hi, table_ref, left_ref, right_ref, *rest):
-    out_refs, left_t = split_refs(rest, outputs)
-
-    @pl.when(pl.program_id(0) == 0)
-    def _():
-        left_t[...] = left_ref[...].T
-
-    fill_product(table_ref, left_t, right_ref, lo, hi, out_refs)
-
-
-def entry_weight_kernel(outputs, lo, hi, table_ref, target_ref, token_ref, lang_ref, right_ref, *rest):
-    out_refs, left_t = split_refs(rest, outputs)
-
-    @pl.when(pl.program_id(0) == 0)
-    def _():
-        start = target_ref[...].astype(f32) + mm(token_ref[...], lang_ref[...])
-        left_t[...] = start.astype(bf16).T
-
-    fill_product(table_ref, left_t, right_ref, lo, hi, out_refs)
-
-
-def rows_weight_kernel(outputs, lo, hi, table_ref, left_ref, right_ref, *rest):
-    out_refs, left_t = split_refs(rest, outputs)
-    left_t[...] = left_ref[...].T
-    fill_product(table_ref, left_t, right_ref, lo, hi, out_refs)
-
-
-def weight_call(
-    kernel, table, lefts, left_specs, right, right_spec, inner, model, lo, hi, at, total, outputs, held
-):
-    tokens = right.shape[0]
+
+
+def feed_rows_kernel(table_ref, left_ref, right_ref, out_ref):
+    inner, _, piece, width = out_ref.shape
+    product = mm(left_ref[...].T, right_ref[...]).astype(bf16)
+    out_ref[:, 0] = product.reshape(inner, piece, width)
+
+
+def feed_weight_grad(kernel, table, left, left_spec, right, right_spec, inner, piece, width, at, total, held=None):
     outer = table.shape[0] - inner
-    width = hi - lo
-    operands = list(lefts) + [right]
-    specs = list(left_specs) + [right_spec]
-    aliases = {}
-    for index, item in enumerate(held or ()):
-        aliases[1 + len(operands)] = index
-        operands.append(item)
+    operands, specs = [left, right], [left_spec, right_spec]
+    if held is not None:
+        operands.append(held)
         specs.append(pl.BlockSpec(memory_space=pl.ANY))
-    part = inner // outputs
     return pl.pallas_call(
-        functools.partial(kernel, outputs, lo, hi),
+        kernel,
         grid_spec=pltpu.PrefetchScalarGridSpec(
             num_scalar_prefetch=1,
             grid=(outer,),
             in_specs=specs,
-            out_specs=[
-                pl.BlockSpec(
-                    (part, 1, model // inner, width), lambda o, table: (0, table[inner + o], 0, at)
-                )
-            ] * outputs,
-            scratch_shapes=[pltpu.VMEM((model, tokens), bf16)],
+            out_specs=pl.BlockSpec(
+                (inner, 1, piece, width), lambda o, table: (0, table[inner + o], 0, at)
+            ),
         ),
-        out_shape=[jax.ShapeDtypeStruct((part, outer, model // inner, total), bf16)] * outputs,
-        input_output_aliases=aliases,
+        out_shape=jax.ShapeDtypeStruct((inner, outer, piece, total), bf16),
+        input_output_aliases={} if held is None else {3: 0},
         compiler_params=params(),
-        cost_estimate=cost(2 * tokens * model * outer * width, 4 * MIB + 4 * model * outer * width),
-        name="weight_grad",
+        cost_estimate=cost(8 * left.shape[1] * 1024 * 1024, 24 * MIB),
+        name="feed_weight_grad",
     )(table, *operands)
 
 
-def column_weight_grad(table, left, right, inner, width, at, total, outputs, held=None):
-    tokens, model = left.shape
-    return weight_call(
-        weight_kernel, table, [left], [whole(left.shape)], right,
-        pl.BlockSpec((tokens, width), lambda o, table: (0, o)), inner, model, 0, width, at, total,
-        outputs, held,
-    )
-
-
-def row_weight_grad(table, left, right, inner, at, total, held=None):
-    tokens, width = right.shape
-    rows = left.shape[1] // (table.shape[0] - inner)
-    return weight_call(
-        rows_weight_kernel, table, [left], [pl.BlockSpec((tokens, rows), lambda o, table: (0, o))],
-        right, whole(right.shape), inner, rows, 0, width, at, total, 1, held,
-    )
-
-
-def target_back_kernel(start_ref, triple_ref, weight_ref, token_t_ref, out_ref, lang_ref):
+def entry_back_kernel(
+    start_ref, triple_ref, pairs_ref, weight_ref, pairs_weight_ref, token_t_ref,
+    out_ref, memory_ref, lang_ref,
+):
     outer, _, width = weight_ref.shape
+    pair_width = pairs_weight_ref.shape[2]
 
     @pl.when(pl.program_id(0) == 0)
     def _():
@@ -638,9 +664,7 @@
 
     grad = 2.0 * start_ref[...]
     for o in range(outer):
-        grad = grad + mm_nt(
-            triple_ref[:, o * width:(o + 1) * width], weight_ref[o]
-        )
+        grad = grad + mm_nt(triple_ref[:, o * width:(o + 1) * width], weight_ref[o])
     out_ref[...] = grad
     high = grad.astype(bf16)
     rest = grad - high.astype(f32)
@@ -648,62 +672,45 @@
     low = (rest - mid.astype(f32)).astype(bf16)
     token_t = token_t_ref[...]
     lang_ref[...] += mm(token_t, high) + mm(token_t, mid) + mm(token_t, low)
-
-
-def target_back_call(start_grad, triple_grad, packed, width, at, token_t):
+    memory_grad = mm_nt(pairs_ref[:, 0:pair_width], pairs_weight_ref[0])
+    for o in range(1, outer):
+        memory_grad = memory_grad + mm_nt(
+            pairs_ref[:, o * pair_width:(o + 1) * pair_width], pairs_weight_ref[o]
+        )
+    memory_ref[...] = memory_grad
+
+
+def entry_back_call(start_grad, triple_grad, pairs_grad, packed, width, pairs_packed, pairs_width, at, token_t):
     tokens, model = start_grad.shape
     outer = packed.shape[0]
+    steps = tokens // BLOCK
+    memory_block = pairs_grad.shape[0] // steps
     row = lambda r: (r, 0)
     return pl.pallas_call(
-        target_back_kernel,
-        grid=(tokens // BLOCK,),
+        entry_back_kernel,
+        grid=(steps,),
         in_specs=[
             pl.BlockSpec((BLOCK, model), row),
             pl.BlockSpec((BLOCK, outer * width), row),
-            weight_block(packed, width, at),
+            pl.BlockSpec((memory_block, outer * pairs_width), row),
+            weight_block(packed, width, 0),
+            weight_block(pairs_packed, pairs_width, at),
             pl.BlockSpec((token_t.shape[0], BLOCK), lambda r: (0, r)),
         ],
         out_specs=[
             pl.BlockSpec((BLOCK, model), row),
+            pl.BlockSpec((memory_block, model), row),
             pl.BlockSpec((token_t.shape[0], model), lambda r: (0, 0)),
         ],
         out_shape=[
             jax.ShapeDtypeStruct((tokens, model), f32),
+            jax.ShapeDtypeStruct(pairs_grad.shape[:1] + (model,), f32),
             jax.ShapeDtypeStruct((token_t.shape[0], model), f32),
         ],
         compiler_params=params(),
-        cost_estimate=cost(2 * tokens * model * outer * width, 20 * MIB),
-        name="target_back",
-    )(start_grad, triple_grad, packed, token_t)
-
-
-def memory_back_kernel(pairs_ref, weight_ref, out_ref):
-    outer, _, width = weight_ref.shape
-    grad = mm_nt(pairs_ref[:, 0:width], weight_ref[0])
-    for o in range(1, outer):
-        grad = grad + mm_nt(
-            pairs_ref[:, o * width:(o + 1) * width], weight_ref[o]
-        )
-    out_ref[...] = grad
-
-
-def memory_back_call(pairs_grad, packed, width, at):
-    tokens = pairs_grad.shape[0]
-    outer, model, _ = packed.shape
-    row = lambda r: (r, 0)
-    return pl.pallas_call(
-        memory_back_kernel,
-        grid=(tokens // BLOCK,),
-        in_specs=[
-            pl.BlockSpec((BLOCK, outer * width), row),
-            weight_block(packed, width, at),
-        ],
-        out_specs=pl.BlockSpec((BLOCK, model), row),
-        out_shape=jax.ShapeDtypeStruct((tokens, model), f32),
-        compiler_params=params(),
-        cost_estimate=cost(2 * tokens * model * outer * width, 8 * MIB),
-        name="memory_back",
-    )(pairs_grad, packed)
+        cost_estimate=cost(2 * tokens * model * outer * (width + pairs_width // 2), 40 * MIB),
+        name="entry_back",
+    )(start_grad, triple_grad, pairs_grad, packed, pairs_packed, token_t)
 
 
 def gather(shard, outer):
@@ -711,68 +718,77 @@
     return full.reshape(outer, full.shape[0] // outer, full.shape[1])
 
 
-def bits_of(count):
-    return count.bit_length() - 1
-
-
-def reverse_bits(number, order):
-    last = len(order) - 1
-    return sum(((number >> bit) & 1) << (last - at) for at, bit in enumerate(order))
-
-
-def place_orders(outer, inner, swapped):
-    inner_order = list(range(bits_of(inner)))
-    if swapped and len(inner_order) > 2:
-        inner_order[1], inner_order[2] = inner_order[2], inner_order[1]
-    return inner_order, list(range(bits_of(outer)))
-
-
-def inner_places(inner, order):
-    places = [0] * inner
-    for number in range(inner):
-        places[reverse_bits(number, order)] = number
-    return jnp.array(places, jnp.int32)
-
-
-def together_with(value, *others):
-    return lax.optimization_barrier((value,) + others)
-
-
-def chain_step(state, devices):
-    keep, send, bits = state
-    moved = lax.ppermute(send, both, [(d, d ^ (1 << bits[0])) for d in range(devices)])
-    if len(bits) == 1:
-        return (keep.astype(f32) + moved.astype(f32))[0], None, ()
-    half = keep.shape[0] // 2
-    send = (keep[half:].astype(f32) + moved[half:].astype(f32)).astype(send.dtype)
-    keep = (keep[:half].astype(f32) + moved[:half].astype(f32)).astype(send.dtype)
-    return keep, send, bits[1:]
-
-
-def chain_start(halves, orders, inner):
-    inner_order, outer_order = orders
-    keep, send = [item.reshape((-1,) + item.shape[2:]) for item in halves]
-    return keep, send, tuple(inner_order + [bits_of(inner) + bit for bit in outer_order])
-
-
-def chain_end(state, devices):
-    while state[2]:
-        state = chain_step(state, devices)
-    return state[0]
-
-
-def hold(value, *states):
-    value, parts = lax.optimization_barrier((value, [state[:2] for state in states]))
-    return value, *[(*part, state[2]) for part, state in zip(parts, states)]
+def swap(value, distance, devices):
+    return lax.ppermute(value, both, [(d, d ^ distance) for d in range(devices)])
+
+
+def total_of(pieces, kind):
+    total = pieces[0].astype(f32)
+    for item in pieces[1:]:
+        total = total + item.astype(f32)
+    return total.astype(kind)
+
+
+def hold(*values):
+    return lax.optimization_barrier(values)
+
+
+def core_stage(keep, send, devices):
+    moved = swap(send, 1, devices)
+    return [total_of((keep[k], moved[k]), keep.dtype) for k in range(keep.shape[0])]
+
+
+def plane_stage(parts, devices):
+    moved = [parts[0]] + [swap(parts[k], 2 * k, devices) for k in range(1, len(parts))]
+    return [total_of([item[o] for item in moved], parts[0].dtype) for o in range(parts[0].shape[0])]
+
+
+def outer_stage(parts, inner, devices):
+    moved = [parts[0]] + [swap(parts[k], inner * k, devices) for k in range(1, len(parts))]
+    return total_of(moved, f32)
+
+
+def outer_half(part, inner, devices):
+    half = part.shape[0] // 2
+    moved = swap(part[half:], inner * half, devices)
+    return (part[:half].astype(f32) + moved.astype(f32)).astype(f32 if half == 1 else part.dtype)
 
 
 def inner_scatter(packed):
     inner, outer, rows, columns = packed.shape
     flat = packed.reshape(inner * outer * rows, columns)
     part = lax.psum_scatter(flat, "inner", scatter_dimension=0, tiled=True)
-    part = part.reshape(outer, rows, columns)
-    bits = tuple(bits_of(inner) + bit for bit in range(bits_of(outer)))
-    return part[:outer // 2], part[outer // 2:], bits
+    return part.reshape(outer, rows, columns)
+
+
+def permuted_column(shard, outer, inner, devices):
+    own = lax.axis_index("outer")
+    column = jnp.zeros((outer,) + shard.shape, shard.dtype)
+    for k in range(outer):
+        moved = swap(shard, inner * k, devices) if k else shard
+        column = lax.dynamic_update_slice(column, moved[None], (own ^ k, 0, 0))
+    return column
+
+
+def plane_moves(column, inner, devices):
+    return [column] + [swap(column, 2 * k, devices) for k in range(1, inner // 2)]
+
+
+def plane_place(moves):
+    chip = lax.axis_index("inner") // 2
+    outer, rows, columns = moves[0].shape
+    plane = jnp.zeros((outer, len(moves), rows, columns), moves[0].dtype)
+    for k, item in enumerate(moves):
+        plane = lax.dynamic_update_slice(plane, item[:, None], (0, chip ^ k, 0, 0))
+    return plane
+
+
+def core_place(plane, moved):
+    core = lax.rem(lax.axis_index("inner"), 2)
+    mine = jnp.arange(2)[None, None, :, None, None] == core
+    full = jnp.where(mine, plane[:, :, None], moved[:, :, None])
+    outer, chips, _, rows, columns = full.shape
+    return full.reshape(outer, chips * 2 * rows, columns)
 
 
 def per_device(
@@ -801,27 +817,29 @@
     )
     n_small = small.shape[0]
     small = jnp.pad(small, ((0, rows - n_small), (0, 128 - piece)))
-    shards = [self_qkv, self_out, cross_kv, cross_q, cross_out, small]
-    weights = gather(jnp.concatenate(shards, axis=1), outer)
-    at_small = w3 + 2 * w1 + w2 + w1
+    first_weights = gather(jnp.concatenate([self_qkv, small], axis=1), outer)
+    at_small = w3
+    column = permuted_column(
+        jnp.concatenate([self_out, cross_q, cross_kv, cross_out], axis=1), outer, inner, devices
+    )
+    moves = plane_moves(column, inner, devices)
     if together:
-        shard, weights = lax.optimization_barrier((jnp.concatenate([ffn_in, ffn_out], axis=1), weights))
+        shard, _ = hold(jnp.concatenate([ffn_in, ffn_out], axis=1), column)
         g_in = gather(shard, outer)
         g_out, at_out = g_in, w4
     else:
         g_in = gather(ffn_in, outer)
         g_out, at_out = gather(ffn_out, outer), 0
 
+    first_weights, moves = hold(first_weights, moves)
+    plane = plane_place(moves)
+    core_move = swap(plane, 1, devices)
     my_inner, my_outer = lax.axis_index("inner"), lax.axis_index("outer")
-    straight = place_orders(outer, inner, False)
-    crossed = place_orders(outer, inner, True)
-    outer_order = straight[1]
-    outer_places = jnp.array([reverse_bits(o, outer_order) for o in range(outer)], jnp.int32)
-    outer_places = outer_places ^ reverse_bits(my_outer, outer_order)
-    table_plain = jnp.concatenate([jnp.arange(inner, dtype=jnp.int32), outer_places])
-    table_a = jnp.concatenate([inner_places(inner, straight[0]) ^ my_inner, outer_places])
-    table_b = jnp.concatenate([inner_places(inner, crossed[0]) ^ my_inner, outer_places])
-
+    outer_places = jnp.arange(outer, dtype=jnp.int32) ^ my_outer
+    inner_order = jnp.array(
+        [chip * 2 + core for core in range(2) for chip in range(inner // 2)], jnp.int32
+    ) ^ my_inner
+    table = jnp.concatenate([inner_order, outer_places])
     seg = segment_ids.reshape(-1)
     hot_seg = seg[:, None] == jnp.arange(directions.shape[1])[None, :]
     token_dir = jnp.sum(jnp.where(hot_seg, directions.reshape(1, -1), 0), axis=-1)
@@ -829,106 +847,110 @@
     token_t = (jnp.arange(langs)[:, None] == token_dir[None, :]).astype(bf16)
     own_column = seg[:, None]
 
-    smalls = weights[:, :, at_small:at_small + piece].reshape(devices, rows, piece)[:, :n_small]
+    smalls = first_weights[:, :, at_small:at_small + piece].reshape(devices, rows, piece)[:, :n_small]
     smalls = smalls.transpose(1, 0, 2)
     lang_rows = jnp.pad(smalls[:langs].reshape(langs, model), ((0, 128 - langs), (0, 0)))
     vec = jnp.pad(smalls[langs:langs + 7].reshape(7, model).astype(f32), ((0, 1), (0, 0)))
     in_bias = smalls[langs + 7:].transpose(1, 0, 2).reshape(1, hidden).astype(f32)
 
-    triple = triple_call(target, token_hot, lang_rows, weights, w3, 0)
+    triple, self_entry_t = triple_call(target, token_hot, lang_rows, first_weights, w3, 0)
+    triple, core_move = hold(triple, core_move)
+    weights = core_place(plane, core_move)
     hg = HEADS // GROUP
-    self_mix, self_levels = attend_call(
+    self_mix, self_mix_t, self_levels = attend_call(
         triple, 0, triple, hg, triple, 2 * hg, own_column, segment_ids, True
     )
-    pairs = pairs_call(memory, weights, w2, 2)
-    normed0, rstd0, cross_entry, queries = middle_call(
-        self_mix, target, token_hot, lang_rows, vec, weights, 3, 6, w1
-    )
-    cross_mix, cross_levels = attend_call(
+    pairs, memory_t = pairs_call(memory, weights, w2, 1)
+    normed0, rstd0, cross_entry_t, queries = middle_call(
+        self_mix, target, token_hot, lang_rows, vec, weights, 0, 1, w1
+    )
+    cross_mix, cross_mix_t, cross_levels = attend_call(
         queries, 0, pairs, 0, pairs, hg, own_column, memory_segments, False
     )
     (
-        layer_output, ffn_entry, act, branch_grad, pre_grad, residual1, cross_grad, cross_mix_grad,
-        sums, bias_sum,
+        layer_output, ffn_entry_t, act, branch_grad_t, pre_grad, residual1, cross_grad,
+        cross_mix_grad, sums, bias_sum,
     ) = feed_call(
-        cross_mix, normed0, cotangent, vec, in_bias, weights, w3 + 2 * w1 + w2, g_in, 0, g_out, at_out, w1
-    )
-
+        cross_mix, normed0, cotangent, vec, in_bias, weights, 2 * w1 + w2, g_in, 0, g_out, at_out, w1
+    )
+
+    plain = jnp.concatenate([jnp.arange(inner, dtype=jnp.int32), outer_places])
+    hidden_step = pl.BlockSpec((tokens, w4), lambda o, table: (0, o))
     if together:
-        ffn_grads = row_weight_grad(table_plain, act, branch_grad, inner, 1, 2 * w4)
-        ffn_grads = column_weight_grad(
-            table_plain, ffn_entry, pre_grad, inner, w4, 0, 2 * w4, 1, ffn_grads
+        ffn_grads = feed_weight_grad(
+            feed_out_kernel, plain, branch_grad_t, whole(branch_grad_t.shape), act, hidden_step,
+            inner, rows, model, 1, 2 * w4,
         )
-        ffn_states = [inner_scatter(ffn_grads[0])]
+        ffn_grads = [feed_weight_grad(
+            feed_in_kernel, plain, ffn_entry_t, whole(ffn_entry_t.shape), pre_grad, hidden_step,
+            inner, rows, w4, 0, 2 * w4, ffn_grads,
+        )]
     else:
-        ffn_grads = column_weight_grad(table_plain, ffn_entry, pre_grad, inner, w4, 0, w4, 1)
-        ffn_grads += row_weight_grad(table_plain, act, branch_grad, inner, 0, model)
-        ffn_states = [inner_scatter(item) for item in ffn_grads]
-
-    cross_mix_grad, _ = lax.optimization_barrier((cross_mix_grad, ffn_grads))
+        branch_grad = branch_grad_t.T
+        ffn_grads = [
+            feed_weight_grad(
+                feed_in_kernel, plain, ffn_entry_t, whole(ffn_entry_t.shape), pre_grad, hidden_step,
+                inner, rows, w4, 0, w4,
+            ),
+            feed_weight_grad(
+                feed_rows_kernel, plain, act, hidden_step, branch_grad, whole(branch_grad.shape),
+                inner, ffn_out.shape[0], model, 0, model,
+            ),
+        ]
+    ffn_parts = [inner_scatter(item) for item in ffn_grads]
+
+    cross_mix_grad, _ = hold(cross_mix_grad, ffn_grads)
     queries_grad, pairs_grad = attend_back_call(
         queries, 0, pairs, 0, pairs, hg, cross_mix_grad, cross_levels, own_column, memory_segments, False
     )
     start_grad, self_grad, self_mix_grad, sums0 = middle_back_call(
-        residual1, queries_grad, normed0, rstd0, vec, weights, 6, 3, w1
-    )
-    grads_a = column_weight_grad(table_a, memory, pairs_grad, inner, w2, 0, w2 + w1, 2)
-    grads_a = column_weight_grad(table_a, self_mix, self_grad, inner, w1, 2, w2 + w1, 2, grads_a)
-    state_a = chain_start(grads_a, straight, inner)
-    queries_grad, state_a = hold(queries_grad, state_a)
-    grads_b = column_weight_grad(table_b, cross_entry, queries_grad, inner, w1, 0, 2 * w1, 2)
-    grads_b = column_weight_grad(table_b, cross_mix, cross_grad, inner, w1, 1, 2 * w1, 2, grads_b)
-    state_b = chain_start(grads_b, crossed, inner)
-    state_a = chain_step(state_a, devices)
-    self_mix_grad, state_a, state_b = hold(self_mix_grad, state_a, state_b)
+        residual1, queries_grad, normed0, rstd0, vec, weights, 1, 0, w1
+    )
+    lefts_a = [memory_t, cross_entry_t, cross_mix_t, self_mix_t]
+    rights_a = [pairs_grad, queries_grad, cross_grad, self_grad]
+    send_a = half_weight_grads(table, lefts_a, rights_a, inner, inner // 2)
+    rights_a, send_a = hold(rights_a, send_a)
+    keep_a = half_weight_grads(table, lefts_a, rights_a, inner, 0)
+    parts_a = core_stage(keep_a, send_a, devices)
+    self_mix_grad, parts_a = hold(self_mix_grad, parts_a)
     (triple_grad,) = attend_back_call(
         triple, 0, triple, hg, triple, 2 * hg, self_mix_grad, self_levels, own_column, segment_ids, True
     )
-    state_a, state_b = chain_step(state_a, devices), chain_step(state_b, devices)
-    triple_grad, state_a, state_b, *ffn_states = hold(triple_grad, state_a, state_b, *ffn_states)
-    middle = (w3 + 255) // 256 * 128
-
-    def triple_weight_grad(table, right, lo, hi):
-        return weight_call(
-            entry_weight_kernel, table, [target, token_hot, lang_rows],
-            [whole(target.shape), whole(token_hot.shape), whole(lang_rows.shape)],
-            right, pl.BlockSpec((tokens, w3), lambda o, table: (0, o)), inner, model, lo, hi, 0,
-            hi - lo, 2, None,
-        )
-
-    state_c = chain_start(triple_weight_grad(table_a, triple_grad, 0, middle), straight, inner)
-    triple_grad, state_c = hold(triple_grad, state_c)
-    state_d = chain_start(triple_weight_grad(table_b, triple_grad, middle, w3), crossed, inner)
-    state_a, state_b = chain_step(state_a, devices), chain_step(state_b, devices)
-    state_c = chain_step(state_c, devices)
-    triple_grad, state_a, state_b, state_c, state_d = hold(
-        triple_grad, state_a, state_b, state_c, state_d
-    )
-    target_grad, lang_sum = target_back_call(start_grad, triple_grad, weights, w3, 0, token_t)
-    state_c, state_d = chain_step(state_c, devices), chain_step(state_d, devices)
-    lang_sum, state_c, state_d = hold(lang_sum, state_c, state_d)
+    parts_a = plane_stage(parts_a, devices)
+    triple_grad, parts_a = hold(triple_grad, parts_a)
+    send_c = half_weight_grads(table, [self_entry_t], [triple_grad], inner, inner // 2)
+    triple_grad, send_c = hold(triple_grad, send_c)
+    keep_c = half_weight_grads(table, [self_entry_t], [triple_grad], inner, 0)
+    parts_c = core_stage(keep_c, send_c, devices)
+    done_a = outer_stage(parts_a, inner, devices)
+    triple_grad, parts_c, ffn_parts, done_a = hold(triple_grad, parts_c, ffn_parts, done_a)
+    target_grad, memory_grad, lang_sum = entry_back_call(
+        start_grad, triple_grad, pairs_grad, first_weights, w3, weights, w2, 1, token_t
+    )
+    parts_c = plane_stage(parts_c, devices)
+    ffn_parts = [outer_half(item, inner, devices) for item in ffn_parts]
+    lang_sum, parts_c, ffn_parts = hold(lang_sum, parts_c, ffn_parts)
 
     stacked = jnp.concatenate(
         [lang_sum, sums0[0:1], sums[3:4], sums[0:1], sums0[1:2], sums[4:5], sums[1:2], sums[2:3]], axis=0
     )
     stacked = stacked.reshape(langs + 7, devices, piece).transpose(1, 0, 2)
     stacked = jnp.concatenate([stacked, bias_sum.reshape(devices, ratio, piece)], axis=1)
-    order = table_a[:inner, None] + inner * (inner_places(outer, outer_order) ^ my_outer)[None, :]
+    order = inner_order[:, None] + inner * outer_places[None, :]
     stacked = jnp.take(stacked, order.reshape(-1), axis=0, mode="clip")
-    half = devices // 2
-    state_e = chain_start(
-        [stacked[:half].reshape(inner // 2, outer, n_small, piece),
-         stacked[half:].reshape(inner // 2, outer, n_small, piece)], straight, inner,
-    )
-    pairs_grad, state_e = hold(pairs_grad, state_e)
-    memory_grad = memory_back_call(pairs_grad, weights, w2, 2)
-
-    done_a, done_b, done_c, done_d, extra = [
-        chain_end(state, devices) for state in (state_a, state_b, state_c, state_d, state_e)
-    ]
-    ffn_done = [chain_end(state, devices) for state in ffn_states]
+    stacked = stacked.reshape(2, inner // 2, outer, n_small, piece)
+    parts_e = core_stage(stacked[0], stacked[1], devices)
+    parts_e = plane_stage(parts_e, devices)
+    while ffn_parts[0].shape[0] > 1:
+        ffn_parts = [outer_half(item, inner, devices) for item in ffn_parts]
+    ffn_done = [item[0] for item in ffn_parts]
+    done_c = outer_stage(parts_c, inner, devices)
+    parts_e, ffn_done, done_c = hold(parts_e, ffn_done, done_c)
+    extra = outer_stage(parts_e, inner, devices)
     if together:
-        ffn_in_grad, ffn_out_grad = ffn_done[0][:, :w4], ffn_done[0][:, w4:]
+        ffn_in_grad = ffn_done[0][:, :w4]
+        ffn_out_grad = ffn_done[0][:, w4:].reshape(rows, model // rows, rows)
+        ffn_out_grad = ffn_out_grad.transpose(2, 1, 0).reshape(rows, model)
     else:
         ffn_in_grad, ffn_out_grad = ffn_done
     return (
@@ -936,11 +958,11 @@
         target_grad,
         memory_grad,
         extra[:langs].T,
-        jnp.concatenate([done_c, done_d], axis=1),
-        done_a[:, w2:],
-        done_b[:, :w1],
+        done_c,
+        done_a[:, w2 + 2 * w1:],
+        done_a[:, w2:w2 + w1],
         done_a[:, :w2],
-        done_b[:, w1:],
+        done_a[:, w2 + w1:w2 + 2 * w1],
         ffn_in_grad,
         extra[langs + 7:].reshape(-1),
         ffn_out_grad,

time: 670 us -> 655 us (0.978)
  Pallas kernels: 357 us -> 339 us
  waiting for transfers between devices: 199 us -> 184 us
  starting transfers between devices: 31.8 us -> 41.4 us
    all_gather x2, waiting for transfers between devices: 144 us -> 1.52 us  [gather(): full = lax.all_gather(shard, both, axis=0, tiled=True)]
    ppermute x27 -> x30, waiting for transfers between devices: 54.6 us -> 182 us  [swap(): lax.ppermute(value, both, [(d, d ^ distance) for d in range(devices)])]
    pallas_call x12 -> x9, Pallas kernels: 137 us -> 117 us  [the longest x4 50.2 us: half_weight_grads(): pl.pallas_call(functools.partial(half_kernel, len(lefts), first), grid_sp...]
    convert_element_type x17 -> x3, other arithmetic: 26.1 us -> 10.9 us  [the longest x2 10.5 us: total_of(): return total.astype(kind)]
    select_n x0 -> x1, other arithmetic: none -> 10.1 us  [core_place(): full = jnp.where(mine, plane[:, :, None], moved[:, :, None])]
    ppermute x27 -> x30, starting transfers between devices: 31.7 us -> 41.2 us  [swap(): lax.ppermute(value, both, [(d, d ^ distance) for d in range(devices)])]
    add x6 -> x8, other arithmetic: 0.15 us -> 9.08 us  [the longest x7 9.01 us: total_of(): total = total + item.astype(f32)]
    dynamic_update_slice x0 -> x8, local copies, waits for them, and re-layouts: none -> 7.49 us  [the longest x4 7.38 us: plane_place(): plane = lax.dynamic_update_slice(plane, item[:, None], (0, chip ^ k, 0, 0))]
  transfers between devices with their start and end apart: 30 -> 33, of which waited for: 15 -> 14; matrix products, arithmetic and copies ran while one was open for 8% -> 9% of each run, Pallas kernels for 40% -> 39%
where the time goes in v2:
time: 655 us; the launch traced here: 646 us
  Pallas kernels  339 us (52%)
  waiting for transfers between devices  184 us (28%)
  starting transfers between devices  41.4 us (6%)
  other arithmetic  36.4 us (6%)
  local copies, waits for them, and re-layouts  30.4 us (5%)
  between operations  14.7 us (2%)
    ppermute x30, waiting for transfers between devices, swap(): lax.ppermute(value, both, [(d, d ^ distance) for d in range(devices)])  182 us
    pallas_call x2, Pallas kernels, attend_back_call(): pl.pallas_call(functools.partial(attend_back_kernel, causal, causal), gri...  86.4 us
    pallas_call x1, Pallas kernels, feed_call(): pl.pallas_call(functools.partial(feed_kernel, at_cross, at_in, at_out), g...  58.2 us
    pallas_call x2, Pallas kernels, attend_call(): pl.pallas_call(functools.partial(attend_kernel, causal, WINDOW), grid=(to...  55.4 us
    pallas_call x4, Pallas kernels, half_weight_grads(): pl.pallas_call(functools.partial(half_kernel, len(lefts), first), grid_sp...  50.2 us
    ppermute x30, starting transfers between devices, swap(): lax.ppermute(value, both, [(d, d ^ distance) for d in range(devices)])  41.2 us
    pallas_call x2, Pallas kernels, feed_weight_grad(): pl.pallas_call(kernel, grid_spec=pltpu.PrefetchScalarGridSpec(num_scalar_...  28.1 us
    pallas_call x1, Pallas kernels, entry_back_call(): pl.pallas_call(entry_back_kernel, grid=(steps,), in_specs=[pl.BlockSpec((...  20.6 us
  transfers between devices with their start and end apart: 33, of which 14 were waited for; matrix products, arithmetic and copies ran while one was open for 9% of the time, Pallas kernels for 39%

profile of v2, /device:TPU:0, one launch (start us, length us, event | category | flops | bytes accessed | tf_op | source)
XLA Modules:
  0.0 646.3 jit_solution(2109887802676851381)
XLA Ops:
  8.0 1.5 concatenate.25
  9.5 1.6 fusion.14
  14.7 3.0 collective-permute-start
  17.7 2.6 collective-permute-start.1
  21.3 13.9 %collective-permute-done = bf16[128,1280]{1,0:T(8,128)(2,1)S(1)} collective-permute-done((bf16[128,1280]{1,0:T(8,128)(2,1)S(1)}, bf16[128,1280]{1,0:T(8,128)(2,1)S(1)}, u32[]{:S(2)}, u32[]{:S(2)}) %collective-permute-start) | collective-permute-done | bytes 327712 | tf_op jit(solution)/shard_map/ppermute | solution.py:722
  35.2 12.8 %collective-permute-done.1 = bf16[128,1280]{1,0:T(8,128)(2,1)S(1)} collective-permute-done((bf16[128,1280]{1,0:T(8,128)(2,1)S(1)}, bf16[128,1280]{1,0:T(8,128)(2,1)S(1)}, u32[]{:S(2)}, u32[]{:S(2)}) %collective-permute-start.1) | collective-permute-done | bytes 327712 | tf_op jit(solution)/shard_map/ppermute | solution.py:722
  48.1 1.7 collective-permute-start.3
  49.9 1.5 collective-permute-start.4
  51.7 39.1 %collective-permute-done.3 = bf16[4,128,1280]{2,1,0:T(8,128)(2,1)S(1)} collective-permute-done((bf16[4,128,1280]{2,1,0:T(8,128)(2,1)S(1)}, bf16[4,128,1280]{2,1,0:T(8,128)(2,1)S(1)}, u32[]{:S(2)}, u32[]{:S(2)}) %collective-permute-start.3) | collective-permute-done | bytes 1310752 | tf_op jit(solution)/shard_map/ppermute | solution.py:722
  90.7 33.8 %collective-permute-done.5 = bf16[4,128,1280]{2,1,0:T(8,128)(2,1)} collective-permute-done((bf16[4,128,1280]{2,1,0:T(8,128)(2,1)S(1)}, bf16[4,128,1280]{2,1,0:T(8,128)(2,1)}, u32[]{:S(2)}, u32[]{:S(2)}) %collective-permute-start.5) | collective-permute-done | bytes 1310752 | tf_op jit(solution)/shard_map/ppermute | solution.py:722
  124.6 2.8 broadcast_in_dim.96
  127.4 1.1 bitcast_dynamic-update-slice_fusion.3
  128.5 1.2 bitcast_dynamic-update-slice_fusion.2
  129.7 2.6 bitcast_dynamic-update-slice_fusion.1
  132.3 2.5 bitcast_dynamic-update-slice_fusion
  134.9 1.0 copy.48.own_ref
  137.5 1.3 slice.310
  140.7 11.8 %triple.1 = (bf16[1024,3072]{1,0:T(8,128)(2,1)}, bf16[1024,1024]{1,0:T(8,128)(2,1)}) custom-call(bf16[1024,1024]{1,0:T(8,128)(2,1)} %target_ref.3, bf16[1024,128]{1,0:T(8,128)(2,1)} %fusion.8.token_ref, bf16[128,1024]{1,0:T(8,128)(2,1)} %pad.15.lang_ref, bf16[4,1024,896]{2,1,0:T(8,128)(2,1)} %bitcast.118), custom_call_target="tpu_custom_call" | custom-call | flops 100663296 | bytes 262144 | tf_op jit(solution)/shard_map/triple/pallas_call | solution.py:88
  153.1 10.1 %bitcast_select_fusion.out_weight_ref.query_weight_ref.weight_ref.cross_hbm.pairs_weight_ref = bf16[4,1024,1280]{2,1,0:T(8,128)(2,1)} fusion(pred[1024]{0:T(1024)(128)(4,1)S(1)} %broadcast_in_dim.102, bf16[4,4,128,1280]{3,2,1,0:T(8,128)(2,1)} %collective-permute-done.6, bf16[4,4,128,1280]{3,2,1,0:T(8,128)(2,1)} %bitcast_dynamic-update-slice_fusion), kind=kLoop, calls=%fused_computation.1 | loop fusion | flops 5242880 | bytes 20972544 | tf_op jit(solution)/shard_map/jit(_where)/select_n | solution.py:789
  163.3 6.4 pairs.1
  169.7 27.8 %attend.2 = (bf16[1024,1024]{1,0:T(8,128)(2,1)}, bf16[1024,1024]{1,0:T(8,128)(2,1)}, f32[1024,128]{1,0:T(8,128)}) custom-call(bf16[1024,3072]{1,0:T(8,128)(2,1)} %get-tuple-element.99.q_ref.k_ref.v_ref, bf16[1024,3072]{1,0:T(8,128)(2,1)} %get-tuple-element.99.q_ref.k_ref.v_ref, bf16[1024,3072]{1,0:T(8,128)(2,1)} %get-tuple-element.99.q_ref.k_ref.v_ref, ...), custom_call_target="tpu_custom_call" | custom-call | flops 250000000 | bytes 196608 | tf_op jit(solution)/shard_map/attend/pallas_call | solution.py:185
  197.5 10.8 %middle.1 = (f32[1024,1024]{1,0:T(8,128)}, f32[1024,1]{1,0:T(8,128)}, bf16[1024,1024]{1,0:T(8,128)(2,1)}, bf16[1024,1024]{1,0:T(8,128)(2,1)}) custom-call(bf16[1024,1024]{1,0:T(8,128)(2,1)} %get-tuple-element.100.mix_ref, bf16[1024,1024]{1,0:T(8,128)(2,1)} %target_ref.3, bf16[1024,128]{1,0:T(8,128)(2,1)} %fusion.8.token_ref, ...), custom_call_target="tpu_custom_call" | custom-call | flops 67108864 | bytes 262144 | tf_op jit(solution)/shard_map/middle/pallas_call | solution.py:327
  208.3 27.6 %attend.3 = (bf16[1024,1024]{1,0:T(8,128)(2,1)}, bf16[1024,1024]{1,0:T(8,128)(2,1)}, f32[1024,128]{1,0:T(8,128)}) custom-call(bf16[1024,1024]{1,0:T(8,128)(2,1)} %get-tuple-element.102.q_ref, bf16[512,2048]{1,0:T(8,128)(2,1)} %get-tuple-element.103.k_ref.v_ref, bf16[512,2048]{1,0:T(8,128)(2,1)} %get-tuple-element.103.k_ref.v_ref, s32[1024,1]{1,0:T(8,128)} %copy.48.own_ref, ...), custom_call_target="tpu_custom_call" | custom-call | flops 250000000 | bytes 196608 | tf_op jit(solution)/shard_map/attend/pallas_call | solution.py:185
  235.8 1.5 all-gather.5.cloned.1.call-done
  237.4 58.2 %feed.1 = (bf16[1024,1024]{1,0:T(8,128)(2,1)}, bf16[1024,1024]{1,0:T(8,128)(2,1)}, bf16[1024,4096]{1,0:T(8,128)(2,1)}, bf16[1024,1024]{1,0:T(8,128)(2,1)}, bf16[...) custom-call(bf16[1024,1024]{1,0:T(8,128)(2,1)} %get-tuple-element.10, ...), custom_call_target="tpu_custom_call" | custom-call | flops 603979776 | bytes 983040 | tf_op jit(solution)/shard_map/feed/pallas_call | solution.py:459
  295.5 14.4 %feed_weight_grad.2.rest_0_ = bf16[8,4,128,2048]{3,2,1,0:T(8,128)(2,1)} custom-call(s32[12]{0:T(128)} %get-tuple-element.208.table_ref, bf16[1024,1024]{1,0:T(8,128)(2,1)} %get-tuple-element.112.left_ref, bf16[1024,4096]{1,0:T(8,128)(2,1)} %get-tuple-element.113.right_ref), custom_call_target="tpu_custom_call" | custom-call | flops 134217728 | bytes 393216 | tf_op jit(solution)/shard_map/feed_weight_grad/pallas_call | solution.py:636
  309.9 13.7 %feed_weight_grad.3 = bf16[8,4,128,2048]{3,2,1,0:T(8,128)(2,1)} custom-call(s32[12]{0:T(128)} %get-tuple-element.208.table_ref, bf16[1024,1024]{1,0:T(8,128)(2,1)} %get-tuple-element.110.left_ref, bf16[1024,4096]{1,0:T(8,128)(2,1)} %get-tuple-element.111.right_ref, bf16[8,4,128,2048]{3,2,1,0:T(8,128)(2,1)} %feed_weight_grad.2.rest_0_), custom_call_target="tpu_custom_call", output_to_operand_aliasing={{}: (3, {})} | custom-call | flops 134217728 | bytes 393216 | tf_op jit(solution)/shard_map/feed_weight_grad/pallas_call | solution.py:636
  323.7 42.1 %attend_back.2 = (bf16[1024,1024]{1,0:T(8,128)(2,1)}, bf16[512,2048]{1,0:T(8,128)(2,1)}) custom-call(bf16[1024,1024]{1,0:T(8,128)(2,1)} %get-tuple-element.102.q_ref, bf16[512,2048]{1,0:T(8,128)(2,1)} %get-tuple-element.103.k_ref.v_ref, bf16[512,2048]{1,0:T(8,128)(2,1)} %get-tuple-element.103.k_ref.v_ref, bf16[1024,1024]{1,0:T(8,128)(2,1)} %get-tuple-element.114.grad_ref, ...), custom_call_target="tpu_custom_call" | custom-call | flops 625000000 | bytes 262144 | tf_op jit(solution)/shard_map/attend_back/pallas_call | solution.py:286
  365.7 11.6 %middle_back.1 = (f32[1024,1024]{1,0:T(8,128)}, bf16[1024,1024]{1,0:T(8,128)(2,1)}, bf16[1024,1024]{1,0:T(8,128)(2,1)}, f32[8,1024]{1,0:T(8,128)}) custom-call(f32[1024,1024]{1,0:T(8,128)} %get-tuple-element.108.residual_ref, bf16[1024,1024]{1,0:T(8,128)(2,1)} %get-tuple-element.128.queries_grad_ref.refs_5_, f32[1024,1024]{1,0:T(8,128)} %get-tuple-element.105.normed_ref, ...), custom_call_target="tpu_custom_call" | custom-call | flops 67108864 | bytes 360448 | tf_op jit(solution)/shard_map/middle_back/pallas_call | solution.py:525
  377.3 16.1 %half_weight_grads.4 = bf16[4,4,128,1280]{3,2,1,0:T(8,128)(2,1)} custom-call(s32[12]{0:T(128)} %get-tuple-element.207.table_ref, bf16[1024,512]{1,0:T(8,128)(2,1)} %get-tuple-element.120.refs_0_, bf16[1024,1024]{1,0:T(8,128)(2,1)} %get-tuple-element.121.refs_1_, bf16[1024,1024]{1,0:T(8,128)(2,1)} %get-tuple-element.122.refs_2_, ...), custom_call_target="tpu_custom_call" | custom-call | flops 67108864 | bytes 196608 | tf_op jit(solution)/shard_map/half_weight_grads/pallas_call | solution.py:585
  393.6 15.9 %half_weight_grads.5 = bf16[4,4,128,1280]{3,2,1,0:T(8,128)(2,1)} custom-call(s32[12]{0:T(128)} %get-tuple-element.207.table_ref, bf16[1024,512]{1,0:T(8,128)(2,1)} %get-tuple-element.120.refs_0_, bf16[1024,1024]{1,0:T(8,128)(2,1)} %get-tuple-element.121.refs_1_, bf16[1024,1024]{1,0:T(8,128)(2,1)} %get-tuple-element.122.refs_2_, ...), custom_call_target="tpu_custom_call" | custom-call | flops 67108864 | bytes 196608 | tf_op jit(solution)/shard_map/half_weight_grads/pallas_call | solution.py:585
  409.6 6.5 %fusion.3 = (bf16[4,128,1280]{2,1,0:T(8,128)(2,1)}, bf16[4,128,1280]{2,1,0:T(8,128)(2,1)}, bf16[4,128,1280]{2,1,0:T(8,128)(2,1)}, bf16[4,128,1280]{2,1,0:T(8,128)(2,1)S(1)}) fusion(bf16[4,4,128,1280]{3,2,1,0:T(8,128)(2,1)} %collective-permute-done.7, bf16[4,4,128,1280]{3,2,1,0:T(8,128)(2,1)} %half_weight_grads.5), kind=kLoop, calls=%fused_computation.14 | loop fusion | flops 10485760 | bytes 15728640 | tf_op jit(solution)/shard_map/convert_element_type | solution.py:729
  416.0 1.5 collective-permute-start.10
  417.6 1.4 collective-permute-start.8
  419.5 44.3 %attend_back.3.refs_1_.triple_ref = bf16[1024,3072]{1,0:T(8,128)(2,1)} custom-call(bf16[1024,3072]{1,0:T(8,128)(2,1)} %get-tuple-element.99.q_ref.k_ref.v_ref, bf16[1024,3072]{1,0:T(8,128)(2,1)} %get-tuple-element.99.q_ref.k_ref.v_ref, bf16[1024,3072]{1,0:T(8,128)(2,1)} %get-tuple-element.99.q_ref.k_ref.v_ref, ...), custom_call_target="tpu_custom_call" | custom-call | flops 625000000 | bytes 262144 | tf_op jit(solution)/shard_map/attend_back/pallas_call | solution.py:286
  463.8 4.5 collective-permute-done.10
  468.4 30.3 %collective-permute-done.8 = bf16[4,128,1280]{2,1,0:T(8,128)(2,1)} collective-permute-done((bf16[4,128,1280]{2,1,0:T(8,128)(2,1)}, bf16[4,128,1280]{2,1,0:T(8,128)(2,1)}, u32[]{:S(2)}, u32[]{:S(2)}) %collective-permute-start.8) | collective-permute-done | bytes 1310752 | tf_op jit(solution)/shard_map/ppermute | solution.py:722
  498.7 3.1 fusion.13
  501.8 9.1 %half_weight_grads.6 = bf16[4,4,128,768]{3,2,1,0:T(8,128)(2,1)} custom-call(s32[12]{0:T(128)} %get-tuple-element.207.table_ref, bf16[1024,1024]{1,0:T(8,128)(2,1)} %get-tuple-element.139.refs_0_, bf16[1024,3072]{1,0:T(8,128)(2,1)} %attend_back.3.refs_1_.triple_ref), custom_call_target="tpu_custom_call" | custom-call | flops 50331648 | bytes 196608 | tf_op jit(solution)/shard_map/half_weight_grads/pallas_call | solution.py:585
  511.1 1.5 collective-permute-start.12
  512.6 1.0 collective-permute-start.13
  513.6 1.9 collective-permute-start.14
  515.7 9.1 %half_weight_grads.7 = bf16[4,4,128,768]{3,2,1,0:T(8,128)(2,1)} custom-call(s32[12]{0:T(128)} %get-tuple-element.207.table_ref, bf16[1024,1024]{1,0:T(8,128)(2,1)} %get-tuple-element.139.refs_0_, bf16[1024,3072]{1,0:T(8,128)(2,1)} %attend_back.3.refs_1_.triple_ref), custom_call_target="tpu_custom_call" | custom-call | flops 50331648 | bytes 196608 | tf_op jit(solution)/shard_map/half_weight_grads/pallas_call | solution.py:585
  524.8 3.2 collective-permute-done.12
  528.0 10.4 %collective-permute-done.13 = bf16[128,1280]{1,0:T(8,128)(2,1)} collective-permute-done((bf16[128,1280]{1,0:T(8,128)(2,1)}, bf16[128,1280]{1,0:T(8,128)(2,1)}, u32[]{:S(2)}, u32[]{:S(2)}) %collective-permute-start.13) | collective-permute-done | bytes 327712 | tf_op jit(solution)/shard_map/ppermute | solution.py:722
  538.4 2.2 convert_add_fusion
  540.6 4.1 fusion.7
  544.7 1.4 slice.364
  546.1 7.8 %collective-permute-start.18 = (bf16[2,128,2048]{2,1,0:T(8,128)(2,1)S(1)}, bf16[2,128,2048]{2,1,0:T(8,128)(2,1)S(1)}, u32[]{:S(2)}, u32[]{:S(2)}) collective-permute-start(bf16[2,128,2048]{2,1,0:T(8,128)(2,1)S(1)} %slice.364), channel_id=1, source_target_pairs={{0,16},{1,17},{2,18},{3,19},{4,20},{5,21},{6,22},{7,23},{8,24},{9,... | collective-permute-start | bytes 3145736 | tf_op jit(solution)/shard_map/ppermute | solution.py:722
  553.9 1.5 collective-permute-start.15
  555.9 1.5 collective-permute-start.17
  560.2 20.6 %entry_back.1 = (f32[1024,1024]{1,0:T(8,128)}, f32[512,1024]{1,0:T(8,128)}, f32[16,1024]{1,0:T(8,128)}) custom-call(f32[1024,1024]{1,0:T(8,128)} %get-tuple-element.118.start_ref, bf16[1024,3072]{1,0:T(8,128)(2,1)} %attend_back.3.refs_1_.triple_ref, bf16[512,2048]{1,0:T(8,128)(2,1)} %get-tuple-element.127.refs_4_.pairs_ref, bf16[4,1024,896]{2,1,0:T(8,128)(2,1)} %bitcast.119, ...), custom_call_target="tpu_custom_call" | custom-call | flops 134217728 | bytes 655360 | tf_op jit(solution)/shard_map/entry_back/pallas_call | solution.py:689
  580.8 9.9 %collective-permute-done.16 = bf16[4,128,768]{2,1,0:T(8,128)(2,1)} collective-permute-done((bf16[4,128,768]{2,1,0:T(8,128)(2,1)}, bf16[4,128,768]{2,1,0:T(8,128)(2,1)}, u32[]{:S(2)}, u32[]{:S(2)}) %collective-permute-start.16) | collective-permute-done | bytes 786464 | tf_op jit(solution)/shard_map/ppermute | solution.py:722
  590.7 2.8 fusion.18
  593.5 5.5 collective-permute-done.18
  600.8 1.4 collective-permute-done.19
  602.2 1.5 collective-permute-start.20
  604.3 1.5 collective-permute-start.22
  607.9 1.4 collective-permute-start.25
  609.3 2.4 collective-permute-start.26
  611.7 16.0 %collective-permute-done.24 = bf16[128,768]{1,0:T(8,128)(2,1)S(1)} collective-permute-done((bf16[128,768]{1,0:T(8,128)(2,1)S(1)}, bf16[128,768]{1,0:T(8,128)(2,1)S(1)}, u32[]{:S(2)}, u32[]{:S(2)}) %collective-permute-start.24) | collective-permute-done | bytes 196640 | tf_op jit(solution)/shard_map/ppermute | solution.py:722
  628.8 2.6 collective-permute-start.28
  631.4 1.7 collective-permute-start.29
  635.4 1.6 collective-permute-done.29
  (132 shorter events, 24.4 us)
Async XLA Ops:
  7.2 13.3 %copy-start.5 = (bf16[128,1024]{1,0:T(8,128)(2,1)S(1)}, bf16[128,1024]{1,0:T(8,128)(2,1)}, u32[]{:S(2)}) copy-start(bf16[128,1024]{1,0:T(8,128)(2,1)} %param.31) | copy-start | bytes 786436
  7.2 13.3 %copy-start.4 = (bf16[128,1024]{1,0:T(8,128)(2,1)S(1)}, bf16[128,1024]{1,0:T(8,128)(2,1)}, u32[]{:S(2)}) copy-start(bf16[128,1024]{1,0:T(8,128)(2,1)} %param.33) | copy-start | bytes 786436
  7.2 117.4 %all-gather.3.cloned.1.call-start = ((), (), s32[]{:S(2)}) async-start(), calls=%async_computation.1 | async-start | bytes 7569408 | tf_op jit(solution)/shard_map/all_gather | solution.py:717
  11.2 226.2 %all-gather.5.cloned.1.call-start = ((), (), s32[]{:S(2)}) async-start(), calls=%async_computation.2 | async-start | bytes 17301504 | tf_op jit(solution)/shard_map/all_gather | solution.py:717
  14.7 20.5 %collective-permute-start = (bf16[128,1280]{1,0:T(8,128)(2,1)S(1)}, bf16[128,1280]{1,0:T(8,128)(2,1)S(1)}, u32[]{:S(2)}, u32[]{:S(2)}) collective-permute-start(bf16[128,1280]{1,0:T(8,128)(2,1)S(1)} %constant_dynamic-update-slice_fusion), channel_id=1, source_target_pairs={{0,8},{1,9},{2,10},{3,11},{4,12},{5,13},{6,14},{7,15},{8,0},{9,1},... | collective-permute-start | bytes 983048 | tf_op jit(solution)/shard_map/ppermute | solution.py:722
  17.7 30.3 %collective-permute-start.1 = (bf16[128,1280]{1,0:T(8,128)(2,1)S(1)}, bf16[128,1280]{1,0:T(8,128)(2,1)S(1)}, u32[]{:S(2)}, u32[]{:S(2)}) collective-permute-start(bf16[128,1280]{1,0:T(8,128)(2,1)S(1)} %constant_dynamic-update-slice_fusion), channel_id=1, source_target_pairs={{0,16},{1,17},{2,18},{3,19},{4,20},{5,21},{6,22},{7,23},{8,24},{9,... | collective-permute-start | bytes 983048 | tf_op jit(solution)/shard_map/ppermute | solution.py:722
  20.3 27.7 %collective-permute-start.2 = (bf16[128,1280]{1,0:T(8,128)(2,1)S(1)}, bf16[128,1280]{1,0:T(8,128)(2,1)S(1)}, u32[]{:S(2)}, u32[]{:S(2)}) collective-permute-start(bf16[128,1280]{1,0:T(8,128)(2,1)S(1)} %constant_dynamic-update-slice_fusion), channel_id=1, source_target_pairs={{0,24},{1,25},{2,26},{3,27},{4,28},{5,29},{6,30},{7,31},{8,16},{9,... | collective-permute-start | bytes 983048 | tf_op jit(solution)/shard_map/ppermute | solution.py:722
  48.1 496.6 %reduce-scatter.2.cloned.1.call-start = ((), (), s32[]{:S(2)}) async-start(), calls=%async_computation.3 | async-start | bytes 18874368 | tf_op jit(solution)/shard_map/reduce_scatter | solution.py:760
  48.1 42.6 %collective-permute-start.3 = (bf16[4,128,1280]{2,1,0:T(8,128)(2,1)S(1)}, bf16[4,128,1280]{2,1,0:T(8,128)(2,1)S(1)}, u32[]{:S(2)}, u32[]{:S(2)}) collective-permute-start(bf16[4,128,1280]{2,1,0:T(8,128)(2,1)S(1)} %bitcast_dynamic-update-slice_fusion.4), channel_id=1, source_target_pairs={{0,2},{1,3},{2,0},{3,1},{4,6},{5,7},{6,4},{7,5},{8,10},{9,11},{10,... | collective-permute-start | bytes 3932168 | tf_op jit(solution)/shard_map/ppermute | solution.py:722
  49.9 40.9 %collective-permute-start.4 = (bf16[4,128,1280]{2,1,0:T(8,128)(2,1)S(1)}, bf16[4,128,1280]{2,1,0:T(8,128)(2,1)}, u32[]{:S(2)}, u32[]{:S(2)}) collective-permute-start(bf16[4,128,1280]{2,1,0:T(8,128)(2,1)S(1)} %bitcast_dynamic-update-slice_fusion.4), channel_id=1, source_target_pairs={{0,4},{1,5},{2,6},{3,7},{4,0},{5,1},{6,2},{7,3},{8,12},{9,13},{10,... | collective-permute-start | bytes 3932168 | tf_op jit(solution)/shard_map/ppermute | solution.py:722
  51.4 73.2 %collective-permute-start.5 = (bf16[4,128,1280]{2,1,0:T(8,128)(2,1)S(1)}, bf16[4,128,1280]{2,1,0:T(8,128)(2,1)}, u32[]{:S(2)}, u32[]{:S(2)}) collective-permute-start(bf16[4,128,1280]{2,1,0:T(8,128)(2,1)S(1)} %bitcast_dynamic-update-slice_fusion.4), channel_id=1, source_target_pairs={{0,6},{1,7},{2,4},{3,5},{4,2},{5,3},{6,0},{7,1},{8,14},{9,15},{10,... | collective-permute-start | bytes 3932168 | tf_op jit(solution)/shard_map/ppermute | solution.py:722
  129.7 5.2 copy-start.10
  132.3 3.6 copy-start.14
  132.3 4.2 copy-start.13
  134.8 18.4 %collective-permute-start.6 = (bf16[4,4,128,1280]{3,2,1,0:T(8,128)(2,1)}, bf16[4,4,128,1280]{3,2,1,0:T(8,128)(2,1)}, u32[]{:S(2)}, u32[]{:S(2)}) collective-permute-start(bf16[4,4,128,1280]{3,2,1,0:T(8,128)(2,1)} %bitcast_dynamic-update-slice_fusion), channel_id=1, source_target_pairs={{0,1},{1,0},{2,3},{3,2},{4,5},{5,4},{6,7},{7,6},{8,9},{9,8},{10,11... | collective-permute-start | bytes 15728648 | tf_op jit(solution)/shard_map/ppermute | solution.py:722
  393.4 16.1 %collective-permute-start.7 = (bf16[4,4,128,1280]{3,2,1,0:T(8,128)(2,1)}, bf16[4,4,128,1280]{3,2,1,0:T(8,128)(2,1)}, u32[]{:S(2)}, u32[]{:S(2)}) collective-permute-start(bf16[4,4,128,1280]{3,2,1,0:T(8,128)(2,1)} %half_weight_grads.4), channel_id=1, source_target_pairs={{0,1},{1,0},{2,3},{3,2},{4,5},{5,4},{6,7},{7,6},{8,9},{9,8},{10,11... | collective-permute-start | bytes 15728648 | tf_op jit(solution)/shard_map/ppermute | solution.py:722
  416.0 52.3 %collective-permute-start.10 = (bf16[4,128,1280]{2,1,0:T(8,128)(2,1)}, bf16[4,128,1280]{2,1,0:T(8,128)(2,1)S(1)}, u32[]{:S(2)}, u32[]{:S(2)}) collective-permute-start(bf16[4,128,1280]{2,1,0:T(8,128)(2,1)} %get-tuple-element.137), channel_id=1, source_target_pairs={{0,6},{1,7},{2,4},{3,5},{4,2},{5,3},{6,0},{7,1},{8,14},{9,15},{10,... | collective-permute-start | bytes 3932168 | tf_op jit(solution)/shard_map/ppermute | solution.py:722
  417.6 81.1 %collective-permute-start.8 = (bf16[4,128,1280]{2,1,0:T(8,128)(2,1)}, bf16[4,128,1280]{2,1,0:T(8,128)(2,1)}, u32[]{:S(2)}, u32[]{:S(2)}) collective-permute-start(bf16[4,128,1280]{2,1,0:T(8,128)(2,1)} %get-tuple-element.135), channel_id=1, source_target_pairs={{0,2},{1,3},{2,0},{3,1},{4,6},{5,7},{6,4},{7,5},{8,10},{9,11},{10,... | collective-permute-start | bytes 3932168 | tf_op jit(solution)/shard_map/ppermute | solution.py:722
  418.9 79.7 %collective-permute-start.9 = (bf16[4,128,1280]{2,1,0:T(8,128)(2,1)}, bf16[4,128,1280]{2,1,0:T(8,128)(2,1)}, u32[]{:S(2)}, u32[]{:S(2)}) collective-permute-start(bf16[4,128,1280]{2,1,0:T(8,128)(2,1)} %get-tuple-element.136), channel_id=1, source_target_pairs={{0,4},{1,5},{2,6},{3,7},{4,0},{5,1},{6,2},{7,3},{8,12},{9,13},{10,... | collective-permute-start | bytes 3932168 | tf_op jit(solution)/shard_map/ppermute | solution.py:722
  510.9 29.7 %collective-permute-start.11 = (bf16[4,4,128,768]{3,2,1,0:T(8,128)(2,1)}, bf16[4,4,128,768]{3,2,1,0:T(8,128)(2,1)S(1)}, u32[]{:S(2)}, u32[]{:S(2)}) collective-permute-start(bf16[4,4,128,768]{3,2,1,0:T(8,128)(2,1)} %half_weight_grads.6), channel_id=1, source_target_pairs={{0,1},{1,0},{2,3},{3,2},{4,5},{5,4},{6,7},{7,6},{8,9},{9,8},{10,11... | collective-permute-start | bytes 9437192 | tf_op jit(solution)/shard_map/ppermute | solution.py:722
  511.1 16.9 %collective-permute-start.12 = (bf16[128,1280]{1,0:T(8,128)(2,1)}, bf16[128,1280]{1,0:T(8,128)(2,1)}, u32[]{:S(2)}, u32[]{:S(2)}) collective-permute-start(bf16[128,1280]{1,0:T(8,128)(2,1)} %get-tuple-element.143), channel_id=1, source_target_pairs={{0,8},{1,9},{2,10},{3,11},{4,12},{5,13},{6,14},{7,15},{8,0},{9,1},... | collective-permute-start | bytes 983048 | tf_op jit(solution)/shard_map/ppermute | solution.py:722
  512.6 25.9 %collective-permute-start.13 = (bf16[128,1280]{1,0:T(8,128)(2,1)}, bf16[128,1280]{1,0:T(8,128)(2,1)}, u32[]{:S(2)}, u32[]{:S(2)}) collective-permute-start(bf16[128,1280]{1,0:T(8,128)(2,1)} %get-tuple-element.144), channel_id=1, source_target_pairs={{0,16},{1,17},{2,18},{3,19},{4,20},{5,21},{6,22},{7,23},{8,24},{9,... | collective-permute-start | bytes 983048 | tf_op jit(solution)/shard_map/ppermute | solution.py:722
  513.6 24.9 %collective-permute-start.14 = (bf16[128,1280]{1,0:T(8,128)(2,1)}, bf16[128,1280]{1,0:T(8,128)(2,1)}, u32[]{:S(2)}, u32[]{:S(2)}) collective-permute-start(bf16[128,1280]{1,0:T(8,128)(2,1)} %get-tuple-element.145), channel_id=1, source_target_pairs={{0,24},{1,25},{2,26},{3,27},{4,28},{5,29},{6,30},{7,31},{8,16},{9,... | collective-permute-start | bytes 983048 | tf_op jit(solution)/shard_map/ppermute | solution.py:722
  544.7 11.2 %copy-start.3 = (bf16[4,128,768]{2,1,0:T(8,128)(2,1)S(1)}, bf16[4,128,768]{2,1,0:T(8,128)(2,1)}, u32[]{:S(2)}) copy-start(bf16[4,128,768]{2,1,0:T(8,128)(2,1)} %get-tuple-element.153) | copy-start | bytes 2359300
  544.7 13.3 %copy-start.12 = (f32[8,1024]{1,0:T(8,128)S(1)}, f32[8,1024]{1,0:T(8,128)}, u32[]{:S(2)}) copy-start(f32[8,1024]{1,0:T(8,128)} %get-tuple-element.157) | copy-start | bytes 98308
  544.7 13.9 %copy-start.11 = (f32[1,4096]{1,0:T(1,128)S(1)}, f32[1,4096]{1,0:T(1,128)}, u32[]{:S(2)}) copy-start(f32[1,4096]{1,0:T(1,128)} %get-tuple-element.158) | copy-start | bytes 49156
  546.1 52.9 %collective-permute-start.18 = (bf16[2,128,2048]{2,1,0:T(8,128)(2,1)S(1)}, bf16[2,128,2048]{2,1,0:T(8,128)(2,1)S(1)}, u32[]{:S(2)}, u32[]{:S(2)}) collective-permute-start(bf16[2,128,2048]{2,1,0:T(8,128)(2,1)S(1)} %slice.364), channel_id=1, source_target_pairs={{0,16},{1,17},{2,18},{3,19},{4,20},{5,21},{6,22},{7,23},{8,24},{9,... | collective-permute-start | bytes 3145736 | tf_op jit(solution)/shard_map/ppermute | solution.py:722
  553.9 26.9 %collective-permute-start.15 = (bf16[4,128,768]{2,1,0:T(8,128)(2,1)}, bf16[4,128,768]{2,1,0:T(8,128)(2,1)}, u32[]{:S(2)}, u32[]{:S(2)}) collective-permute-start(bf16[4,128,768]{2,1,0:T(8,128)(2,1)} %get-tuple-element.151), channel_id=1, source_target_pairs={{0,2},{1,3},{2,0},{3,1},{4,6},{5,7},{6,4},{7,5},{8,10},{9,11},{10,... | collective-permute-start | bytes 2359304 | tf_op jit(solution)/shard_map/ppermute | solution.py:722
  555.3 35.4 %collective-permute-start.16 = (bf16[4,128,768]{2,1,0:T(8,128)(2,1)}, bf16[4,128,768]{2,1,0:T(8,128)(2,1)}, u32[]{:S(2)}, u32[]{:S(2)}) collective-permute-start(bf16[4,128,768]{2,1,0:T(8,128)(2,1)} %get-tuple-element.152), channel_id=1, source_target_pairs={{0,4},{1,5},{2,6},{3,7},{4,0},{5,1},{6,2},{7,3},{8,12},{9,13},{10,... | collective-permute-start | bytes 2359304 | tf_op jit(solution)/shard_map/ppermute | solution.py:722
  555.9 34.8 %collective-permute-start.17 = (bf16[4,128,768]{2,1,0:T(8,128)(2,1)S(1)}, bf16[4,128,768]{2,1,0:T(8,128)(2,1)}, u32[]{:S(2)}, u32[]{:S(2)}) collective-permute-start(bf16[4,128,768]{2,1,0:T(8,128)(2,1)S(1)} %copy-done.3), channel_id=1, source_target_pairs={{0,6},{1,7},{2,4},{3,5},{4,2},{5,3},{6,0},{7,1},{8,14},{9,15},{10,... | collective-permute-start | bytes 2359304 | tf_op jit(solution)/shard_map/ppermute | solution.py:722
  560.2 30.6 %copy-start = (bf16[4,128,768]{2,1,0:T(8,128)(2,1)S(1)}, bf16[4,128,768]{2,1,0:T(8,128)(2,1)}, u32[]{:S(2)}) copy-start(bf16[4,128,768]{2,1,0:T(8,128)(2,1)} %get-tuple-element.150) | copy-start | bytes 2359300
  580.8 18.2 %copy-start.2 = (bf16[512,2048]{1,0:T(8,128)(2,1)S(1)}, bf16[512,2048]{1,0:T(8,128)(2,1)}, u32[]{:S(2)}) copy-start(bf16[512,2048]{1,0:T(8,128)(2,1)} %reduce-scatter.2.cloned.1.call-done) | copy-start | bytes 6291460
  593.5 5.9 copy-start.9
  599.9 5.9 copy-start.1
  600.5 6.7 %copy-start.8 = (bf16[128,768]{1,0:T(8,128)(2,1)S(1)}, bf16[128,768]{1,0:T(8,128)(2,1)}, u32[]{:S(2)}) copy-start(bf16[128,768]{1,0:T(8,128)(2,1)} %get-tuple-element.161) | copy-start | bytes 589828
  600.5 7.4 %copy-start.7 = (bf16[128,768]{1,0:T(8,128)(2,1)S(1)}, bf16[128,768]{1,0:T(8,128)(2,1)}, u32[]{:S(2)}) copy-start(bf16[128,768]{1,0:T(8,128)(2,1)} %get-tuple-element.162) | copy-start | bytes 589828
  600.6 8.7 %copy-start.6 = (bf16[128,768]{1,0:T(8,128)(2,1)S(1)}, bf16[128,768]{1,0:T(8,128)(2,1)}, u32[]{:S(2)}) copy-start(bf16[128,768]{1,0:T(8,128)(2,1)} %get-tuple-element.163) | copy-start | bytes 589828
  600.6 1.6 collective-permute-start.19
  600.7 27.9 %collective-permute-start.23 = (bf16[1,128,2048]{2,1,0:T(8,128)(2,1)S(1)}, bf16[1,128,2048]{2,1,0:T(8,128)(2,1)S(1)}, u32[]{:S(2)}, u32[]{:S(2)}) collective-permute-start(bf16[1,128,2048]{2,1,0:T(8,128)(2,1)S(1)} %slice.397), channel_id=1, source_target_pairs={{0,8},{1,9},{2,10},{3,11},{4,12},{5,13},{6,14},{7,15},{8,0},{9,1},... | collective-permute-start | bytes 1572872 | tf_op jit(solution)/shard_map/ppermute | solution.py:722
  602.2 5.7 collective-permute-start.20
  603.8 5.5 collective-permute-start.21
  604.3 7.3 %collective-permute-start.22 = (f32[4,27,32]{2,1,0:T(8,128)S(1)}, f32[4,27,32]{2,1,0:T(8,128)S(1)}, u32[]{:S(2)}, u32[]{:S(2)}) collective-permute-start(f32[4,27,32]{2,1,0:T(8,128)S(1)} %get-tuple-element.190), channel_id=1, source_target_pairs={{0,6},{1,7},{2,4},{3,5},{4,2},{5,3},{6,0},{7,1},{8,14},{9,15},{10,... | collective-permute-start | bytes 41480 | tf_op jit(solution)/shard_map/ppermute | solution.py:722
  607.3 20.5 %collective-permute-start.24 = (bf16[128,768]{1,0:T(8,128)(2,1)S(1)}, bf16[128,768]{1,0:T(8,128)(2,1)S(1)}, u32[]{:S(2)}, u32[]{:S(2)}) collective-permute-start(bf16[128,768]{1,0:T(8,128)(2,1)S(1)} %copy-done.8), channel_id=1, source_target_pairs={{0,8},{1,9},{2,10},{3,11},{4,12},{5,13},{6,14},{7,15},{8,0},{9,1},... | collective-permute-start | bytes 589832 | tf_op jit(solution)/shard_map/ppermute | solution.py:722
  607.9 19.9 %collective-permute-start.25 = (bf16[128,768]{1,0:T(8,128)(2,1)S(1)}, bf16[128,768]{1,0:T(8,128)(2,1)S(1)}, u32[]{:S(2)}, u32[]{:S(2)}) collective-permute-start(bf16[128,768]{1,0:T(8,128)(2,1)S(1)} %copy-done.7), channel_id=1, source_target_pairs={{0,16},{1,17},{2,18},{3,19},{4,20},{5,21},{6,22},{7,23},{8,24},{9,... | collective-permute-start | bytes 589832 | tf_op jit(solution)/shard_map/ppermute | solution.py:722
  609.3 18.5 %collective-permute-start.26 = (bf16[128,768]{1,0:T(8,128)(2,1)S(1)}, bf16[128,768]{1,0:T(8,128)(2,1)S(1)}, u32[]{:S(2)}, u32[]{:S(2)}) collective-permute-start(bf16[128,768]{1,0:T(8,128)(2,1)S(1)} %copy-done.6), channel_id=1, source_target_pairs={{0,24},{1,25},{2,26},{3,27},{4,28},{5,29},{6,30},{7,31},{8,16},{9,... | collective-permute-start | bytes 589832 | tf_op jit(solution)/shard_map/ppermute | solution.py:722
  628.7 6.6 %collective-permute-start.27 = (f32[27,32]{1,0:T(8,128)S(1)}, f32[27,32]{1,0:T(8,128)S(1)}, u32[]{:S(2)}, u32[]{:S(2)}) collective-permute-start(f32[27,32]{1,0:T(8,128)S(1)} %get-tuple-element.165), channel_id=1, source_target_pairs={{0,8},{1,9},{2,10},{3,11},{4,12},{5,13},{6,14},{7,15},{8,0},{9,1},... | collective-permute-start | bytes 10376 | tf_op jit(solution)/shard_map/ppermute | solution.py:722
  628.8 6.6 %collective-permute-start.28 = (f32[27,32]{1,0:T(8,128)S(1)}, f32[27,32]{1,0:T(8,128)S(1)}, u32[]{:S(2)}, u32[]{:S(2)}) collective-permute-start(f32[27,32]{1,0:T(8,128)S(1)} %get-tuple-element.166), channel_id=1, source_target_pairs={{0,16},{1,17},{2,18},{3,19},{4,20},{5,21},{6,22},{7,23},{8,24},{9,... | collective-permute-start | bytes 10376 | tf_op jit(solution)/shard_map/ppermute | solution.py:722
  631.4 5.5 collective-permute-start.29
Sparse Core Ops, SparseCore 0:
  11.4 109.4 all-gather.2
  123.8 113.5 all-gather.4
  323.8 169.7 reduce-scatter.1

commit v3 on v2

--- a/solution.py
+++ b/solution.py
@@ -11,7 +11,8 @@
 HEAD_DIM = 64
 GROUP = 4
 BLOCK = 256
-WINDOW = 512
+CHUNK = 128
+WINDOWS = (256, 384, 512)
 
 epsilon = 1e-05
 masked_score = -1000000000.0
@@ -140,138 +141,170 @@
     return jnp.where(allowed, 0.0, masked_score).astype(f32)
 
 
-def window_start(block_index, causal):
-    if not causal:
-        return 0
-    return pl.multiple_of(jnp.maximum(block_index - 1, 0) * BLOCK, BLOCK)
-
-
-def attend_kernel(causal, window, q_ref, k_ref, v_ref, own_ref, other_ref, mix_ref, mix_t_ref, level_ref, bias_ref):
-    start = window_start(pl.program_id(0), causal)
+def for_window(table_ref, body):
+    block_index = pl.program_id(0)
+    start = pl.multiple_of(table_ref[block_index], CHUNK)
+    chunks = table_ref[pl.num_programs(0) + block_index]
+    for window in WINDOWS:
+        @pl.when(chunks == window // CHUNK)
+        def _():
+            body(start, window)
+
+
+def self_windows(ids):
+    blocks = ids.shape[0] // BLOCK
+    below = jnp.sum(ids[None, :] < ids[::BLOCK][:, None], axis=1)
+    start = below // CHUNK * CHUNK
+    ends = (jnp.arange(blocks) + 1) * BLOCK
+    return jnp.concatenate([start, (ends - start) // CHUNK]).astype(jnp.int32)
+
+
+def cross_windows(ids, others):
+    below = jnp.sum(others[None, :] < ids[::BLOCK][:, None], axis=1)
+    ends = jnp.sum(others[None, :] <= ids[BLOCK - 1::BLOCK][:, None], axis=1)
+    start = below // CHUNK * CHUNK
+    chunks = jnp.clip((ends - start + CHUNK - 1) // CHUNK, WINDOWS[0] // CHUNK, WINDOWS[-1] // CHUNK)
+    start = jnp.minimum(start, others.shape[0] - chunks * CHUNK)
+    return jnp.concatenate([start, chunks]).astype(jnp.int32)
+
+
+def attend_kernel(
+    causal, table_ref, q_ref, k_ref, v_ref, own_ref, other_ref, mix_ref, mix_t_ref, level_ref, bias_ref
+):
     group = pl.program_id(1)
-
-    @pl.when(group == 0)
-    def _():
-        bias_ref[...] = mask_bias(own_ref, other_ref, start, window, causal)
-        level_ref[...] = jnp.zeros_like(level_ref)
-
     width = q_ref.shape[1]
     owner = lax.broadcasted_iota(jnp.int32, (1, width), 1) // HEAD_DIM
     lane = lax.broadcasted_iota(jnp.int32, (1, 128), 1)
-    queries = q_ref[...] * bf16(HEAD_DIM ** -0.5)
-    keys = k_ref[pl.ds(start, window), :]
-    values = v_ref[pl.ds(start, window), :]
-    mix = jnp.zeros(q_ref.shape, f32)
-    levels = level_ref[...]
-    for head in range(GROUP):
-        chosen = owner == head
-        scores = mm_nt(queries * chosen.astype(bf16), keys) + bias_ref[...]
-        row_max = jnp.max(scores, axis=-1, keepdims=True)
-        exps = jnp.exp(scores - row_max)
-        total = jnp.sum(exps, axis=-1, keepdims=True)
-        probs = (exps * (1.0 / total)).astype(bf16)
-        mix = jnp.where(chosen, mm(probs, values), mix)
-        levels = jnp.where(lane == group * GROUP + head, row_max + jnp.log(total), levels)
-    mix = mix.astype(bf16)
-    mix_ref[...] = mix
-    mix_t_ref[...] = mix.T
-    level_ref[...] = levels
-
-
-def attend_call(q_array, q_at, k_array, k_at, v_array, v_at, own_column, other_row, causal):
+
+    def body(start, window):
+        @pl.when(group == 0)
+        def _():
+            bias_ref[:, :window] = mask_bias(own_ref, other_ref, start, window, causal)
+            level_ref[...] = jnp.zeros_like(level_ref)
+
+        queries = q_ref[...] * bf16(HEAD_DIM ** -0.5)
+        keys = k_ref[pl.ds(start, window), :]
+        values = v_ref[pl.ds(start, window), :]
+        bias = bias_ref[:, :window]
+        mix = jnp.zeros(q_ref.shape, f32)
+        levels = level_ref[...]
+        for head in range(GROUP):
+            chosen = owner == head
+            scores = mm_nt(queries * chosen.astype(bf16), keys) + bias
+            row_max = jnp.max(scores, axis=-1, keepdims=True)
+            exps = jnp.exp(scores - row_max)
+            total = jnp.sum(exps, axis=-1, keepdims=True)
+            probs = (exps * (1.0 / total)).astype(bf16)
+            mix = jnp.where(chosen, mm(probs, values), mix)
+            levels = jnp.where(lane == group * GROUP + head, row_max + jnp.log(total), levels)
+        mix = mix.astype(bf16)
+        mix_ref[...] = mix
+        mix_t_ref[...] = mix.T
+        level_ref[...] = levels
+
+    for_window(table_ref, body)
+
+
+def attend_call(table, q_array, q_at, k_array, k_at, v_array, v_at, own_column, other_row, causal):
     tokens, others = q_array.shape[0], k_array.shape[0]
     width = GROUP * HEAD_DIM
     model = HEADS * HEAD_DIM
     return pl.pallas_call(
-        functools.partial(attend_kernel, causal, WINDOW),
-        grid=(tokens // BLOCK, HEADS // GROUP),
-        in_specs=[
-            pl.BlockSpec((BLOCK, width), lambda b, g: (b, q_at + g)),
-            pl.BlockSpec((others, width), lambda b, g: (0, k_at + g)),
-            pl.BlockSpec((others, width), lambda b, g: (0, v_at + g)),
-            pl.BlockSpec((BLOCK, 1), lambda b, g: (b, 0)),
-            pl.BlockSpec((1, others), lambda b, g: (0, 0)),
-        ],
-        out_specs=[
-            pl.BlockSpec((BLOCK, width), lambda b, g: (b, g)),
-            pl.BlockSpec((width, BLOCK), lambda b, g: (g, b)),
-            pl.BlockSpec((BLOCK, 128), lambda b, g: (b, 0)),
-        ],
+        functools.partial(attend_kernel, causal),
+        grid_spec=pltpu.PrefetchScalarGridSpec(
+            num_scalar_prefetch=1,
+            grid=(tokens // BLOCK, HEADS // GROUP),
+            in_specs=[
+                pl.BlockSpec((BLOCK, width), lambda b, g, t: (b, q_at + g)),
+                pl.BlockSpec((others, width), lambda b, g, t: (0, k_at + g)),
+                pl.BlockSpec((others, width), lambda b, g, t: (0, v_at + g)),
+                pl.BlockSpec((BLOCK, 1), lambda b, g, t: (b, 0)),
+                pl.BlockSpec((1, others), lambda b, g, t: (0, 0)),
+            ],
+            out_specs=[
+                pl.BlockSpec((BLOCK, width), lambda b, g, t: (b, g)),
+                pl.BlockSpec((width, BLOCK), lambda b, g, t: (g, b)),
+                pl.BlockSpec((BLOCK, 128), lambda b, g, t: (b, 0)),
+            ],
+            scratch_shapes=[pltpu.VMEM((BLOCK, WINDOWS[-1]), f32)],
+        ),
         out_shape=[
             jax.ShapeDtypeStruct((tokens, model), bf16),
             jax.ShapeDtypeStruct((model, tokens), bf16),
             jax.ShapeDtypeStruct((tokens, 128), f32),
         ],
-        scratch_shapes=[pltpu.VMEM((BLOCK, WINDOW), f32)],
         compiler_params=params(),
-        cost_estimate=cost(16e9, 12 * MIB, HEADS * tokens * WINDOW),
+        cost_estimate=cost(12e9, 12 * MIB, HEADS * tokens * 384),
         name="attend",
-    )(q_array, k_array, v_array, own_column, other_row)
+    )(table, q_array, k_array, v_array, own_column, other_row)
 
 
 def attend_back_kernel(
-    causal, joined, q_ref, k_ref, v_ref, grad_ref, level_ref, own_ref, other_ref, *rest
+    causal, table_ref, q_ref, k_ref, v_ref, grad_ref, level_ref, own_ref, other_ref, *rest
 ):
-    if joined:
+    if causal:
         out_ref, keys_t, values_t = rest
     else:
         out_ref, pair_ref, keys_t, values_t = rest
     block_index = pl.program_id(0)
     group = pl.program_id(1)
     blocks = pl.num_programs(0)
-    start = window_start(block_index, causal)
-    window = WINDOW
     width = q_ref.shape[1]
     model = HEADS * HEAD_DIM
     rows = pl.ds(pl.multiple_of(group * width, width), width)
+    columns = pl.multiple_of(group * width, width)
+    owner = lax.broadcasted_iota(jnp.int32, (1, width), 1) // HEAD_DIM
+    lane = lax.broadcasted_iota(jnp.int32, (1, 128), 1)
 
     @pl.when(block_index == 0)
     def _():
         keys_t[rows, :] = jnp.zeros((width, keys_t.shape[1]), f32)
         values_t[rows, :] = jnp.zeros((width, keys_t.shape[1]), f32)
 
-    bias = mask_bias(own_ref, other_ref, start, window, causal)
-    owner = lax.broadcasted_iota(jnp.int32, (1, width), 1) // HEAD_DIM
-    lane = lax.broadcasted_iota(jnp.int32, (1, 128), 1)
-    queries = q_ref[...] * bf16(HEAD_DIM ** -0.5)
-    grads = grad_ref[...]
-    queries_t = queries.T
-    grads_t = grads.T
-    keys = k_ref[pl.ds(start, window), :]
-    values = v_ref[pl.ds(start, window), :]
-    levels = level_ref[...]
-    grad_q = jnp.zeros(q_ref.shape, f32)
-    spot = pl.ds(start, window)
-    for head in range(GROUP):
-        chosen = owner == head
-        picked = chosen.astype(bf16)
-        scores = mm_nt(queries * picked, keys) + bias
-        level = jnp.sum(
-            jnp.where(lane == group * GROUP + head, levels, 0.0), axis=-1, keepdims=True
-        )
-        probs = jnp.exp(scores - level)
-        grad_probs = mm_nt(grads * picked, values)
-        inner = jnp.sum(probs * grad_probs, axis=-1, keepdims=True)
-        grad_scores = (probs * (grad_probs - inner)).astype(bf16)
-        band = slice(head * HEAD_DIM, (head + 1) * HEAD_DIM)
-        target_rows = pl.ds(pl.multiple_of(group * width + head * HEAD_DIM, HEAD_DIM), HEAD_DIM)
-        values_t[target_rows, spot] += mm(grads_t[band, :], probs.astype(bf16))
-        keys_t[target_rows, spot] += mm(queries_t[band, :], grad_scores)
-        grad_q = jnp.where(chosen, mm(grad_scores, keys), grad_q)
-    grad_q = (grad_q * HEAD_DIM ** -0.5).astype(bf16)
-    own_rows = pl.ds(pl.multiple_of(block_index * BLOCK, BLOCK), BLOCK)
-    columns = pl.multiple_of(group * width, width)
-    out_ref[own_rows, pl.ds(columns, width)] = grad_q
-    other_ref_out, shift = (out_ref, model) if joined else (pair_ref, 0)
+    def body(start, window):
+        bias = mask_bias(own_ref, other_ref, start, window, causal)
+        queries = q_ref[...] * bf16(HEAD_DIM ** -0.5)
+        grads = grad_ref[...]
+        queries_t = queries.T
+        grads_t = grads.T
+        spot = pl.ds(start, window)
+        keys = k_ref[spot, :]
+        values = v_ref[spot, :]
+        levels = level_ref[...]
+        grad_q = jnp.zeros(q_ref.shape, f32)
+        for head in range(GROUP):
+            chosen = owner == head
+            picked = chosen.astype(bf16)
+            scores = mm_nt(queries * picked, keys) + bias
+            level = jnp.sum(
+                jnp.where(lane == group * GROUP + head, levels, 0.0), axis=-1, keepdims=True
+            )
+            probs = jnp.exp(scores - level)
+            grad_probs = mm_nt(grads * picked, values)
+            inner = jnp.sum(probs * grad_probs, axis=-1, keepdims=True)
+            grad_scores = (probs * (grad_probs - inner)).astype(bf16)
+            band = slice(head * HEAD_DIM, (head + 1) * HEAD_DIM)
+            target_rows = pl.ds(
+                pl.multiple_of(group * width + head * HEAD_DIM, HEAD_DIM), HEAD_DIM
+            )
+            values_t[target_rows, spot] += mm(grads_t[band, :], probs.astype(bf16))
+            keys_t[target_rows, spot] += mm(queries_t[band, :], grad_scores)
+            grad_q = jnp.where(chosen, mm(grad_scores, keys), grad_q)
+        grad_q = (grad_q * HEAD_DIM ** -0.5).astype(bf16)
+        own_rows = pl.ds(pl.multiple_of(block_index * BLOCK, BLOCK), BLOCK)
+        out_ref[own_rows, pl.ds(columns, width)] = grad_q
+
+    for_window(table_ref, body)
+    pair_out, shift = (out_ref, model) if causal else (pair_ref, 0)
 
     @pl.when(block_index == blocks - 1)
     def _():
-        other_ref_out[:, pl.ds(columns + shift, width)] = keys_t[rows, :].astype(bf16).T
-        other_ref_out[:, pl.ds(columns + shift + model, width)] = values_t[rows, :].astype(bf16).T
+        pair_out[:, pl.ds(columns + shift, width)] = keys_t[rows, :].astype(bf16).T
+        pair_out[:, pl.ds(columns + shift + model, width)] = values_t[rows, :].astype(bf16).T
 
 
 def attend_back_call(
-    q_array, q_at, k_array, k_at, v_array, v_at, grad_mix, levels, own_column, other_row, causal
+    table, q_array, q_at, k_array, k_at, v_array, v_at, grad_mix, levels, own_column, other_row, causal
 ):
     tokens, others = q_array.shape[0], k_array.shape[0]
     width = GROUP * HEAD_DIM
@@ -284,24 +317,27 @@
             jax.ShapeDtypeStruct((others, 2 * model), bf16),
         ]
     return pl.pallas_call(
-        functools.partial(attend_back_kernel, causal, causal),
-        grid=(tokens // BLOCK, HEADS // GROUP),
-        in_specs=[
-            pl.BlockSpec((BLOCK, width), lambda b, g: (b, q_at + g)),
-            pl.BlockSpec((others, width), lambda b, g: (0, k_at + g)),
-            pl.BlockSpec((others, width), lambda b, g: (0, v_at + g)),
-            pl.BlockSpec((BLOCK, width), lambda b, g: (b, g)),
-            pl.BlockSpec((BLOCK, 128), lambda b, g: (b, 0)),
-            pl.BlockSpec((BLOCK, 1), lambda b, g: (b, 0)),
-            pl.BlockSpec((1, others), lambda b, g: (0, 0)),
-        ],
-        out_specs=[whole(item.shape) for item in out_shape],
+        functools.partial(attend_back_kernel, causal),
+        grid_spec=pltpu.PrefetchScalarGridSpec(
+            num_scalar_prefetch=1,
+            grid=(tokens // BLOCK, HEADS // GROUP),
+            in_specs=[
+                pl.BlockSpec((BLOCK, width), lambda b, g, t: (b, q_at + g)),
+                pl.BlockSpec((others, width), lambda b, g, t: (0, k_at + g)),
+                pl.BlockSpec((others, width), lambda b, g, t: (0, v_at + g)),
+                pl.BlockSpec((BLOCK, width), lambda b, g, t: (b, g)),
+                pl.BlockSpec((BLOCK, 128), lambda b, g, t: (b, 0)),
+                pl.BlockSpec((BLOCK, 1), lambda b, g, t: (b, 0)),
+                pl.BlockSpec((1, others), lambda b, g, t: (0, 0)),
+            ],
+            out_specs=[whole(item.shape) for item in out_shape],
+            scratch_shapes=[pltpu.VMEM((model, others), f32), pltpu.VMEM((model, others), f32)],
+        ),
         out_shape=out_shape,
-        scratch_shapes=[pltpu.VMEM((model, others), f32), pltpu.VMEM((model, others), f32)],
         compiler_params=params(),
-        cost_estimate=cost(40e9, 16 * MIB, HEADS * tokens * WINDOW),
+        cost_estimate=cost(30e9, 16 * MIB, HEADS * tokens * 384),
         name="attend_back",
-    )(q_array, k_array, v_array, grad_mix, levels, own_column, other_row)
+    )(table, q_array, k_array, v_array, grad_mix, levels, own_column, other_row)
 
 
 def middle_kernel(
@@ -604,51 +640,47 @@
     )(table, *lefts, *rights)
 
 
-def feed_in_kernel(table_ref, left_ref, right_ref, *rest):
+def feed_in_kernel(left_ref, right_ref, *rest):
     out_ref = rest[-1]
-    inner, _, piece, width = out_ref.shape
+    _, inner, piece, width = out_ref.shape
     product = mm(left_ref[...], right_ref[...]).astype(bf16)
-    out_ref[:, 0] = product.reshape(inner, piece, width)
-
-
-def feed_out_kernel(table_ref, left_ref, right_ref, out_ref):
-    inner, _, piece, width = out_ref.shape
+    out_ref[0] = product.reshape(inner, piece, width)
+
+
+def feed_out_kernel(left_ref, right_ref, out_ref):
+    _, inner, piece, width = out_ref.shape
     product = mm(left_ref[...], right_ref[...]).astype(bf16)
     for i in range(inner):
         for b in range(width // piece):
-            out_ref[i, 0, :, b * piece:(b + 1) * piece] = product[
+            out_ref[0, i, :, b * piece:(b + 1) * piece] = product[
                 b * piece:(b + 1) * piece, i * piece:(i + 1) * piece
             ]
 
 
-def feed_rows_kernel(table_ref, left_ref, right_ref, out_ref):
-    inner, _, piece, width = out_ref.shape
+def feed_rows_kernel(left_ref, right_ref, out_ref):
+    _, inner, piece, width = out_ref.shape
     product = mm(left_ref[...].T, right_ref[...]).astype(bf16)
-    out_ref[:, 0] = product.reshape(inner, piece, width)
-
-
-def feed_weight_grad(kernel, table, left, left_spec, right, right_spec, inner, piece, width, at, total, held=None):
-    outer = table.shape[0] - inner
+    out_ref[0] = product.reshape(inner, piece, width)
+
+
+def feed_weight_grad(
+    kernel, left, left_spec, right, right_spec, outer, inner, piece, width, at, total, held=None
+):
     operands, specs = [left, right], [left_spec, right_spec]
     if held is not None:
         operands.append(held)
         specs.append(pl.BlockSpec(memory_space=pl.ANY))
     return pl.pallas_call(
         kernel,
-        grid_spec=pltpu.PrefetchScalarGridSpec(
-            num_scalar_prefetch=1,
-            grid=(outer,),
-            in_specs=specs,
-            out_specs=pl.BlockSpec(
-                (inner, 1, piece, width), lambda o, table: (0, table[inner + o], 0, at)
-            ),
-        ),
-        out_shape=jax.ShapeDtypeStruct((inner, outer, piece, total), bf16),
-        input_output_aliases={} if held is None else {3: 0},
+        grid=(outer,),
+        in_specs=specs,
+        out_specs=pl.BlockSpec((1, inner, piece, width), lambda o: (o, 0, 0, at)),
+        out_shape=jax.ShapeDtypeStruct((outer, inner, piece, total), bf16),
+        input_output_aliases={} if held is None else {2: 0},
         compiler_params=params(),
         cost_estimate=cost(8 * left.shape[1] * 1024 * 1024, 24 * MIB),
         name="feed_weight_grad",
-    )(table, *operands)
+    )(*operands)
 
 
 def entry_back_kernel(
@@ -748,17 +780,50 @@
     return total_of(moved, f32)
 
 
-def outer_half(part, inner, devices):
-    half = part.shape[0] // 2
-    moved = swap(part[half:], inner * half, devices)
-    return (part[:half].astype(f32) + moved.astype(f32)).astype(f32 if half == 1 else part.dtype)
-
-
-def inner_scatter(packed):
-    inner, outer, rows, columns = packed.shape
-    flat = packed.reshape(inner * outer * rows, columns)
-    part = lax.psum_scatter(flat, "inner", scatter_dimension=0, tiled=True)
-    return part.reshape(outer, rows, columns)
+def joint_scatter(packed):
+    outer, inner, rows, columns = packed.shape
+    flat = packed.reshape(outer * inner * rows, columns)
+    return lax.psum_scatter(flat, both, scatter_dimension=0, tiled=True).astype(f32)
+
+
+def core_halves(keep, send, devices):
+    moved = swap(send, 1, devices)
+    cut = keep.shape[-1] // 256 * 128
+    result = []
+    for columns, kept, sent in (
+        (slice(0, cut), slice(0, None, 2), slice(1, None, 2)),
+        (slice(cut, None), slice(0, 2), slice(2, 4)),
+    ):
+        for rows in (kept, sent):
+            result.append(total_of((keep[rows, ..., columns], moved[rows, ..., columns]), keep.dtype))
+    return result
+
+
+def first_halves(parts, devices):
+    keep_x, send_x, keep_y, send_y = parts
+    result = []
+    for keep, send, distance in ((keep_x, send_x, 2), (keep_y, send_y, 4)):
+        moved = swap(send, distance, devices)
+        result += [total_of((keep[k], moved[k]), keep.dtype) for k in range(2)]
+    return result
+
+
+def second_halves(parts, devices):
+    keep_x, send_x, keep_y, send_y = parts
+    moved_x, moved_y = swap(send_x, 4, devices), swap(send_y, 2, devices)
+    return [
+        jnp.concatenate(
+            [total_of((keep_x[o], moved_x[o]), keep_x.dtype),
+             total_of((keep_y[o], moved_y[o]), keep_y.dtype)], axis=-1,
+        )
+        for o in range(keep_x.shape[0])
+    ]
+
+
+def chain_stages(chips):
+    if chips == 4:
+        return core_halves, first_halves, second_halves
+    return core_stage, plane_stage, lambda parts, devices: parts
 
 
 def permuted_column(shard, outer, inner, devices):
@@ -846,6 +911,8 @@
     token_hot = (token_dir[:, None] == jnp.arange(128)[None, :]).astype(bf16)
     token_t = (jnp.arange(langs)[:, None] == token_dir[None, :]).astype(bf16)
     own_column = seg[:, None]
+    self_table = self_windows(seg)
+    cross_table = cross_windows(seg, memory_segments.reshape(-1))
 
     smalls = first_weights[:, :, at_small:at_small + piece].reshape(devices, rows, piece)[:, :n_small]
     smalls = smalls.transpose(1, 0, 2)
@@ -858,14 +925,14 @@
     weights = core_place(plane, core_move)
     hg = HEADS // GROUP
     self_mix, self_mix_t, self_levels = attend_call(
-        triple, 0, triple, hg, triple, 2 * hg, own_column, segment_ids, True
+        self_table, triple, 0, triple, hg, triple, 2 * hg, own_column, segment_ids, True
     )
     pairs, memory_t = pairs_call(memory, weights, w2, 1)
     normed0, rstd0, cross_entry_t, queries = middle_call(
         self_mix, target, token_hot, lang_rows, vec, weights, 0, 1, w1
     )
     cross_mix, cross_mix_t, cross_levels = attend_call(
-        queries, 0, pairs, 0, pairs, hg, own_column, memory_segments, False
+        cross_table, queries, 0, pairs, 0, pairs, hg, own_column, memory_segments, False
     )
     (
         layer_output, ffn_entry_t, act, branch_grad_t, pre_grad, residual1, cross_grad,
@@ -874,34 +941,34 @@
         cross_mix, normed0, cotangent, vec, in_bias, weights, 2 * w1 + w2, g_in, 0, g_out, at_out, w1
     )
 
-    plain = jnp.concatenate([jnp.arange(inner, dtype=jnp.int32), outer_places])
-    hidden_step = pl.BlockSpec((tokens, w4), lambda o, table: (0, o))
+    hidden_step = pl.BlockSpec((tokens, w4), lambda o: (0, o))
     if together:
         ffn_grads = feed_weight_grad(
-            feed_out_kernel, plain, branch_grad_t, whole(branch_grad_t.shape), act, hidden_step,
-            inner, rows, model, 1, 2 * w4,
+            feed_out_kernel, branch_grad_t, whole(branch_grad_t.shape), act, hidden_step,
+            outer, inner, rows, model, 1, 2 * w4,
         )
         ffn_grads = [feed_weight_grad(
-            feed_in_kernel, plain, ffn_entry_t, whole(ffn_entry_t.shape), pre_grad, hidden_step,
-            inner, rows, w4, 0, 2 * w4, ffn_grads,
+            feed_in_kernel, ffn_entry_t, whole(ffn_entry_t.shape), pre_grad, hidden_step,
+            outer, inner, rows, w4, 0, 2 * w4, ffn_grads,
         )]
     else:
         branch_grad = branch_grad_t.T
         ffn_grads = [
             feed_weight_grad(
-                feed_in_kernel, plain, ffn_entry_t, whole(ffn_entry_t.shape), pre_grad, hidden_step,
-                inner, rows, w4, 0, w4,
+                feed_in_kernel, ffn_entry_t, whole(ffn_entry_t.shape), pre_grad, hidden_step,
+                outer, inner, rows, w4, 0, w4,
             ),
             feed_weight_grad(
-                feed_rows_kernel, plain, act, hidden_step, branch_grad, whole(branch_grad.shape),
-                inner, ffn_out.shape[0], model, 0, model,
+                feed_rows_kernel, act, hidden_step, branch_grad, whole(branch_grad.shape),
+                outer, inner, ffn_out.shape[0], model, 0, model,
             ),
         ]
-    ffn_parts = [inner_scatter(item) for item in ffn_grads]
+    ffn_done = [joint_scatter(item) for item in ffn_grads]
+    core, first_plane, second_plane = chain_stages(inner // 2)
 
     cross_mix_grad, _ = hold(cross_mix_grad, ffn_grads)
     queries_grad, pairs_grad = attend_back_call(
-        queries, 0, pairs, 0, pairs, hg, cross_mix_grad, cross_levels, own_column, memory_segments, False
+        cross_table, queries, 0, pairs, 0, pairs, hg, cross_mix_grad, cross_levels, own_column, memory_segments, False
     )
     start_grad, self_grad, self_mix_grad, sums0 = middle_back_call(
         residual1, queries_grad, normed0, rstd0, vec, weights, 1, 0, w1
@@ -911,25 +978,25 @@
     send_a = half_weight_grads(table, lefts_a, rights_a, inner, inner // 2)
     rights_a, send_a = hold(rights_a, send_a)
     keep_a = half_weight_grads(table, lefts_a, rights_a, inner, 0)
-    parts_a = core_stage(keep_a, send_a, devices)
+    parts_a = core(keep_a, send_a, devices)
     self_mix_grad, parts_a = hold(self_mix_grad, parts_a)
     (triple_grad,) = attend_back_call(
-        triple, 0, triple, hg, triple, 2 * hg, self_mix_grad, self_levels, own_column, segment_ids, True
-    )
-    parts_a = plane_stage(parts_a, devices)
+        self_table, triple, 0, triple, hg, triple, 2 * hg, self_mix_grad, self_levels, own_column, segment_ids, True
+    )
+    parts_a = first_plane(parts_a, devices)
     triple_grad, parts_a = hold(triple_grad, parts_a)
     send_c = half_weight_grads(table, [self_entry_t], [triple_grad], inner, inner // 2)
     triple_grad, send_c = hold(triple_grad, send_c)
     keep_c = half_weight_grads(table, [self_entry_t], [triple_grad], inner, 0)
-    parts_c = core_stage(keep_c, send_c, devices)
-    done_a = outer_stage(parts_a, inner, devices)
-    triple_grad, parts_c, ffn_parts, done_a = hold(triple_grad, parts_c, ffn_parts, done_a)
+    parts_c = core(keep_c, send_c, devices)
+    parts_a = second_plane(parts_a, devices)
+    triple_grad, parts_c, parts_a = hold(triple_grad, parts_c, parts_a)
     target_grad, memory_grad, lang_sum = entry_back_call(
         start_grad, triple_grad, pairs_grad, first_weights, w3, weights, w2, 1, token_t
     )
-    parts_c = plane_stage(parts_c, devices)
-    ffn_parts = [outer_half(item, inner, devices) for item in ffn_parts]
-    lang_sum, parts_c, ffn_parts = hold(lang_sum, parts_c, ffn_parts)
+    parts_c = first_plane(parts_c, devices)
+    done_a = outer_stage(parts_a, inner, devices)
+    lang_sum, parts_c, done_a = hold(lang_sum, parts_c, done_a)
 
     stacked = jnp.concatenate(
         [lang_sum, sums0[0:1], sums[3:4], sums[0:1], sums0[1:2], sums[4:5], sums[1:2], sums[2:3]], axis=0
@@ -940,12 +1007,11 @@
     stacked = jnp.take(stacked, order.reshape(-1), axis=0, mode="clip")
     stacked = stacked.reshape(2, inner // 2, outer, n_small, piece)
     parts_e = core_stage(stacked[0], stacked[1], devices)
+    parts_c = second_plane(parts_c, devices)
+    parts_e, parts_c = hold(parts_e, parts_c)
     parts_e = plane_stage(parts_e, devices)
-    while ffn_parts[0].shape[0] > 1:
-        ffn_parts = [outer_half(item, inner, devices) for item in ffn_parts]
-    ffn_done = [item[0] for item in ffn_parts]
     done_c = outer_stage(parts_c, inner, devices)
-    parts_e, ffn_done, done_c = hold(parts_e, ffn_done, done_c)
+    parts_e, done_c = hold(parts_e, done_c)
     extra = outer_stage(parts_e, inner, devices)
     if together:
         ffn_in_grad = ffn_done[0][:, :w4]

time: 655 us -> 634 us (0.968)
  Pallas kernels: 339 us -> 323 us
    pallas_call x6, Pallas kernels: 170 us -> 153 us  [the longest x2 77.2 us: attend_back_call(): pl.pallas_call(functools.partial(attend_back_kernel, causal), grid_spec=p...]
    convert_element_type x2 -> x10, other arithmetic: 10.5 us -> 18.6 us  [total_of(): return total.astype(kind)]
    add x7 -> x5, other arithmetic: 9.01 us -> 2.26 us  [total_of(): total = total + item.astype(f32)]
  transfers between devices with their start and end apart: 33 -> 33, of which waited for: 14 -> 18; matrix products, arithmetic and copies ran while one was open for 9% -> 10% of each run, Pallas kernels for 39% -> 38%
where the time goes in v3:
time: 634 us; the launch traced here: 628 us
  Pallas kernels  323 us (51%)
  waiting for transfers between devices  182 us (29%)
  other arithmetic  41.4 us (7%)
  starting transfers between devices  35.5 us (6%)
  local copies, waits for them, and re-layouts  31.3 us (5%)
  between operations  14.5 us (2%)
    ppermute x30, waiting for transfers between devices, swap(): lax.ppermute(value, both, [(d, d ^ distance) for d in range(devices)])  177 us
    pallas_call x2, Pallas kernels, attend_back_call(): pl.pallas_call(functools.partial(attend_back_kernel, causal), grid_spec=p...  77.2 us
    pallas_call x1, Pallas kernels, feed_call(): pl.pallas_call(functools.partial(feed_kernel, at_cross, at_in, at_out), g...  58.1 us
    pallas_call x4, Pallas kernels, half_weight_grads(): pl.pallas_call(functools.partial(half_kernel, len(lefts), first), grid_sp...  50.6 us
    pallas_call x2, Pallas kernels, attend_call(): pl.pallas_call(functools.partial(attend_kernel, causal), grid_spec=pltpu....  49.5 us
    ppermute x30, starting transfers between devices, swap(): lax.ppermute(value, both, [(d, d ^ distance) for d in range(devices)])  35.4 us
    pallas_call x2, Pallas kernels, feed_weight_grad(): pl.pallas_call(kernel, grid=(outer,), in_specs=specs, out_specs=pl.BlockS...  26.6 us
    pallas_call x1, Pallas kernels, entry_back_call(): pl.pallas_call(entry_back_kernel, grid=(steps,), in_specs=[pl.BlockSpec((...  20.4 us
  transfers between devices with their start and end apart: 33, of which 18 were waited for; matrix products, arithmetic and copies ran while one was open for 10% of the time, Pallas kernels for 38%

profile of v3, /device:TPU:0, one launch (start us, length us, event | category | flops | bytes accessed | tf_op | source)
XLA Modules:
  0.0 628.3 jit_solution(13711975826510503278)
XLA Ops:
  8.0 1.5 concatenate.54
  9.5 1.6 fusion.10
  14.7 3.0 collective-permute-start
  17.7 2.6 collective-permute-start.1
  21.3 13.9 %collective-permute-done = bf16[128,1280]{1,0:T(8,128)(2,1)S(1)} collective-permute-done((bf16[128,1280]{1,0:T(8,128)(2,1)S(1)}, bf16[128,1280]{1,0:T(8,128)(2,1)S(1)}, u32[]{:S(2)}, u32[]{:S(2)}) %collective-permute-start) | collective-permute-done | bytes 327712 | tf_op jit(solution)/shard_map/ppermute | solution.py:754
  35.2 12.8 %collective-permute-done.1 = bf16[128,1280]{1,0:T(8,128)(2,1)S(1)} collective-permute-done((bf16[128,1280]{1,0:T(8,128)(2,1)S(1)}, bf16[128,1280]{1,0:T(8,128)(2,1)S(1)}, u32[]{:S(2)}, u32[]{:S(2)}) %collective-permute-start.1) | collective-permute-done | bytes 327712 | tf_op jit(solution)/shard_map/ppermute | solution.py:754
  48.1 1.7 collective-permute-start.3
  49.9 1.5 collective-permute-start.4
  51.7 39.1 %collective-permute-done.3 = bf16[4,128,1280]{2,1,0:T(8,128)(2,1)S(1)} collective-permute-done((bf16[4,128,1280]{2,1,0:T(8,128)(2,1)S(1)}, bf16[4,128,1280]{2,1,0:T(8,128)(2,1)S(1)}, u32[]{:S(2)}, u32[]{:S(2)}) %collective-permute-start.3) | collective-permute-done | bytes 1310752 | tf_op jit(solution)/shard_map/ppermute | solution.py:754
  90.7 33.8 %collective-permute-done.5 = bf16[4,128,1280]{2,1,0:T(8,128)(2,1)} collective-permute-done((bf16[4,128,1280]{2,1,0:T(8,128)(2,1)S(1)}, bf16[4,128,1280]{2,1,0:T(8,128)(2,1)}, u32[]{:S(2)}, u32[]{:S(2)}) %collective-permute-start.5) | collective-permute-done | bytes 1310752 | tf_op jit(solution)/shard_map/ppermute | solution.py:754
  124.6 2.9 broadcast_in_dim.99
  127.5 1.2 bitcast_dynamic-update-slice_fusion.3
  128.6 1.1 bitcast_dynamic-update-slice_fusion.2
  129.8 2.6 bitcast_dynamic-update-slice_fusion.1
  132.4 2.5 bitcast_dynamic-update-slice_fusion
  138.8 1.3 slice.355
  142.0 12.3 %triple.1 = (bf16[1024,3072]{1,0:T(8,128)(2,1)}, bf16[1024,1024]{1,0:T(8,128)(2,1)}) custom-call(bf16[1024,1024]{1,0:T(8,128)(2,1)} %target_ref.3, bf16[1024,128]{1,0:T(8,128)(2,1)} %fusion.4.token_ref, bf16[128,1024]{1,0:T(8,128)(2,1)} %pad.15.lang_ref, bf16[4,1024,896]{2,1,0:T(8,128)(2,1)} %bitcast.132), custom_call_target="tpu_custom_call" | custom-call | flops 100663296 | bytes 262144 | tf_op jit(solution)/shard_map/triple/pallas_call | solution.py:89
  154.9 10.1 %bitcast_select_fusion.out_weight_ref.query_weight_ref.weight_ref.cross_hbm.pairs_weight_ref = bf16[4,1024,1280]{2,1,0:T(8,128)(2,1)} fusion(pred[1024]{0:T(1024)(128)(4,1)S(1)} %broadcast_in_dim.105, bf16[4,4,128,1280]{3,2,1,0:T(8,128)(2,1)} %collective-permute-done.6, bf16[4,4,128,1280]{3,2,1,0:T(8,128)(2,1)} %bitcast_dynamic-update-slice_fusion), kind=kLoop, calls=%fused_computation.1 | loop fusion | flops 5242880 | bytes 20972544 | tf_op jit(solution)/shard_map/jit(_where)/select_n | solution.py:854
  165.0 6.4 %pairs.1 = (bf16[512,2048]{1,0:T(8,128)(2,1)}, bf16[1024,512]{1,0:T(8,128)(2,1)}) custom-call(bf16[512,1024]{1,0:T(8,128)(2,1)} %memory_ref.1, bf16[4,1024,1280]{2,1,0:T(8,128)(2,1)} %bitcast_select_fusion.out_weight_ref.query_weight_ref.weight_ref.cross_hbm.pairs_weight_ref), custom_call_target="tpu_custom_call" | custom-call | flops 33554432 | bytes 131072 | tf_op jit(solution)/shard_map/pairs/pallas_call | solution.py:119
  171.4 25.0 %attend.2 = (bf16[1024,1024]{1,0:T(8,128)(2,1)}, bf16[1024,1024]{1,0:T(8,128)(2,1)}, f32[1024,128]{1,0:T(8,128)}) custom-call(s32[8]{0:T(128)} %pad_add_fusion.1.table_ref, bf16[1024,3072]{1,0:T(8,128)(2,1)} %get-tuple-element.108.q_ref.k_ref.v_ref, bf16[1024,3072]{1,0:T(8,128)(2,1)} %get-tuple-element.108.q_ref.k_ref.v_ref, ...), custom_call_target="tpu_custom_call" | custom-call | flops 187500000 | bytes 196608 | tf_op jit(solution)/shard_map/attend/pallas_call | solution.py:212
  196.4 10.8 %middle.1 = (f32[1024,1024]{1,0:T(8,128)}, f32[1024,1]{1,0:T(8,128)}, bf16[1024,1024]{1,0:T(8,128)(2,1)}, bf16[1024,1024]{1,0:T(8,128)(2,1)}) custom-call(bf16[1024,1024]{1,0:T(8,128)(2,1)} %get-tuple-element.109.mix_ref, bf16[1024,1024]{1,0:T(8,128)(2,1)} %target_ref.3, bf16[1024,128]{1,0:T(8,128)(2,1)} %fusion.4.token_ref, ...), custom_call_target="tpu_custom_call" | custom-call | flops 67108864 | bytes 262144 | tf_op jit(solution)/shard_map/middle/pallas_call | solution.py:363
  207.2 24.5 %attend.3 = (bf16[1024,1024]{1,0:T(8,128)(2,1)}, bf16[1024,1024]{1,0:T(8,128)(2,1)}, f32[1024,128]{1,0:T(8,128)}) custom-call(s32[8]{0:T(128)} %pad_add_fusion.table_ref, bf16[1024,1024]{1,0:T(8,128)(2,1)} %get-tuple-element.111.q_ref, bf16[512,2048]{1,0:T(8,128)(2,1)} %get-tuple-element.112.k_ref.v_ref, bf16[512,2048]{1,0:T(8,128)(2,1)} %get-tuple-element.112.k_ref.v_ref, ...), custom_call_target="tpu_custom_call" | custom-call | flops 187500000 | bytes 196608 | tf_op jit(solution)/shard_map/attend/pallas_call | solution.py:212
  231.7 5.7 all-gather.5.cloned.1.call-done
  237.4 58.1 %feed.1 = (bf16[1024,1024]{1,0:T(8,128)(2,1)}, bf16[1024,1024]{1,0:T(8,128)(2,1)}, bf16[1024,4096]{1,0:T(8,128)(2,1)}, bf16[1024,1024]{1,0:T(8,128)(2,1)}, bf16[...) custom-call(bf16[1024,1024]{1,0:T(8,128)(2,1)} %get-tuple-element.11, ...), custom_call_target="tpu_custom_call" | custom-call | flops 603979776 | bytes 983040 | tf_op jit(solution)/shard_map/feed/pallas_call | solution.py:495
  295.5 13.6 %feed_weight_grad.2.rest_0_ = bf16[4,8,128,2048]{3,2,1,0:T(8,128)(2,1)} custom-call(bf16[1024,1024]{1,0:T(8,128)(2,1)} %get-tuple-element.121.left_ref, bf16[1024,4096]{1,0:T(8,128)(2,1)} %get-tuple-element.122.right_ref), custom_call_target="tpu_custom_call" | custom-call | flops 134217728 | bytes 393216 | tf_op jit(solution)/shard_map/feed_weight_grad/pallas_call | solution.py:673
  309.2 12.9 %feed_weight_grad.3 = bf16[4,8,128,2048]{3,2,1,0:T(8,128)(2,1)} custom-call(bf16[1024,1024]{1,0:T(8,128)(2,1)} %get-tuple-element.119.left_ref, bf16[1024,4096]{1,0:T(8,128)(2,1)} %get-tuple-element.120.right_ref, bf16[4,8,128,2048]{3,2,1,0:T(8,128)(2,1)} %feed_weight_grad.2.rest_0_), custom_call_target="tpu_custom_call", output_to_operand_aliasing={{}: (2, {})} | custom-call | flops 134217728 | bytes 393216 | tf_op jit(solution)/shard_map/feed_weight_grad/pallas_call | solution.py:673
  323.3 37.7 %attend_back.2 = (bf16[1024,1024]{1,0:T(8,128)(2,1)}, bf16[512,2048]{1,0:T(8,128)(2,1)}) custom-call(s32[8]{0:T(128)} %pad_add_fusion.table_ref, bf16[1024,1024]{1,0:T(8,128)(2,1)} %get-tuple-element.111.q_ref, bf16[512,2048]{1,0:T(8,128)(2,1)} %get-tuple-element.112.k_ref.v_ref, bf16[512,2048]{1,0:T(8,128)(2,1)} %get-tuple-element.112.k_ref.v_ref, ...), custom_call_target="tpu_custom_call" | custom-call | flops 468750016 | bytes 262144 | tf_op jit(solution)/shard_map/attend_back/pallas_call | solution.py:319
  361.1 11.5 %middle_back.1 = (f32[1024,1024]{1,0:T(8,128)}, bf16[1024,1024]{1,0:T(8,128)(2,1)}, bf16[1024,1024]{1,0:T(8,128)(2,1)}, f32[8,1024]{1,0:T(8,128)}) custom-call(f32[1024,1024]{1,0:T(8,128)} %get-tuple-element.117.residual_ref, bf16[1024,1024]{1,0:T(8,128)(2,1)} %get-tuple-element.137.queries_grad_ref.refs_5_, f32[1024,1024]{1,0:T(8,128)} %get-tuple-element.114.normed_ref, ...), custom_call_target="tpu_custom_call" | custom-call | flops 67108864 | bytes 360448 | tf_op jit(solution)/shard_map/middle_back/pallas_call | solution.py:561
  372.6 15.9 %half_weight_grads.4 = bf16[4,4,128,1280]{3,2,1,0:T(8,128)(2,1)} custom-call(s32[12]{0:T(128)} %pad_add_fusion.2.table_ref, bf16[1024,512]{1,0:T(8,128)(2,1)} %get-tuple-element.129.refs_0_, bf16[1024,1024]{1,0:T(8,128)(2,1)} %get-tuple-element.130.refs_1_, bf16[1024,1024]{1,0:T(8,128)(2,1)} %get-tuple-element.131.refs_2_, ...), custom_call_target="tpu_custom_call" | custom-call | flops 67108864 | bytes 196608 | tf_op jit(solution)/shard_map/half_weight_grads/pallas_call | solution.py:621
  388.5 16.3 %half_weight_grads.5 = bf16[4,4,128,1280]{3,2,1,0:T(8,128)(2,1)} custom-call(s32[12]{0:T(128)} %pad_add_fusion.2.table_ref, bf16[1024,512]{1,0:T(8,128)(2,1)} %get-tuple-element.129.refs_0_, bf16[1024,1024]{1,0:T(8,128)(2,1)} %get-tuple-element.130.refs_1_, bf16[1024,1024]{1,0:T(8,128)(2,1)} %get-tuple-element.131.refs_2_, ...), custom_call_target="tpu_custom_call" | custom-call | flops 67108864 | bytes 196608 | tf_op jit(solution)/shard_map/half_weight_grads/pallas_call | solution.py:621
  404.8 5.8 add_convert_fusion
  410.6 1.4 collective-permute-start.9
  412.1 39.5 %attend_back.3.refs_1_.triple_ref = bf16[1024,3072]{1,0:T(8,128)(2,1)} custom-call(s32[8]{0:T(128)} %pad_add_fusion.1.table_ref, bf16[1024,3072]{1,0:T(8,128)(2,1)} %get-tuple-element.108.q_ref.k_ref.v_ref, bf16[1024,3072]{1,0:T(8,128)(2,1)} %get-tuple-element.108.q_ref.k_ref.v_ref, bf16[1024,3072]{1,0:T(8,128)(2,1)} %get-tuple-element.108.q_ref.k_ref.v_ref, ...), custom_call_target="tpu_custom_call" | custom-call | flops 468750016 | bytes 262144 | tf_op jit(solution)/shard_map/attend_back/pallas_call | solution.py:319
  451.6 1.1 collective-permute-done.9
  452.6 1.6 fusion.3
  454.3 17.7 %collective-permute-done.8 = bf16[2,4,128,640]{3,2,1,0:T(8,128)(2,1)} collective-permute-done((bf16[2,4,128,640]{3,2,1,0:T(8,128)(2,1)}, bf16[2,4,128,640]{3,2,1,0:T(8,128)(2,1)}, u32[]{:S(2)}, u32[]{:S(2)}) %collective-permute-start.8) | collective-permute-done | bytes 1310752 | tf_op jit(solution)/shard_map/ppermute | solution.py:754
  472.0 2.5 fusion.1
  474.5 9.2 %half_weight_grads.6 = bf16[4,4,128,768]{3,2,1,0:T(8,128)(2,1)} custom-call(s32[12]{0:T(128)} %pad_add_fusion.2.table_ref, bf16[1024,1024]{1,0:T(8,128)(2,1)} %get-tuple-element.148.refs_0_, bf16[1024,3072]{1,0:T(8,128)(2,1)} %attend_back.3.refs_1_.triple_ref), custom_call_target="tpu_custom_call" | custom-call | flops 50331648 | bytes 196608 | tf_op jit(solution)/shard_map/half_weight_grads/pallas_call | solution.py:621
  486.6 9.3 %half_weight_grads.7 = bf16[4,4,128,768]{3,2,1,0:T(8,128)(2,1)} custom-call(s32[12]{0:T(128)} %pad_add_fusion.2.table_ref, bf16[1024,1024]{1,0:T(8,128)(2,1)} %get-tuple-element.148.refs_0_, bf16[1024,3072]{1,0:T(8,128)(2,1)} %attend_back.3.refs_1_.triple_ref), custom_call_target="tpu_custom_call" | custom-call | flops 50331648 | bytes 196608 | tf_op jit(solution)/shard_map/half_weight_grads/pallas_call | solution.py:621
  495.9 13.3 %collective-permute-done.11 = bf16[4,128,640]{2,1,0:T(8,128)(2,1)S(1)} collective-permute-done((bf16[4,128,640]{2,1,0:T(8,128)(2,1)}, bf16[4,128,640]{2,1,0:T(8,128)(2,1)S(1)}, u32[]{:S(2)}, u32[]{:S(2)}) %collective-permute-start.11) | collective-permute-done | bytes 655392 | tf_op jit(solution)/shard_map/ppermute | solution.py:754
  509.4 6.7 %collective-permute-done.12 = bf16[4,128,640]{2,1,0:T(8,128)(2,1)S(1)} collective-permute-done((bf16[4,128,640]{2,1,0:T(8,128)(2,1)S(1)}, bf16[4,128,640]{2,1,0:T(8,128)(2,1)S(1)}, u32[]{:S(2)}, u32[]{:S(2)}) %collective-permute-start.12) | collective-permute-done | bytes 655392 | tf_op jit(solution)/shard_map/ppermute | solution.py:754
  517.1 3.7 add_convert_fusion.4
  520.8 3.2 collective-permute-start.15
  524.0 2.4 collective-permute-start.16
  526.5 3.1 collective-permute-start.14
  532.5 20.4 %entry_back.1 = (f32[1024,1024]{1,0:T(8,128)}, f32[512,1024]{1,0:T(8,128)}, f32[16,1024]{1,0:T(8,128)}) custom-call(f32[1024,1024]{1,0:T(8,128)} %get-tuple-element.127.start_ref, bf16[1024,3072]{1,0:T(8,128)(2,1)} %attend_back.3.refs_1_.triple_ref, bf16[512,2048]{1,0:T(8,128)(2,1)} %get-tuple-element.136.refs_4_.pairs_ref, bf16[4,1024,896]{2,1,0:T(8,128)(2,1)} %bitcast.133, ...), custom_call_target="tpu_custom_call" | custom-call | flops 134217728 | bytes 655360 | tf_op jit(solution)/shard_map/entry_back/pallas_call | solution.py:721
  552.9 5.6 collective-permute-done.17
  558.4 1.3 convert_add_fusion
  559.8 2.1 fusion.9
  561.9 6.7 %collective-permute-done.13 = bf16[2,4,128,384]{3,2,1,0:T(8,128)(2,1)} collective-permute-done((bf16[2,4,128,384]{3,2,1,0:T(8,128)(2,1)S(1)}, bf16[2,4,128,384]{3,2,1,0:T(8,128)(2,1)}, u32[]{:S(2)}, u32[]{:S(2)}) %collective-permute-start.13) | collective-permute-done | bytes 786464 | tf_op jit(solution)/shard_map/ppermute | solution.py:754
  568.6 1.3 fusion.7
  573.6 5.7 collective-permute-done.19
  579.3 1.1 fusion.25
  580.5 3.1 collective-permute-done.20
  584.5 1.7 collective-permute-start.22
  586.2 1.2 collective-permute-start.23
  587.4 2.0 collective-permute-start.24
  589.4 2.3 collective-permute-start.25
  591.9 4.2 collective-permute-done.24
  596.1 10.0 %collective-permute-done.25 = bf16[128,768]{1,0:T(8,128)(2,1)S(1)} collective-permute-done((bf16[128,768]{1,0:T(8,128)(2,1)S(1)}, bf16[128,768]{1,0:T(8,128)(2,1)S(1)}, u32[]{:S(2)}, u32[]{:S(2)}) %collective-permute-start.25) | collective-permute-done | bytes 196640 | tf_op jit(solution)/shard_map/ppermute | solution.py:754
  606.9 3.0 collective-permute-start.27
  610.4 1.9 collective-permute-start.29
  614.6 1.4 collective-permute-done.29
  618.3 1.1 convert_element_type.604
  (145 shorter events, 33.2 us)
Async XLA Ops:
  7.2 13.3 %copy-start.4 = (bf16[128,1024]{1,0:T(8,128)(2,1)S(1)}, bf16[128,1024]{1,0:T(8,128)(2,1)}, u32[]{:S(2)}) copy-start(bf16[128,1024]{1,0:T(8,128)(2,1)} %param.31) | copy-start | bytes 786436
  7.2 13.3 %copy-start.3 = (bf16[128,1024]{1,0:T(8,128)(2,1)S(1)}, bf16[128,1024]{1,0:T(8,128)(2,1)}, u32[]{:S(2)}) copy-start(bf16[128,1024]{1,0:T(8,128)(2,1)} %param.33) | copy-start | bytes 786436
  7.2 117.4 %all-gather.3.cloned.1.call-start = ((), (), s32[]{:S(2)}) async-start(), calls=%async_computation.1 | async-start | bytes 7569408 | tf_op jit(solution)/shard_map/all_gather | solution.py:749
  11.2 226.2 %all-gather.5.cloned.1.call-start = ((), (), s32[]{:S(2)}) async-start(), calls=%async_computation.2 | async-start | bytes 17301504 | tf_op jit(solution)/shard_map/all_gather | solution.py:749
  14.7 20.5 %collective-permute-start = (bf16[128,1280]{1,0:T(8,128)(2,1)S(1)}, bf16[128,1280]{1,0:T(8,128)(2,1)S(1)}, u32[]{:S(2)}, u32[]{:S(2)}) collective-permute-start(bf16[128,1280]{1,0:T(8,128)(2,1)S(1)} %constant_dynamic-update-slice_fusion), channel_id=1, source_target_pairs={{0,8},{1,9},{2,10},{3,11},{4,12},{5,13},{6,14},{7,15},{8,0},{9,1},... | collective-permute-start | bytes 983048 | tf_op jit(solution)/shard_map/ppermute | solution.py:754
  17.7 30.3 %collective-permute-start.1 = (bf16[128,1280]{1,0:T(8,128)(2,1)S(1)}, bf16[128,1280]{1,0:T(8,128)(2,1)S(1)}, u32[]{:S(2)}, u32[]{:S(2)}) collective-permute-start(bf16[128,1280]{1,0:T(8,128)(2,1)S(1)} %constant_dynamic-update-slice_fusion), channel_id=1, source_target_pairs={{0,16},{1,17},{2,18},{3,19},{4,20},{5,21},{6,22},{7,23},{8,24},{9,... | collective-permute-start | bytes 983048 | tf_op jit(solution)/shard_map/ppermute | solution.py:754
  20.3 27.7 %collective-permute-start.2 = (bf16[128,1280]{1,0:T(8,128)(2,1)S(1)}, bf16[128,1280]{1,0:T(8,128)(2,1)S(1)}, u32[]{:S(2)}, u32[]{:S(2)}) collective-permute-start(bf16[128,1280]{1,0:T(8,128)(2,1)S(1)} %constant_dynamic-update-slice_fusion), channel_id=1, source_target_pairs={{0,24},{1,25},{2,26},{3,27},{4,28},{5,29},{6,30},{7,31},{8,16},{9,... | collective-permute-start | bytes 983048 | tf_op jit(solution)/shard_map/ppermute | solution.py:754
  48.1 570.2 %reduce-scatter.2.cloned.1.call-start = ((), (), s32[]{:S(2)}) async-start(), calls=%async_computation.3 | async-start | bytes 17301504 | tf_op jit(solution)/shard_map/reduce_scatter | solution.py:786
  48.1 42.6 %collective-permute-start.3 = (bf16[4,128,1280]{2,1,0:T(8,128)(2,1)S(1)}, bf16[4,128,1280]{2,1,0:T(8,128)(2,1)S(1)}, u32[]{:S(2)}, u32[]{:S(2)}) collective-permute-start(bf16[4,128,1280]{2,1,0:T(8,128)(2,1)S(1)} %bitcast_dynamic-update-slice_fusion.4), channel_id=1, source_target_pairs={{0,2},{1,3},{2,0},{3,1},{4,6},{5,7},{6,4},{7,5},{8,10},{9,11},{10,... | collective-permute-start | bytes 3932168 | tf_op jit(solution)/shard_map/ppermute | solution.py:754
  49.9 40.9 %collective-permute-start.4 = (bf16[4,128,1280]{2,1,0:T(8,128)(2,1)S(1)}, bf16[4,128,1280]{2,1,0:T(8,128)(2,1)}, u32[]{:S(2)}, u32[]{:S(2)}) collective-permute-start(bf16[4,128,1280]{2,1,0:T(8,128)(2,1)S(1)} %bitcast_dynamic-update-slice_fusion.4), channel_id=1, source_target_pairs={{0,4},{1,5},{2,6},{3,7},{4,0},{5,1},{6,2},{7,3},{8,12},{9,13},{10,... | collective-permute-start | bytes 3932168 | tf_op jit(solution)/shard_map/ppermute | solution.py:754
  51.4 73.2 %collective-permute-start.5 = (bf16[4,128,1280]{2,1,0:T(8,128)(2,1)S(1)}, bf16[4,128,1280]{2,1,0:T(8,128)(2,1)}, u32[]{:S(2)}, u32[]{:S(2)}) collective-permute-start(bf16[4,128,1280]{2,1,0:T(8,128)(2,1)S(1)} %bitcast_dynamic-update-slice_fusion.4), channel_id=1, source_target_pairs={{0,6},{1,7},{2,4},{3,5},{4,2},{5,3},{6,0},{7,1},{8,14},{9,15},{10,... | collective-permute-start | bytes 3932168 | tf_op jit(solution)/shard_map/ppermute | solution.py:754
  129.8 5.1 copy-start.5
  132.4 4.0 copy-start.7
  132.4 5.5 copy-start.10
  134.9 20.0 %collective-permute-start.6 = (bf16[4,4,128,1280]{3,2,1,0:T(8,128)(2,1)}, bf16[4,4,128,1280]{3,2,1,0:T(8,128)(2,1)}, u32[]{:S(2)}, u32[]{:S(2)}) collective-permute-start(bf16[4,4,128,1280]{3,2,1,0:T(8,128)(2,1)} %bitcast_dynamic-update-slice_fusion), channel_id=1, source_target_pairs={{0,1},{1,0},{2,3},{3,2},{4,5},{5,4},{6,7},{7,6},{8,9},{9,8},{10,11... | collective-permute-start | bytes 15728648 | tf_op jit(solution)/shard_map/ppermute | solution.py:754
  322.1 0.7 copy-start.11
  388.5 16.4 %collective-permute-start.7 = (bf16[4,4,128,1280]{3,2,1,0:T(8,128)(2,1)}, bf16[4,4,128,1280]{3,2,1,0:T(8,128)(2,1)}, u32[]{:S(2)}, u32[]{:S(2)}) collective-permute-start(bf16[4,4,128,1280]{3,2,1,0:T(8,128)(2,1)} %half_weight_grads.4), channel_id=1, source_target_pairs={{0,1},{1,0},{2,3},{3,2},{4,5},{5,4},{6,7},{7,6},{8,9},{9,8},{10,11... | collective-permute-start | bytes 15728648 | tf_op jit(solution)/shard_map/ppermute | solution.py:754
  410.6 42.0 %collective-permute-start.9 = (bf16[2,4,128,640]{3,2,1,0:T(8,128)(2,1)S(1)}, bf16[2,4,128,640]{3,2,1,0:T(8,128)(2,1)}, u32[]{:S(2)}, u32[]{:S(2)}) collective-permute-start(bf16[2,4,128,640]{3,2,1,0:T(8,128)(2,1)S(1)} %get-tuple-element.146), channel_id=1, source_target_pairs={{0,4},{1,5},{2,6},{3,7},{4,0},{5,1},{6,2},{7,3},{8,12},{9,13},{10,... | collective-permute-start | bytes 3932168 | tf_op jit(solution)/shard_map/ppermute | solution.py:754
  412.1 59.9 %collective-permute-start.8 = (bf16[2,4,128,640]{3,2,1,0:T(8,128)(2,1)}, bf16[2,4,128,640]{3,2,1,0:T(8,128)(2,1)}, u32[]{:S(2)}, u32[]{:S(2)}) collective-permute-start(bf16[2,4,128,640]{3,2,1,0:T(8,128)(2,1)} %get-tuple-element.144), channel_id=1, source_target_pairs={{0,2},{1,3},{2,0},{3,1},{4,6},{5,7},{6,4},{7,5},{8,10},{9,11},{10,... | collective-permute-start | bytes 3932168 | tf_op jit(solution)/shard_map/ppermute | solution.py:754
  483.6 33.4 %collective-permute-start.10 = (bf16[4,4,128,768]{3,2,1,0:T(8,128)(2,1)}, bf16[4,4,128,768]{3,2,1,0:T(8,128)(2,1)}, u32[]{:S(2)}, u32[]{:S(2)}) collective-permute-start(bf16[4,4,128,768]{3,2,1,0:T(8,128)(2,1)} %half_weight_grads.6), channel_id=1, source_target_pairs={{0,1},{1,0},{2,3},{3,2},{4,5},{5,4},{6,7},{7,6},{8,9},{9,8},{10,11... | collective-permute-start | bytes 9437192 | tf_op jit(solution)/shard_map/ppermute | solution.py:754
  483.7 25.5 %collective-permute-start.11 = (bf16[4,128,640]{2,1,0:T(8,128)(2,1)}, bf16[4,128,640]{2,1,0:T(8,128)(2,1)S(1)}, u32[]{:S(2)}, u32[]{:S(2)}) collective-permute-start(bf16[4,128,640]{2,1,0:T(8,128)(2,1)} %get-tuple-element.152), channel_id=1, source_target_pairs={{0,4},{1,5},{2,6},{3,7},{4,0},{5,1},{6,2},{7,3},{8,12},{9,13},{10,... | collective-permute-start | bytes 1966088 | tf_op jit(solution)/shard_map/ppermute | solution.py:754
  484.3 31.7 %collective-permute-start.12 = (bf16[4,128,640]{2,1,0:T(8,128)(2,1)S(1)}, bf16[4,128,640]{2,1,0:T(8,128)(2,1)S(1)}, u32[]{:S(2)}, u32[]{:S(2)}) collective-permute-start(bf16[4,128,640]{2,1,0:T(8,128)(2,1)S(1)} %get-tuple-element.154), channel_id=1, source_target_pairs={{0,2},{1,3},{2,0},{3,1},{4,6},{5,7},{6,4},{7,5},{8,10},{9,11},{10,... | collective-permute-start | bytes 1966088 | tf_op jit(solution)/shard_map/ppermute | solution.py:754
  509.3 7.7 %copy-start = (bf16[4,4,128,768]{3,2,1,0:T(8,128)(2,1)S(1)}, bf16[4,4,128,768]{3,2,1,0:T(8,128)(2,1)}, u32[]{:S(2)}) copy-start(bf16[4,4,128,768]{3,2,1,0:T(8,128)(2,1)} %half_weight_grads.7) | copy-start | bytes 9437188
  517.0 13.4 %copy-start.9 = (f32[8,1024]{1,0:T(8,128)S(1)}, f32[8,1024]{1,0:T(8,128)}, u32[]{:S(2)}) copy-start(f32[8,1024]{1,0:T(8,128)} %get-tuple-element.169) | copy-start | bytes 98308
  517.1 13.9 %copy-start.8 = (f32[1,4096]{1,0:T(1,128)S(1)}, f32[1,4096]{1,0:T(1,128)}, u32[]{:S(2)}) copy-start(f32[1,4096]{1,0:T(1,128)} %get-tuple-element.170) | copy-start | bytes 49156
  520.8 32.0 %collective-permute-start.15 = (bf16[128,1280]{1,0:T(8,128)(2,1)}, bf16[128,1280]{1,0:T(8,128)(2,1)}, u32[]{:S(2)}, u32[]{:S(2)}) collective-permute-start(bf16[128,1280]{1,0:T(8,128)(2,1)} %pad_maximum_fusion.3), channel_id=1, source_target_pairs={{0,8},{1,9},{2,10},{3,11},{4,12},{5,13},{6,14},{7,15},{8,0},{9,1},... | collective-permute-start | bytes 983048 | tf_op jit(solution)/shard_map/ppermute | solution.py:754
  524.0 28.8 %collective-permute-start.16 = (bf16[128,1280]{1,0:T(8,128)(2,1)S(1)}, bf16[128,1280]{1,0:T(8,128)(2,1)}, u32[]{:S(2)}, u32[]{:S(2)}) collective-permute-start(bf16[128,1280]{1,0:T(8,128)(2,1)S(1)} %pad_maximum_fusion.4), channel_id=1, source_target_pairs={{0,16},{1,17},{2,18},{3,19},{4,20},{5,21},{6,22},{7,23},{8,24},{9,... | collective-permute-start | bytes 983048 | tf_op jit(solution)/shard_map/ppermute | solution.py:754
  526.5 32.0 %collective-permute-start.17 = (bf16[128,1280]{1,0:T(8,128)(2,1)S(1)}, bf16[128,1280]{1,0:T(8,128)(2,1)}, u32[]{:S(2)}, u32[]{:S(2)}) collective-permute-start(bf16[128,1280]{1,0:T(8,128)(2,1)S(1)} %pad_maximum_fusion.5), channel_id=1, source_target_pairs={{0,24},{1,25},{2,26},{3,27},{4,28},{5,29},{6,30},{7,31},{8,16},{9,... | collective-permute-start | bytes 983048 | tf_op jit(solution)/shard_map/ppermute | solution.py:754
  526.5 33.3 %collective-permute-start.14 = (bf16[2,4,128,384]{3,2,1,0:T(8,128)(2,1)}, bf16[2,4,128,384]{3,2,1,0:T(8,128)(2,1)}, u32[]{:S(2)}, u32[]{:S(2)}) collective-permute-start(bf16[2,4,128,384]{3,2,1,0:T(8,128)(2,1)} %get-tuple-element.162), channel_id=1, source_target_pairs={{0,4},{1,5},{2,6},{3,7},{4,0},{5,1},{6,2},{7,3},{8,12},{9,13},{10,... | collective-permute-start | bytes 2359304 | tf_op jit(solution)/shard_map/ppermute | solution.py:754
  532.4 36.2 %collective-permute-start.13 = (bf16[2,4,128,384]{3,2,1,0:T(8,128)(2,1)S(1)}, bf16[2,4,128,384]{3,2,1,0:T(8,128)(2,1)}, u32[]{:S(2)}, u32[]{:S(2)}) collective-permute-start(bf16[2,4,128,384]{3,2,1,0:T(8,128)(2,1)S(1)} %get-tuple-element.160), channel_id=1, source_target_pairs={{0,2},{1,3},{2,0},{3,1},{4,6},{5,7},{6,4},{7,5},{8,10},{9,11},{10,... | collective-permute-start | bytes 2359304 | tf_op jit(solution)/shard_map/ppermute | solution.py:754
  559.8 10.2 %copy-start.6 = (f32[16,1024]{1,0:T(8,128)S(1)}, f32[16,1024]{1,0:T(8,128)}, u32[]{:S(2)}) copy-start(f32[16,1024]{1,0:T(8,128)} %get-tuple-element.167) | copy-start | bytes 196612
  569.9 2.2 copy-start.2
  569.9 9.4 %collective-permute-start.19 = (bf16[4,128,384]{2,1,0:T(8,128)(2,1)S(1)}, bf16[4,128,384]{2,1,0:T(8,128)(2,1)}, u32[]{:S(2)}, u32[]{:S(2)}) collective-permute-start(bf16[4,128,384]{2,1,0:T(8,128)(2,1)S(1)} %get-tuple-element.172), channel_id=1, source_target_pairs={{0,4},{1,5},{2,6},{3,7},{4,0},{5,1},{6,2},{7,3},{8,12},{9,13},{10,... | collective-permute-start | bytes 1179656 | tf_op jit(solution)/shard_map/ppermute | solution.py:754
  572.0 1.6 collective-permute-start.18
  572.1 11.5 %collective-permute-start.20 = (bf16[4,128,384]{2,1,0:T(8,128)(2,1)S(1)}, bf16[4,128,384]{2,1,0:T(8,128)(2,1)S(1)}, u32[]{:S(2)}, u32[]{:S(2)}) collective-permute-start(bf16[4,128,384]{2,1,0:T(8,128)(2,1)S(1)} %copy-done.2), channel_id=1, source_target_pairs={{0,2},{1,3},{2,0},{3,1},{4,6},{5,7},{6,4},{7,5},{8,10},{9,11},{10,... | collective-permute-start | bytes 1179656 | tf_op jit(solution)/shard_map/ppermute | solution.py:754
  583.8 7.8 %collective-permute-start.21 = (f32[4,27,32]{2,1,0:T(8,128)S(1)}, f32[4,27,32]{2,1,0:T(8,128)S(1)}, u32[]{:S(2)}, u32[]{:S(2)}) collective-permute-start(f32[4,27,32]{2,1,0:T(8,128)S(1)} %get-tuple-element.176), channel_id=1, source_target_pairs={{0,2},{1,3},{2,0},{3,1},{4,6},{5,7},{6,4},{7,5},{8,10},{9,11},{10,... | collective-permute-start | bytes 41480 | tf_op jit(solution)/shard_map/ppermute | solution.py:754
  584.5 7.4 %collective-permute-start.22 = (f32[4,27,32]{2,1,0:T(8,128)S(1)}, f32[4,27,32]{2,1,0:T(8,128)S(1)}, u32[]{:S(2)}, u32[]{:S(2)}) collective-permute-start(f32[4,27,32]{2,1,0:T(8,128)S(1)} %get-tuple-element.177), channel_id=1, source_target_pairs={{0,4},{1,5},{2,6},{3,7},{4,0},{5,1},{6,2},{7,3},{8,12},{9,13},{10,... | collective-permute-start | bytes 41480 | tf_op jit(solution)/shard_map/ppermute | solution.py:754
  586.2 5.7 collective-permute-start.23
  587.4 8.7 %collective-permute-start.24 = (bf16[128,768]{1,0:T(8,128)(2,1)S(1)}, bf16[128,768]{1,0:T(8,128)(2,1)S(1)}, u32[]{:S(2)}, u32[]{:S(2)}) collective-permute-start(bf16[128,768]{1,0:T(8,128)(2,1)S(1)} %pad_maximum_fusion.7), channel_id=1, source_target_pairs={{0,8},{1,9},{2,10},{3,11},{4,12},{5,13},{6,14},{7,15},{8,0},{9,1},... | collective-permute-start | bytes 589832 | tf_op jit(solution)/shard_map/ppermute | solution.py:754
  589.4 16.7 %collective-permute-start.25 = (bf16[128,768]{1,0:T(8,128)(2,1)S(1)}, bf16[128,768]{1,0:T(8,128)(2,1)S(1)}, u32[]{:S(2)}, u32[]{:S(2)}) collective-permute-start(bf16[128,768]{1,0:T(8,128)(2,1)S(1)} %pad_maximum_fusion.8), channel_id=1, source_target_pairs={{0,16},{1,17},{2,18},{3,19},{4,20},{5,21},{6,22},{7,23},{8,24},{9,... | collective-permute-start | bytes 589832 | tf_op jit(solution)/shard_map/ppermute | solution.py:754
  591.7 14.4 %collective-permute-start.26 = (bf16[128,768]{1,0:T(8,128)(2,1)S(1)}, bf16[128,768]{1,0:T(8,128)(2,1)S(1)}, u32[]{:S(2)}, u32[]{:S(2)}) collective-permute-start(bf16[128,768]{1,0:T(8,128)(2,1)S(1)} %pad_maximum_fusion.9), channel_id=1, source_target_pairs={{0,24},{1,25},{2,26},{3,27},{4,28},{5,29},{6,30},{7,31},{8,16},{9,... | collective-permute-start | bytes 589832 | tf_op jit(solution)/shard_map/ppermute | solution.py:754
  606.9 6.8 %collective-permute-start.27 = (f32[27,32]{1,0:T(8,128)S(1)}, f32[27,32]{1,0:T(8,128)S(1)}, u32[]{:S(2)}, u32[]{:S(2)}) collective-permute-start(f32[27,32]{1,0:T(8,128)S(1)} %get-tuple-element.184), channel_id=1, source_target_pairs={{0,8},{1,9},{2,10},{3,11},{4,12},{5,13},{6,14},{7,15},{8,0},{9,1},... | collective-permute-start | bytes 10376 | tf_op jit(solution)/shard_map/ppermute | solution.py:754
  609.9 4.6 collective-permute-start.28
  610.4 5.5 collective-permute-start.29
  619.4 1.3 copy-start.1
Sparse Core Ops, SparseCore 0:
  11.4 109.4 all-gather.2
  123.8 113.5 all-gather.4
  322.2 239.1 reduce-scatter.1

commit v4 on v3

--- a/solution.py
+++ b/solution.py
@@ -640,21 +640,48 @@
     )(table, *lefts, *rights)
 
 
-def feed_in_kernel(left_ref, right_ref, *rest):
-    out_ref = rest[-1]
+def feed_out_half_kernel(first, table_ref, left_ref, right_ref, out_ref, held):
+    part, _, piece, width = out_ref.shape
+    for row in range(part):
+        column = pl.multiple_of(table_ref[first + row] * piece, piece)
+        held[:, row * piece:(row + 1) * piece] = right_ref[:, pl.ds(column, piece)]
+    product = mm(left_ref[...], held[...]).astype(bf16)
+    for row in range(part):
+        for b in range(width // piece):
+            out_ref[row, 0, :, b * piece:(b + 1) * piece] = product[
+                b * piece:(b + 1) * piece, row * piece:(row + 1) * piece
+            ]
+
+
+def feed_out_half(table, left, right, inner, first):
+    outer = table.shape[0] - inner
+    model, tokens = left.shape
+    width = right.shape[1] // outer
+    part, piece = inner // 2, width // inner
+    return pl.pallas_call(
+        functools.partial(feed_out_half_kernel, first),
+        grid_spec=pltpu.PrefetchScalarGridSpec(
+            num_scalar_prefetch=1,
+            grid=(outer,),
+            in_specs=[
+                whole(left.shape), pl.BlockSpec((tokens, width), lambda o, table: (0, o)),
+            ],
+            out_specs=pl.BlockSpec(
+                (part, 1, piece, model), lambda o, table: (0, table[inner + o], 0, 0)
+            ),
+            scratch_shapes=[pltpu.VMEM((tokens, part * piece), bf16)],
+        ),
+        out_shape=jax.ShapeDtypeStruct((part, outer, piece, model), bf16),
+        compiler_params=params(),
+        cost_estimate=cost(right.size * model, 16 * MIB),
+        name="feed_out_half",
+    )(table, left, right)
+
+
+def feed_in_kernel(left_ref, right_ref, out_ref):
     _, inner, piece, width = out_ref.shape
     product = mm(left_ref[...], right_ref[...]).astype(bf16)
     out_ref[0] = product.reshape(inner, piece, width)
-
-
-def feed_out_kernel(left_ref, right_ref, out_ref):
-    _, inner, piece, width = out_ref.shape
-    product = mm(left_ref[...], right_ref[...]).astype(bf16)
-    for i in range(inner):
-        for b in range(width // piece):
-            out_ref[0, i, :, b * piece:(b + 1) * piece] = product[
-                b * piece:(b + 1) * piece, i * piece:(i + 1) * piece
-            ]
 
 
 def feed_rows_kernel(left_ref, right_ref, out_ref):
@@ -663,24 +690,17 @@
     out_ref[0] = product.reshape(inner, piece, width)
 
 
-def feed_weight_grad(
-    kernel, left, left_spec, right, right_spec, outer, inner, piece, width, at, total, held=None
-):
-    operands, specs = [left, right], [left_spec, right_spec]
-    if held is not None:
-        operands.append(held)
-        specs.append(pl.BlockSpec(memory_space=pl.ANY))
+def feed_weight_grad(kernel, left, left_spec, right, right_spec, outer, inner, piece, width):
     return pl.pallas_call(
         kernel,
         grid=(outer,),
-        in_specs=specs,
-        out_specs=pl.BlockSpec((1, inner, piece, width), lambda o: (o, 0, 0, at)),
-        out_shape=jax.ShapeDtypeStruct((outer, inner, piece, total), bf16),
-        input_output_aliases={} if held is None else {2: 0},
+        in_specs=[left_spec, right_spec],
+        out_specs=pl.BlockSpec((1, inner, piece, width), lambda o: (o, 0, 0, 0)),
+        out_shape=jax.ShapeDtypeStruct((outer, inner, piece, width), bf16),
         compiler_params=params(),
         cost_estimate=cost(8 * left.shape[1] * 1024 * 1024, 24 * MIB),
         name="feed_weight_grad",
-    )(*operands)
+    )(left, right)
 
 
 def entry_back_kernel(
@@ -786,17 +806,23 @@
     return lax.psum_scatter(flat, both, scatter_dimension=0, tiled=True).astype(f32)
 
 
+def halves_of(keep, moved, along_x, columns=slice(None)):
+    kept, sent = (slice(0, None, 2), slice(1, None, 2)) if along_x else (slice(0, 2), slice(2, 4))
+    return [
+        total_of((keep[rows, ..., columns], moved[rows, ..., columns]), keep.dtype)
+        for rows in (kept, sent)
+    ]
+
+
 def core_halves(keep, send, devices):
     moved = swap(send, 1, devices)
     cut = keep.shape[-1] // 256 * 128
-    result = []
-    for columns, kept, sent in (
-        (slice(0, cut), slice(0, None, 2), slice(1, None, 2)),
-        (slice(cut, None), slice(0, 2), slice(2, 4)),
-    ):
-        for rows in (kept, sent):
-            result.append(total_of((keep[rows, ..., columns], moved[rows, ..., columns]), keep.dtype))
-    return result
+    return halves_of(keep, moved, True, slice(0, cut)) + halves_of(keep, moved, False, slice(cut, None))
+
+
+def core_pair(keep_x, send_x, keep_y, send_y, devices):
+    moved_x, moved_y = swap(send_x, 1, devices), swap(send_y, 1, devices)
+    return halves_of(keep_x, moved_x, True) + halves_of(keep_y, moved_y, False)
 
 
 def first_halves(parts, devices):
@@ -818,6 +844,18 @@
         )
         for o in range(keep_x.shape[0])
     ]
+
+
+def outer_steps(parts):
+    return jnp.stack(parts[0::2]), jnp.stack(parts[1::2])
+
+
+def outer_step(keep, send, distance, devices):
+    moved = swap(send, distance, devices)
+    if keep.shape[0] == 1:
+        return keep[0].astype(f32) + moved[0].astype(f32)
+    totals = [total_of((keep[k], moved[k]), keep.dtype) for k in range(keep.shape[0])]
+    return outer_steps(totals)
 
 
 def chain_stages(chips):
@@ -941,50 +979,63 @@
         cross_mix, normed0, cotangent, vec, in_bias, weights, 2 * w1 + w2, g_in, 0, g_out, at_out, w1
     )
 
-    hidden_step = pl.BlockSpec((tokens, w4), lambda o: (0, o))
-    if together:
-        ffn_grads = feed_weight_grad(
-            feed_out_kernel, branch_grad_t, whole(branch_grad_t.shape), act, hidden_step,
-            outer, inner, rows, model, 1, 2 * w4,
-        )
-        ffn_grads = [feed_weight_grad(
-            feed_in_kernel, ffn_entry_t, whole(ffn_entry_t.shape), pre_grad, hidden_step,
-            outer, inner, rows, w4, 0, 2 * w4, ffn_grads,
-        )]
+    core, first_plane, second_plane = chain_stages(inner // 2)
+    chained = together and inner == 8
+    if chained:
+        half = inner // 2
+        send_in = half_weight_grads(table, [ffn_entry_t], [pre_grad], inner, half)
+        act, send_in = hold(act, send_in)
+        send_out = feed_out_half(table, branch_grad_t, act, inner, half)
+        pre_grad, send_out = hold(pre_grad, send_out)
+        keep_in = half_weight_grads(table, [ffn_entry_t], [pre_grad], inner, 0)
+        act, keep_in = hold(act, keep_in)
+        keep_out = feed_out_half(table, branch_grad_t, act, inner, 0)
+        parts_f = core_pair(keep_in, send_in, keep_out, send_out, devices)
     else:
+        hidden_step = pl.BlockSpec((tokens, w4), lambda o: (0, o))
         branch_grad = branch_grad_t.T
         ffn_grads = [
             feed_weight_grad(
                 feed_in_kernel, ffn_entry_t, whole(ffn_entry_t.shape), pre_grad, hidden_step,
-                outer, inner, rows, w4, 0, w4,
+                outer, inner, rows, w4,
             ),
             feed_weight_grad(
                 feed_rows_kernel, act, hidden_step, branch_grad, whole(branch_grad.shape),
-                outer, inner, ffn_out.shape[0], model, 0, model,
+                outer, inner, ffn_out.shape[0], model,
             ),
         ]
-    ffn_done = [joint_scatter(item) for item in ffn_grads]
-    core, first_plane, second_plane = chain_stages(inner // 2)
-
-    cross_mix_grad, _ = hold(cross_mix_grad, ffn_grads)
+        parts_f = ffn_done = [joint_scatter(item) for item in ffn_grads]
+    cross_mix_grad, parts_f = hold(cross_mix_grad, parts_f)
     queries_grad, pairs_grad = attend_back_call(
         cross_table, queries, 0, pairs, 0, pairs, hg, cross_mix_grad, cross_levels, own_column, memory_segments, False
     )
+    if chained:
+        parts_f = first_halves(parts_f, devices)
+    queries_grad, parts_f = hold(queries_grad, parts_f)
     start_grad, self_grad, self_mix_grad, sums0 = middle_back_call(
         residual1, queries_grad, normed0, rstd0, vec, weights, 1, 0, w1
     )
     lefts_a = [memory_t, cross_entry_t, cross_mix_t, self_mix_t]
     rights_a = [pairs_grad, queries_grad, cross_grad, self_grad]
     send_a = half_weight_grads(table, lefts_a, rights_a, inner, inner // 2)
-    rights_a, send_a = hold(rights_a, send_a)
+    if chained:
+        parts_f = outer_steps(second_halves(parts_f, devices))
+    rights_a, send_a, parts_f = hold(rights_a, send_a, parts_f)
     keep_a = half_weight_grads(table, lefts_a, rights_a, inner, 0)
     parts_a = core(keep_a, send_a, devices)
-    self_mix_grad, parts_a = hold(self_mix_grad, parts_a)
+    distance = inner
+    if chained:
+        parts_f = outer_step(*parts_f, distance, devices)
+    self_mix_grad, parts_a, parts_f = hold(self_mix_grad, parts_a, parts_f)
     (triple_grad,) = attend_back_call(
         self_table, triple, 0, triple, hg, triple, 2 * hg, self_mix_grad, self_levels, own_column, segment_ids, True
     )
     parts_a = first_plane(parts_a, devices)
-    triple_grad, parts_a = hold(triple_grad, parts_a)
+    while chained and isinstance(parts_f, (tuple, list)):
+        distance *= 2
+        parts_f = outer_step(*parts_f, distance, devices)
+    done_f = parts_f
+    triple_grad, parts_a, done_f = hold(triple_grad, parts_a, done_f)
     send_c = half_weight_grads(table, [self_entry_t], [triple_grad], inner, inner // 2)
     triple_grad, send_c = hold(triple_grad, send_c)
     keep_c = half_weight_grads(table, [self_entry_t], [triple_grad], inner, 0)
@@ -1013,9 +1064,9 @@
     done_c = outer_stage(parts_c, inner, devices)
     parts_e, done_c = hold(parts_e, done_c)
     extra = outer_stage(parts_e, inner, devices)
-    if together:
-        ffn_in_grad = ffn_done[0][:, :w4]
-        ffn_out_grad = ffn_done[0][:, w4:].reshape(rows, model // rows, rows)
+    if chained:
+        ffn_in_grad = done_f[:, :w4]
+        ffn_out_grad = done_f[:, w4:].reshape(rows, model // rows, rows)
         ffn_out_grad = ffn_out_grad.transpose(2, 1, 0).reshape(rows, model)
     else:
         ffn_in_grad, ffn_out_grad = ffn_done

time: 634 us -> 658 us (1.038)
  waiting for transfers between devices: 182 us -> 151 us
  other arithmetic: 41.4 us -> 67.8 us
  Pallas kernels: 323 us -> 340 us
  starting transfers between devices: 35.5 us -> 48 us
    ppermute x30 -> x38, waiting for transfers between devices: 177 us -> 146 us  [swap(): lax.ppermute(value, both, [(d, d ^ distance) for d in range(devices)])]
    convert_element_type x10 -> x17, other arithmetic: 18.6 us -> 40.7 us  [total_of(): return total.astype(kind)]
    pallas_call x4 -> x6, Pallas kernels: 50.6 us -> 71.4 us  [half_weight_grads(): pl.pallas_call(functools.partial(half_kernel, len(lefts), first), grid_sp...]
    ppermute x30 -> x38, starting transfers between devices: 35.4 us -> 47.9 us  [swap(): lax.ppermute(value, both, [(d, d ^ distance) for d in range(devices)])]
  transfers between devices with their start and end apart: 33 -> 40, of which waited for: 18 -> 16; matrix products, arithmetic and copies ran while one was open for 10% -> 10% of each run, Pallas kernels for 38% -> 38%
where the time goes in v4:
time: 658 us; the launch traced here: 653 us
  Pallas kernels  340 us (52%)
  waiting for transfers between devices  151 us (23%)
  other arithmetic  67.8 us (10%)
  starting transfers between devices  48 us (7%)
  local copies, waits for them, and re-layouts  31.9 us (5%)
  between operations  14.9 us (2%)
    ppermute x38, waiting for transfers between devices, swap(): lax.ppermute(value, both, [(d, d ^ distance) for d in range(devices)])  146 us
    pallas_call x2, Pallas kernels, attend_back_call(): pl.pallas_call(functools.partial(attend_back_kernel, causal), grid_spec=p...  77.9 us
    pallas_call x6, Pallas kernels, half_weight_grads(): pl.pallas_call(functools.partial(half_kernel, len(lefts), first), grid_sp...  71.4 us
    pallas_call x1, Pallas kernels, feed_call(): pl.pallas_call(functools.partial(feed_kernel, at_cross, at_in, at_out), g...  58.5 us
    pallas_call x2, Pallas kernels, attend_call(): pl.pallas_call(functools.partial(attend_kernel, causal), grid_spec=pltpu....  50.4 us
    ppermute x38, starting transfers between devices, swap(): lax.ppermute(value, both, [(d, d ^ distance) for d in range(devices)])  47.9 us
    convert_element_type x17, other arithmetic, total_of(): return total.astype(kind)  40.7 us
    pallas_call x2, Pallas kernels, feed_out_half(): pl.pallas_call(functools.partial(feed_out_half_kernel, first), grid_spec=...  21 us
  transfers between devices with their start and end apart: 40, of which 16 were waited for; matrix products, arithmetic and copies ran while one was open for 10% of the time, Pallas kernels for 38%

profile of v4, /device:TPU:0, one launch (start us, length us, event | category | flops | bytes accessed | tf_op | source)
XLA Modules:
  0.0 653.4 jit_solution(12528748587401770454)
XLA Ops:
  8.0 1.5 concatenate.66
  9.5 1.6 fusion.22
  14.7 3.0 collective-permute-start
  17.7 2.6 collective-permute-start.1
  21.3 13.9 %collective-permute-done = bf16[128,1280]{1,0:T(8,128)(2,1)S(1)} collective-permute-done((bf16[128,1280]{1,0:T(8,128)(2,1)S(1)}, bf16[128,1280]{1,0:T(8,128)(2,1)S(1)}, u32[]{:S(2)}, u32[]{:S(2)}) %collective-permute-start) | collective-permute-done | bytes 327712 | tf_op jit(solution)/shard_map/ppermute | solution.py:774
  35.2 12.8 %collective-permute-done.1 = bf16[128,1280]{1,0:T(8,128)(2,1)S(1)} collective-permute-done((bf16[128,1280]{1,0:T(8,128)(2,1)S(1)}, bf16[128,1280]{1,0:T(8,128)(2,1)S(1)}, u32[]{:S(2)}, u32[]{:S(2)}) %collective-permute-start.1) | collective-permute-done | bytes 327712 | tf_op jit(solution)/shard_map/ppermute | solution.py:774
  48.1 1.7 collective-permute-start.3
  49.8 1.5 collective-permute-start.4
  51.6 39.0 %collective-permute-done.3 = bf16[4,128,1280]{2,1,0:T(8,128)(2,1)S(1)} collective-permute-done((bf16[4,128,1280]{2,1,0:T(8,128)(2,1)S(1)}, bf16[4,128,1280]{2,1,0:T(8,128)(2,1)S(1)}, u32[]{:S(2)}, u32[]{:S(2)}) %collective-permute-start.3) | collective-permute-done | bytes 1310752 | tf_op jit(solution)/shard_map/ppermute | solution.py:774
  90.6 33.9 %collective-permute-done.5 = bf16[4,128,1280]{2,1,0:T(8,128)(2,1)} collective-permute-done((bf16[4,128,1280]{2,1,0:T(8,128)(2,1)S(1)}, bf16[4,128,1280]{2,1,0:T(8,128)(2,1)}, u32[]{:S(2)}, u32[]{:S(2)}) %collective-permute-start.5) | collective-permute-done | bytes 1310752 | tf_op jit(solution)/shard_map/ppermute | solution.py:774
  124.5 2.9 broadcast_in_dim.99
  129.8 2.6 bitcast_dynamic-update-slice_fusion.1
  132.4 2.6 bitcast_dynamic-update-slice_fusion
  142.6 12.1 %triple.1 = (bf16[1024,3072]{1,0:T(8,128)(2,1)}, bf16[1024,1024]{1,0:T(8,128)(2,1)}) custom-call(bf16[1024,1024]{1,0:T(8,128)(2,1)} %target_ref.3, bf16[1024,128]{1,0:T(8,128)(2,1)} %fusion.8.token_ref, bf16[128,1024]{1,0:T(8,128)(2,1)} %pad.15.lang_ref, bf16[4,1024,896]{2,1,0:T(8,128)(2,1)} %bitcast.165), custom_call_target="tpu_custom_call" | custom-call | flops 100663296 | bytes 262144 | tf_op jit(solution)/shard_map/triple/pallas_call | solution.py:89
  155.4 10.2 %bitcast_select_fusion.out_weight_ref.query_weight_ref.weight_ref.cross_hbm.pairs_weight_ref = bf16[4,1024,1280]{2,1,0:T(8,128)(2,1)} fusion(pred[1024]{0:T(1024)(128)(4,1)S(1)} %broadcast_in_dim.105, bf16[4,4,128,1280]{3,2,1,0:T(8,128)(2,1)} %collective-permute-done.6, bf16[4,4,128,1280]{3,2,1,0:T(8,128)(2,1)} %bitcast_dynamic-update-slice_fusion), kind=kLoop, calls=%fused_computation.1 | loop fusion | flops 5242880 | bytes 20972544 | tf_op jit(solution)/shard_map/jit(_where)/select_n | solution.py:892
  165.5 6.4 pairs.1
  171.9 26.2 %attend.2 = (bf16[1024,1024]{1,0:T(8,128)(2,1)}, bf16[1024,1024]{1,0:T(8,128)(2,1)}, f32[1024,128]{1,0:T(8,128)}) custom-call(s32[8]{0:T(128)} %pad_add_fusion.1.table_ref, bf16[1024,3072]{1,0:T(8,128)(2,1)} %get-tuple-element.128.q_ref.k_ref.v_ref, bf16[1024,3072]{1,0:T(8,128)(2,1)} %get-tuple-element.128.q_ref.k_ref.v_ref, ...), custom_call_target="tpu_custom_call" | custom-call | flops 187500000 | bytes 196608 | tf_op jit(solution)/shard_map/attend/pallas_call | solution.py:212
  198.1 10.8 %middle.1 = (f32[1024,1024]{1,0:T(8,128)}, f32[1024,1]{1,0:T(8,128)}, bf16[1024,1024]{1,0:T(8,128)(2,1)}, bf16[1024,1024]{1,0:T(8,128)(2,1)}) custom-call(bf16[1024,1024]{1,0:T(8,128)(2,1)} %get-tuple-element.129.mix_ref, bf16[1024,1024]{1,0:T(8,128)(2,1)} %target_ref.3, bf16[1024,128]{1,0:T(8,128)(2,1)} %fusion.8.token_ref, ...), custom_call_target="tpu_custom_call" | custom-call | flops 67108864 | bytes 262144 | tf_op jit(solution)/shard_map/middle/pallas_call | solution.py:363
  208.9 24.2 %attend.3 = (bf16[1024,1024]{1,0:T(8,128)(2,1)}, bf16[1024,1024]{1,0:T(8,128)(2,1)}, f32[1024,128]{1,0:T(8,128)}) custom-call(s32[8]{0:T(128)} %pad_add_fusion.table_ref, bf16[1024,1024]{1,0:T(8,128)(2,1)} %get-tuple-element.131.q_ref, bf16[512,2048]{1,0:T(8,128)(2,1)} %get-tuple-element.132.k_ref.v_ref, bf16[512,2048]{1,0:T(8,128)(2,1)} %get-tuple-element.132.k_ref.v_ref, ...), custom_call_target="tpu_custom_call" | custom-call | flops 187500000 | bytes 196608 | tf_op jit(solution)/shard_map/attend/pallas_call | solution.py:212
  233.1 4.2 all-gather.5.cloned.1.call-done
  237.4 58.5 %feed.1 = (bf16[1024,1024]{1,0:T(8,128)(2,1)}, bf16[1024,1024]{1,0:T(8,128)(2,1)}, bf16[1024,4096]{1,0:T(8,128)(2,1)}, bf16[1024,1024]{1,0:T(8,128)(2,1)}, bf16[...) custom-call(bf16[1024,1024]{1,0:T(8,128)(2,1)} %get-tuple-element.13, ...), custom_call_target="tpu_custom_call" | custom-call | flops 603979776 | bytes 983040 | tf_op jit(solution)/shard_map/feed/pallas_call | solution.py:495
  295.9 10.8 %half_weight_grads.6 = bf16[4,4,128,1024]{3,2,1,0:T(8,128)(2,1)} custom-call(s32[12]{0:T(128)} %pad_add_fusion.2.table_ref, bf16[1024,1024]{1,0:T(8,128)(2,1)} %get-tuple-element.140.refs_0_, bf16[1024,4096]{1,0:T(8,128)(2,1)} %get-tuple-element.144.refs_1_), custom_call_target="tpu_custom_call" | custom-call | flops 67108864 | bytes 196608 | tf_op jit(solution)/shard_map/half_weight_grads/pallas_call | solution.py:621
  306.6 10.5 %feed_out_half.2 = bf16[4,4,128,1024]{3,2,1,0:T(8,128)(2,1)} custom-call(s32[12]{0:T(128)} %pad_add_fusion.2.table_ref, bf16[1024,1024]{1,0:T(8,128)(2,1)} %get-tuple-element.143.left_ref, bf16[1024,4096]{1,0:T(8,128)(2,1)} %get-tuple-element.147.right_ref), custom_call_target="tpu_custom_call" | custom-call | flops 67108864 | bytes 262144 | tf_op jit(solution)/shard_map/feed_out_half/pallas_call | solution.py:661
  317.6 10.6 %half_weight_grads.7 = bf16[4,4,128,1024]{3,2,1,0:T(8,128)(2,1)} custom-call(s32[12]{0:T(128)} %pad_add_fusion.2.table_ref, bf16[1024,1024]{1,0:T(8,128)(2,1)} %get-tuple-element.140.refs_0_, bf16[1024,4096]{1,0:T(8,128)(2,1)} %get-tuple-element.144.refs_1_), custom_call_target="tpu_custom_call" | custom-call | flops 67108864 | bytes 196608 | tf_op jit(solution)/shard_map/half_weight_grads/pallas_call | solution.py:621
  328.2 10.5 %feed_out_half.3 = bf16[4,4,128,1024]{3,2,1,0:T(8,128)(2,1)} custom-call(s32[12]{0:T(128)} %pad_add_fusion.2.table_ref, bf16[1024,1024]{1,0:T(8,128)(2,1)} %get-tuple-element.143.left_ref, bf16[1024,4096]{1,0:T(8,128)(2,1)} %get-tuple-element.147.right_ref), custom_call_target="tpu_custom_call" | custom-call | flops 67108864 | bytes 262144 | tf_op jit(solution)/shard_map/feed_out_half/pallas_call | solution.py:661
  338.7 5.6 add_convert_fusion
  344.3 4.9 add_convert_fusion.2
  349.2 1.5 collective-permute-start.10
  351.3 35.6 %attend_back.2 = (bf16[1024,1024]{1,0:T(8,128)(2,1)}, bf16[512,2048]{1,0:T(8,128)(2,1)}) custom-call(s32[8]{0:T(128)} %pad_add_fusion.table_ref, bf16[1024,1024]{1,0:T(8,128)(2,1)} %get-tuple-element.131.q_ref, bf16[512,2048]{1,0:T(8,128)(2,1)} %get-tuple-element.132.k_ref.v_ref, bf16[512,2048]{1,0:T(8,128)(2,1)} %get-tuple-element.132.k_ref.v_ref, ...), custom_call_target="tpu_custom_call" | custom-call | flops 468750016 | bytes 262144 | tf_op jit(solution)/shard_map/attend_back/pallas_call | solution.py:319
  386.9 10.5 %collective-permute-done.10 = bf16[2,4,128,1024]{3,2,1,0:T(8,128)(2,1)} collective-permute-done((bf16[2,4,128,1024]{3,2,1,0:T(8,128)(2,1)}, bf16[2,4,128,1024]{3,2,1,0:T(8,128)(2,1)}, u32[]{:S(2)}, u32[]{:S(2)}) %collective-permute-start.10) | collective-permute-done | bytes 2097184 | tf_op jit(solution)/shard_map/ppermute | solution.py:774
  397.3 3.5 fusion.3
  400.9 3.6 fusion.1
  406.5 11.3 %middle_back.1 = (f32[1024,1024]{1,0:T(8,128)}, bf16[1024,1024]{1,0:T(8,128)(2,1)}, bf16[1024,1024]{1,0:T(8,128)(2,1)}, f32[8,1024]{1,0:T(8,128)}) custom-call(f32[1024,1024]{1,0:T(8,128)} %get-tuple-element.137.residual_ref, bf16[1024,1024]{1,0:T(8,128)(2,1)} %get-tuple-element.172.queries_grad_ref.refs_5_, f32[1024,1024]{1,0:T(8,128)} %get-tuple-element.134.normed_ref, ...), custom_call_target="tpu_custom_call" | custom-call | flops 67108864 | bytes 360448 | tf_op jit(solution)/shard_map/middle_back/pallas_call | solution.py:561
  417.9 15.9 %half_weight_grads.8 = bf16[4,4,128,1280]{3,2,1,0:T(8,128)(2,1)} custom-call(s32[12]{0:T(128)} %pad_add_fusion.2.table_ref, bf16[1024,512]{1,0:T(8,128)(2,1)} %get-tuple-element.160.refs_0_, bf16[1024,1024]{1,0:T(8,128)(2,1)} %get-tuple-element.161.refs_1_, bf16[1024,1024]{1,0:T(8,128)(2,1)} %get-tuple-element.162.refs_2_, ...), custom_call_target="tpu_custom_call" | custom-call | flops 67108864 | bytes 196608 | tf_op jit(solution)/shard_map/half_weight_grads/pallas_call | solution.py:621
  433.7 1.6 fusion.18
  436.2 5.6 collective-permute-start.14
  441.8 15.9 %half_weight_grads.9 = bf16[4,4,128,1280]{3,2,1,0:T(8,128)(2,1)} custom-call(s32[12]{0:T(128)} %pad_add_fusion.2.table_ref, bf16[1024,512]{1,0:T(8,128)(2,1)} %get-tuple-element.160.refs_0_, bf16[1024,1024]{1,0:T(8,128)(2,1)} %get-tuple-element.161.refs_1_, bf16[1024,1024]{1,0:T(8,128)(2,1)} %get-tuple-element.162.refs_2_, ...), custom_call_target="tpu_custom_call" | custom-call | flops 67108864 | bytes 196608 | tf_op jit(solution)/shard_map/half_weight_grads/pallas_call | solution.py:621
  457.7 7.9 %collective-permute-done.14 = bf16[2,128,2048]{2,1,0:T(8,128)(2,1)S(1)} collective-permute-done((bf16[2,128,2048]{2,1,0:T(8,128)(2,1)S(1)}, bf16[2,128,2048]{2,1,0:T(8,128)(2,1)S(1)}, u32[]{:S(2)}, u32[]{:S(2)}) %collective-permute-start.14) | collective-permute-done | bytes 1048608 | tf_op jit(solution)/shard_map/ppermute | solution.py:774
  466.8 5.9 add_convert_fusion.4
  472.7 1.7 collective-permute-start.16
  475.9 42.4 %attend_back.3.refs_1_.triple_ref = bf16[1024,3072]{1,0:T(8,128)(2,1)} custom-call(s32[8]{0:T(128)} %pad_add_fusion.1.table_ref, bf16[1024,3072]{1,0:T(8,128)(2,1)} %get-tuple-element.128.q_ref.k_ref.v_ref, bf16[1024,3072]{1,0:T(8,128)(2,1)} %get-tuple-element.128.q_ref.k_ref.v_ref, bf16[1024,3072]{1,0:T(8,128)(2,1)} %get-tuple-element.128.q_ref.k_ref.v_ref, ...), custom_call_target="tpu_custom_call" | custom-call | flops 468750016 | bytes 262144 | tf_op jit(solution)/shard_map/attend_back/pallas_call | solution.py:319
  519.6 2.7 fusion.7
  522.3 2.5 fusion.5
  524.8 9.1 %half_weight_grads.10 = bf16[4,4,128,768]{3,2,1,0:T(8,128)(2,1)} custom-call(s32[12]{0:T(128)} %pad_add_fusion.2.table_ref, bf16[1024,1024]{1,0:T(8,128)(2,1)} %get-tuple-element.187.refs_0_, bf16[1024,3072]{1,0:T(8,128)(2,1)} %attend_back.3.refs_1_.triple_ref), custom_call_target="tpu_custom_call" | custom-call | flops 50331648 | bytes 196608 | tf_op jit(solution)/shard_map/half_weight_grads/pallas_call | solution.py:621
  534.1 3.5 collective-permute-start.20
  538.9 9.2 %half_weight_grads.11 = bf16[4,4,128,768]{3,2,1,0:T(8,128)(2,1)} custom-call(s32[12]{0:T(128)} %pad_add_fusion.2.table_ref, bf16[1024,1024]{1,0:T(8,128)(2,1)} %get-tuple-element.187.refs_0_, bf16[1024,3072]{1,0:T(8,128)(2,1)} %attend_back.3.refs_1_.triple_ref), custom_call_target="tpu_custom_call" | custom-call | flops 50331648 | bytes 196608 | tf_op jit(solution)/shard_map/half_weight_grads/pallas_call | solution.py:621
  548.1 3.3 collective-permute-done.19
  554.6 4.0 add_convert_fusion.12
  558.5 2.3 collective-permute-start.24
  560.8 2.1 collective-permute-start.25
  567.2 2.2 collective-permute-start.21
  569.4 20.4 %entry_back.1 = (f32[1024,1024]{1,0:T(8,128)}, f32[512,1024]{1,0:T(8,128)}, f32[16,1024]{1,0:T(8,128)}) custom-call(f32[1024,1024]{1,0:T(8,128)} %get-tuple-element.158.start_ref, bf16[1024,3072]{1,0:T(8,128)(2,1)} %attend_back.3.refs_1_.triple_ref, bf16[512,2048]{1,0:T(8,128)(2,1)} %get-tuple-element.171.refs_4_.pairs_ref, bf16[4,1024,896]{2,1,0:T(8,128)(2,1)} %bitcast.166, ...), custom_call_target="tpu_custom_call" | custom-call | flops 134217728 | bytes 655360 | tf_op jit(solution)/shard_map/entry_back/pallas_call | solution.py:741
  589.8 2.2 convert_add_fusion
  593.4 2.1 fusion.11
  601.0 4.1 collective-permute-done.27
  606.2 4.1 collective-permute-done.28
  612.3 2.5 collective-permute-start.31
  617.3 2.1 collective-permute-start.33
  619.4 1.9 collective-permute-start.34
  622.1 3.6 collective-permute-done.32
  625.8 8.3 %collective-permute-done.33 = bf16[128,768]{1,0:T(8,128)(2,1)S(1)} collective-permute-done((bf16[128,768]{1,0:T(8,128)(2,1)S(1)}, bf16[128,768]{1,0:T(8,128)(2,1)S(1)}, u32[]{:S(2)}, u32[]{:S(2)}) %collective-permute-start.33) | collective-permute-done | bytes 196640 | tf_op jit(solution)/shard_map/ppermute | solution.py:774
  634.9 2.7 collective-permute-start.35
  638.5 1.5 collective-permute-start.37
  642.3 1.7 collective-permute-done.37
  (184 shorter events, 52.8 us)
Async XLA Ops:
  7.2 13.3 %copy-start.6 = (bf16[128,1024]{1,0:T(8,128)(2,1)S(1)}, bf16[128,1024]{1,0:T(8,128)(2,1)}, u32[]{:S(2)}) copy-start(bf16[128,1024]{1,0:T(8,128)(2,1)} %param.31) | copy-start | bytes 786436
  7.2 13.3 %copy-start.5 = (bf16[128,1024]{1,0:T(8,128)(2,1)S(1)}, bf16[128,1024]{1,0:T(8,128)(2,1)}, u32[]{:S(2)}) copy-start(bf16[128,1024]{1,0:T(8,128)(2,1)} %param.33) | copy-start | bytes 786436
  7.2 117.3 %all-gather.3.cloned.1.call-start = ((), (), s32[]{:S(2)}) async-start(), calls=%async_computation | async-start | bytes 7569408 | tf_op jit(solution)/shard_map/all_gather | solution.py:769
  11.2 226.2 %all-gather.5.cloned.1.call-start = ((), (), s32[]{:S(2)}) async-start(), calls=%async_computation.1 | async-start | bytes 17301504 | tf_op jit(solution)/shard_map/all_gather | solution.py:769
  14.7 20.5 %collective-permute-start = (bf16[128,1280]{1,0:T(8,128)(2,1)S(1)}, bf16[128,1280]{1,0:T(8,128)(2,1)S(1)}, u32[]{:S(2)}, u32[]{:S(2)}) collective-permute-start(bf16[128,1280]{1,0:T(8,128)(2,1)S(1)} %constant_dynamic-update-slice_fusion), channel_id=1, source_target_pairs={{0,8},{1,9},{2,10},{3,11},{4,12},{5,13},{6,14},{7,15},{8,0},{9,1},... | collective-permute-start | bytes 983048 | tf_op jit(solution)/shard_map/ppermute | solution.py:774
  17.7 30.3 %collective-permute-start.1 = (bf16[128,1280]{1,0:T(8,128)(2,1)S(1)}, bf16[128,1280]{1,0:T(8,128)(2,1)S(1)}, u32[]{:S(2)}, u32[]{:S(2)}) collective-permute-start(bf16[128,1280]{1,0:T(8,128)(2,1)S(1)} %constant_dynamic-update-slice_fusion), channel_id=1, source_target_pairs={{0,16},{1,17},{2,18},{3,19},{4,20},{5,21},{6,22},{7,23},{8,24},{9,... | collective-permute-start | bytes 983048 | tf_op jit(solution)/shard_map/ppermute | solution.py:774
  20.3 27.7 %collective-permute-start.2 = (bf16[128,1280]{1,0:T(8,128)(2,1)S(1)}, bf16[128,1280]{1,0:T(8,128)(2,1)S(1)}, u32[]{:S(2)}, u32[]{:S(2)}) collective-permute-start(bf16[128,1280]{1,0:T(8,128)(2,1)S(1)} %constant_dynamic-update-slice_fusion), channel_id=1, source_target_pairs={{0,24},{1,25},{2,26},{3,27},{4,28},{5,29},{6,30},{7,31},{8,16},{9,... | collective-permute-start | bytes 983048 | tf_op jit(solution)/shard_map/ppermute | solution.py:774
  48.1 42.6 %collective-permute-start.3 = (bf16[4,128,1280]{2,1,0:T(8,128)(2,1)S(1)}, bf16[4,128,1280]{2,1,0:T(8,128)(2,1)S(1)}, u32[]{:S(2)}, u32[]{:S(2)}) collective-permute-start(bf16[4,128,1280]{2,1,0:T(8,128)(2,1)S(1)} %bitcast_dynamic-update-slice_fusion.4), channel_id=1, source_target_pairs={{0,2},{1,3},{2,0},{3,1},{4,6},{5,7},{6,4},{7,5},{8,10},{9,11},{10,... | collective-permute-start | bytes 3932168 | tf_op jit(solution)/shard_map/ppermute | solution.py:774
  49.8 40.8 %collective-permute-start.4 = (bf16[4,128,1280]{2,1,0:T(8,128)(2,1)S(1)}, bf16[4,128,1280]{2,1,0:T(8,128)(2,1)}, u32[]{:S(2)}, u32[]{:S(2)}) collective-permute-start(bf16[4,128,1280]{2,1,0:T(8,128)(2,1)S(1)} %bitcast_dynamic-update-slice_fusion.4), channel_id=1, source_target_pairs={{0,4},{1,5},{2,6},{3,7},{4,0},{5,1},{6,2},{7,3},{8,12},{9,13},{10,... | collective-permute-start | bytes 3932168 | tf_op jit(solution)/shard_map/ppermute | solution.py:774
  51.4 73.2 %collective-permute-start.5 = (bf16[4,128,1280]{2,1,0:T(8,128)(2,1)S(1)}, bf16[4,128,1280]{2,1,0:T(8,128)(2,1)}, u32[]{:S(2)}, u32[]{:S(2)}) collective-permute-start(bf16[4,128,1280]{2,1,0:T(8,128)(2,1)S(1)} %bitcast_dynamic-update-slice_fusion.4), channel_id=1, source_target_pairs={{0,6},{1,7},{2,4},{3,5},{4,2},{5,3},{6,0},{7,1},{8,14},{9,15},{10,... | collective-permute-start | bytes 3932168 | tf_op jit(solution)/shard_map/ppermute | solution.py:774
  129.7 5.2 copy-start.8
  132.4 4.1 copy-start.11
  132.4 5.5 copy-start.17
  132.4 6.1 copy-start.16
  134.9 20.4 %collective-permute-start.6 = (bf16[4,4,128,1280]{3,2,1,0:T(8,128)(2,1)}, bf16[4,4,128,1280]{3,2,1,0:T(8,128)(2,1)}, u32[]{:S(2)}, u32[]{:S(2)}) collective-permute-start(bf16[4,4,128,1280]{3,2,1,0:T(8,128)(2,1)} %bitcast_dynamic-update-slice_fusion), channel_id=1, source_target_pairs={{0,1},{1,0},{2,3},{3,2},{4,5},{5,4},{6,7},{7,6},{8,9},{9,8},{10,11... | collective-permute-start | bytes 15728648 | tf_op jit(solution)/shard_map/ppermute | solution.py:774
  317.1 21.6 %collective-permute-start.8 = (bf16[4,4,128,1024]{3,2,1,0:T(8,128)(2,1)}, bf16[4,4,128,1024]{3,2,1,0:T(8,128)(2,1)}, u32[]{:S(2)}, u32[]{:S(2)}) collective-permute-start(bf16[4,4,128,1024]{3,2,1,0:T(8,128)(2,1)} %feed_out_half.2), channel_id=1, source_target_pairs={{0,1},{1,0},{2,3},{3,2},{4,5},{5,4},{6,7},{7,6},{8,9},{9,8},{10,11... | collective-permute-start | bytes 12582920 | tf_op jit(solution)/shard_map/ppermute | solution.py:774
  317.4 26.9 %collective-permute-start.7 = (bf16[4,4,128,1024]{3,2,1,0:T(8,128)(2,1)}, bf16[4,4,128,1024]{3,2,1,0:T(8,128)(2,1)}, u32[]{:S(2)}, u32[]{:S(2)}) collective-permute-start(bf16[4,4,128,1024]{3,2,1,0:T(8,128)(2,1)} %half_weight_grads.6), channel_id=1, source_target_pairs={{0,1},{1,0},{2,3},{3,2},{4,5},{5,4},{6,7},{7,6},{8,9},{9,8},{10,11... | collective-permute-start | bytes 12582920 | tf_op jit(solution)/shard_map/ppermute | solution.py:774
  338.7 5.6 copy-start
  349.2 48.1 %collective-permute-start.10 = (bf16[2,4,128,1024]{3,2,1,0:T(8,128)(2,1)}, bf16[2,4,128,1024]{3,2,1,0:T(8,128)(2,1)}, u32[]{:S(2)}, u32[]{:S(2)}) collective-permute-start(bf16[2,4,128,1024]{3,2,1,0:T(8,128)(2,1)} %get-tuple-element.155), channel_id=1, source_target_pairs={{0,4},{1,5},{2,6},{3,7},{4,0},{5,1},{6,2},{7,3},{8,12},{9,13},{10,... | collective-permute-start | bytes 6291464 | tf_op jit(solution)/shard_map/ppermute | solution.py:774
  350.7 50.2 %collective-permute-start.9 = (bf16[2,4,128,1024]{3,2,1,0:T(8,128)(2,1)}, bf16[2,4,128,1024]{3,2,1,0:T(8,128)(2,1)}, u32[]{:S(2)}, u32[]{:S(2)}) collective-permute-start(bf16[2,4,128,1024]{3,2,1,0:T(8,128)(2,1)} %get-tuple-element.153), channel_id=1, source_target_pairs={{0,2},{1,3},{2,0},{3,1},{4,6},{5,7},{6,4},{7,5},{8,10},{9,11},{10,... | collective-permute-start | bytes 6291464 | tf_op jit(solution)/shard_map/ppermute | solution.py:774
  386.9 14.0 %copy-start.2 = (bf16[2,4,128,1024]{3,2,1,0:T(8,128)(2,1)S(1)}, bf16[2,4,128,1024]{3,2,1,0:T(8,128)(2,1)}, u32[]{:S(2)}) copy-start(bf16[2,4,128,1024]{3,2,1,0:T(8,128)(2,1)} %get-tuple-element.152) | copy-start | bytes 6291460
  404.5 29.3 %collective-permute-start.11 = (bf16[4,128,1024]{2,1,0:T(8,128)(2,1)}, bf16[4,128,1024]{2,1,0:T(8,128)(2,1)}, u32[]{:S(2)}, u32[]{:S(2)}) collective-permute-start(bf16[4,128,1024]{2,1,0:T(8,128)(2,1)} %get-tuple-element.168), channel_id=1, source_target_pairs={{0,4},{1,5},{2,6},{3,7},{4,0},{5,1},{6,2},{7,3},{8,12},{9,13},{10,... | collective-permute-start | bytes 3145736 | tf_op jit(solution)/shard_map/ppermute | solution.py:774
  406.0 29.4 %collective-permute-start.12 = (bf16[4,128,1024]{2,1,0:T(8,128)(2,1)}, bf16[4,128,1024]{2,1,0:T(8,128)(2,1)S(1)}, u32[]{:S(2)}, u32[]{:S(2)}) collective-permute-start(bf16[4,128,1024]{2,1,0:T(8,128)(2,1)} %get-tuple-element.170), channel_id=1, source_target_pairs={{0,2},{1,3},{2,0},{3,1},{4,6},{5,7},{6,4},{7,5},{8,10},{9,11},{10,... | collective-permute-start | bytes 3145736 | tf_op jit(solution)/shard_map/ppermute | solution.py:774
  436.1 30.6 %collective-permute-start.13 = (bf16[4,4,128,1280]{3,2,1,0:T(8,128)(2,1)}, bf16[4,4,128,1280]{3,2,1,0:T(8,128)(2,1)}, u32[]{:S(2)}, u32[]{:S(2)}) collective-permute-start(bf16[4,4,128,1280]{3,2,1,0:T(8,128)(2,1)} %half_weight_grads.8), channel_id=1, source_target_pairs={{0,1},{1,0},{2,3},{3,2},{4,5},{5,4},{6,7},{7,6},{8,9},{9,8},{10,11... | collective-permute-start | bytes 15728648 | tf_op jit(solution)/shard_map/ppermute | solution.py:774
  436.2 29.4 %collective-permute-start.14 = (bf16[2,128,2048]{2,1,0:T(8,128)(2,1)S(1)}, bf16[2,128,2048]{2,1,0:T(8,128)(2,1)S(1)}, u32[]{:S(2)}, u32[]{:S(2)}) collective-permute-start(bf16[2,128,2048]{2,1,0:T(8,128)(2,1)S(1)} %pad_maximum_fusion.1), channel_id=1, source_target_pairs={{0,8},{1,9},{2,10},{3,11},{4,12},{5,13},{6,14},{7,15},{8,0},{9,1},... | collective-permute-start | bytes 3145736 | tf_op jit(solution)/shard_map/ppermute | solution.py:774
  472.7 47.0 %collective-permute-start.16 = (bf16[2,4,128,640]{3,2,1,0:T(8,128)(2,1)}, bf16[2,4,128,640]{3,2,1,0:T(8,128)(2,1)}, u32[]{:S(2)}, u32[]{:S(2)}) collective-permute-start(bf16[2,4,128,640]{3,2,1,0:T(8,128)(2,1)} %get-tuple-element.183), channel_id=1, source_target_pairs={{0,4},{1,5},{2,6},{3,7},{4,0},{5,1},{6,2},{7,3},{8,12},{9,13},{10,... | collective-permute-start | bytes 3932168 | tf_op jit(solution)/shard_map/ppermute | solution.py:774
  474.4 43.9 %collective-permute-start.17 = (bf16[1,128,2048]{2,1,0:T(8,128)(2,1)S(1)}, bf16[1,128,2048]{2,1,0:T(8,128)(2,1)}, u32[]{:S(2)}, u32[]{:S(2)}) collective-permute-start(bf16[1,128,2048]{2,1,0:T(8,128)(2,1)S(1)} %get-tuple-element.185), channel_id=1, source_target_pairs={{0,16},{1,17},{2,18},{3,19},{4,20},{5,21},{6,22},{7,23},{8,24},{9,... | collective-permute-start | bytes 1572872 | tf_op jit(solution)/shard_map/ppermute | solution.py:774
  475.5 46.8 %collective-permute-start.15 = (bf16[2,4,128,640]{3,2,1,0:T(8,128)(2,1)}, bf16[2,4,128,640]{3,2,1,0:T(8,128)(2,1)}, u32[]{:S(2)}, u32[]{:S(2)}) collective-permute-start(bf16[2,4,128,640]{3,2,1,0:T(8,128)(2,1)} %get-tuple-element.181), channel_id=1, source_target_pairs={{0,2},{1,3},{2,0},{3,1},{4,6},{5,7},{6,4},{7,5},{8,10},{9,11},{10,... | collective-permute-start | bytes 3932168 | tf_op jit(solution)/shard_map/ppermute | solution.py:774
  533.9 20.6 %collective-permute-start.18 = (bf16[4,4,128,768]{3,2,1,0:T(8,128)(2,1)}, bf16[4,4,128,768]{3,2,1,0:T(8,128)(2,1)}, u32[]{:S(2)}, u32[]{:S(2)}) collective-permute-start(bf16[4,4,128,768]{3,2,1,0:T(8,128)(2,1)} %half_weight_grads.10), channel_id=1, source_target_pairs={{0,1},{1,0},{2,3},{3,2},{4,5},{5,4},{6,7},{7,6},{8,9},{9,8},{10,11... | collective-permute-start | bytes 9437192 | tf_op jit(solution)/shard_map/ppermute | solution.py:774
  534.0 17.4 %collective-permute-start.19 = (bf16[4,128,640]{2,1,0:T(8,128)(2,1)}, bf16[4,128,640]{2,1,0:T(8,128)(2,1)S(1)}, u32[]{:S(2)}, u32[]{:S(2)}) collective-permute-start(bf16[4,128,640]{2,1,0:T(8,128)(2,1)} %get-tuple-element.191), channel_id=1, source_target_pairs={{0,4},{1,5},{2,6},{3,7},{4,0},{5,1},{6,2},{7,3},{8,12},{9,13},{10,... | collective-permute-start | bytes 1966088 | tf_op jit(solution)/shard_map/ppermute | solution.py:774
  534.1 18.7 %collective-permute-start.20 = (bf16[4,128,640]{2,1,0:T(8,128)(2,1)}, bf16[4,128,640]{2,1,0:T(8,128)(2,1)S(1)}, u32[]{:S(2)}, u32[]{:S(2)}) collective-permute-start(bf16[4,128,640]{2,1,0:T(8,128)(2,1)} %get-tuple-element.193), channel_id=1, source_target_pairs={{0,2},{1,3},{2,0},{3,1},{4,6},{5,7},{6,4},{7,5},{8,10},{9,11},{10,... | collective-permute-start | bytes 1966088 | tf_op jit(solution)/shard_map/ppermute | solution.py:774
  548.1 4.7 copy-start.4
  551.5 3.1 copy-start.1
  554.5 8.7 %copy-start.15 = (f32[8,1024]{1,0:T(8,128)S(1)}, f32[8,1024]{1,0:T(8,128)}, u32[]{:S(2)}) copy-start(f32[8,1024]{1,0:T(8,128)} %get-tuple-element.208) | copy-start | bytes 98308
  554.5 10.4 %copy-start.12 = (f32[1,4096]{1,0:T(1,128)S(1)}, f32[1,4096]{1,0:T(1,128)}, u32[]{:S(2)}) copy-start(f32[1,4096]{1,0:T(1,128)} %get-tuple-element.209) | copy-start | bytes 49156
  558.5 31.2 %collective-permute-start.23 = (bf16[128,1280]{1,0:T(8,128)(2,1)}, bf16[128,1280]{1,0:T(8,128)(2,1)}, u32[]{:S(2)}, u32[]{:S(2)}) collective-permute-start(bf16[128,1280]{1,0:T(8,128)(2,1)} %pad_maximum_fusion.5), channel_id=1, source_target_pairs={{0,8},{1,9},{2,10},{3,11},{4,12},{5,13},{6,14},{7,15},{8,0},{9,1},... | collective-permute-start | bytes 983048 | tf_op jit(solution)/shard_map/ppermute | solution.py:774
  558.5 31.2 %collective-permute-start.24 = (bf16[128,1280]{1,0:T(8,128)(2,1)}, bf16[128,1280]{1,0:T(8,128)(2,1)}, u32[]{:S(2)}, u32[]{:S(2)}) collective-permute-start(bf16[128,1280]{1,0:T(8,128)(2,1)} %pad_maximum_fusion.6), channel_id=1, source_target_pairs={{0,16},{1,17},{2,18},{3,19},{4,20},{5,21},{6,22},{7,23},{8,24},{9,... | collective-permute-start | bytes 983048 | tf_op jit(solution)/shard_map/ppermute | solution.py:774
  560.8 29.0 %collective-permute-start.25 = (bf16[128,1280]{1,0:T(8,128)(2,1)S(1)}, bf16[128,1280]{1,0:T(8,128)(2,1)}, u32[]{:S(2)}, u32[]{:S(2)}) collective-permute-start(bf16[128,1280]{1,0:T(8,128)(2,1)S(1)} %pad_maximum_fusion.7), channel_id=1, source_target_pairs={{0,24},{1,25},{2,26},{3,27},{4,28},{5,29},{6,30},{7,31},{8,16},{9,... | collective-permute-start | bytes 983048 | tf_op jit(solution)/shard_map/ppermute | solution.py:774
  562.9 29.1 %collective-permute-start.22 = (bf16[2,4,128,384]{3,2,1,0:T(8,128)(2,1)}, bf16[2,4,128,384]{3,2,1,0:T(8,128)(2,1)}, u32[]{:S(2)}, u32[]{:S(2)}) collective-permute-start(bf16[2,4,128,384]{3,2,1,0:T(8,128)(2,1)} %get-tuple-element.201), channel_id=1, source_target_pairs={{0,4},{1,5},{2,6},{3,7},{4,0},{5,1},{6,2},{7,3},{8,12},{9,13},{10,... | collective-permute-start | bytes 2359304 | tf_op jit(solution)/shard_map/ppermute | solution.py:774
  567.2 26.2 %collective-permute-start.21 = (bf16[2,4,128,384]{3,2,1,0:T(8,128)(2,1)}, bf16[2,4,128,384]{3,2,1,0:T(8,128)(2,1)}, u32[]{:S(2)}, u32[]{:S(2)}) collective-permute-start(bf16[2,4,128,384]{3,2,1,0:T(8,128)(2,1)} %get-tuple-element.199), channel_id=1, source_target_pairs={{0,2},{1,3},{2,0},{3,1},{4,6},{5,7},{6,4},{7,5},{8,10},{9,11},{10,... | collective-permute-start | bytes 2359304 | tf_op jit(solution)/shard_map/ppermute | solution.py:774
  592.0 4.7 copy-start.9
  592.0 4.7 copy-start.10
  592.0 4.7 copy-start.13
  592.0 4.7 copy-start.14
  595.4 9.6 %collective-permute-start.27 = (bf16[4,128,384]{2,1,0:T(8,128)(2,1)}, bf16[4,128,384]{2,1,0:T(8,128)(2,1)}, u32[]{:S(2)}, u32[]{:S(2)}) collective-permute-start(bf16[4,128,384]{2,1,0:T(8,128)(2,1)} %get-tuple-element.211), channel_id=1, source_target_pairs={{0,4},{1,5},{2,6},{3,7},{4,0},{5,1},{6,2},{7,3},{8,12},{9,13},{10,... | collective-permute-start | bytes 1179656 | tf_op jit(solution)/shard_map/ppermute | solution.py:774
  598.7 1.6 collective-permute-start.26
  598.8 11.5 %collective-permute-start.28 = (bf16[4,128,384]{2,1,0:T(8,128)(2,1)S(1)}, bf16[4,128,384]{2,1,0:T(8,128)(2,1)S(1)}, u32[]{:S(2)}, u32[]{:S(2)}) collective-permute-start(bf16[4,128,384]{2,1,0:T(8,128)(2,1)S(1)} %get-tuple-element.213), channel_id=1, source_target_pairs={{0,2},{1,3},{2,0},{3,1},{4,6},{5,7},{6,4},{7,5},{8,10},{9,11},{10,... | collective-permute-start | bytes 1179656 | tf_op jit(solution)/shard_map/ppermute | solution.py:774
  611.2 8.2 %collective-permute-start.29 = (f32[4,27,32]{2,1,0:T(8,128)}, f32[4,27,32]{2,1,0:T(8,128)S(1)}, u32[]{:S(2)}, u32[]{:S(2)}) collective-permute-start(f32[4,27,32]{2,1,0:T(8,128)} %get-tuple-element.215), channel_id=1, source_target_pairs={{0,2},{1,3},{2,0},{3,1},{4,6},{5,7},{6,4},{7,5},{8,10},{9,11},{10,... | collective-permute-start | bytes 41480 | tf_op jit(solution)/shard_map/ppermute | solution.py:774
  611.5 9.8 %collective-permute-start.30 = (f32[4,27,32]{2,1,0:T(8,128)}, f32[4,27,32]{2,1,0:T(8,128)}, u32[]{:S(2)}, u32[]{:S(2)}) collective-permute-start(f32[4,27,32]{2,1,0:T(8,128)} %get-tuple-element.216), channel_id=1, source_target_pairs={{0,4},{1,5},{2,6},{3,7},{4,0},{5,1},{6,2},{7,3},{8,12},{9,13},{10,... | collective-permute-start | bytes 41480 | tf_op jit(solution)/shard_map/ppermute | solution.py:774
  612.3 9.0 %collective-permute-start.31 = (f32[4,27,32]{2,1,0:T(8,128)S(1)}, f32[4,27,32]{2,1,0:T(8,128)}, u32[]{:S(2)}, u32[]{:S(2)}) collective-permute-start(f32[4,27,32]{2,1,0:T(8,128)S(1)} %get-tuple-element.217), channel_id=1, source_target_pairs={{0,6},{1,7},{2,4},{3,5},{4,2},{5,3},{6,0},{7,1},{8,14},{9,15},{10,... | collective-permute-start | bytes 41480 | tf_op jit(solution)/shard_map/ppermute | solution.py:774
  615.6 1.3 copy-start.7
  615.6 24.4 %copy-start.3 = (f32[128,1280]{1,0:T(8,128)S(1)}, f32[128,1280]{1,0:T(8,128)}, u32[]{:S(2)}) copy-start(f32[128,1280]{1,0:T(8,128)} %convert_add_fusion) | copy-start | bytes 1966084
  616.9 8.9 %collective-permute-start.32 = (bf16[128,768]{1,0:T(8,128)(2,1)S(1)}, bf16[128,768]{1,0:T(8,128)(2,1)S(1)}, u32[]{:S(2)}, u32[]{:S(2)}) collective-permute-start(bf16[128,768]{1,0:T(8,128)(2,1)S(1)} %copy-done.7), channel_id=1, source_target_pairs={{0,8},{1,9},{2,10},{3,11},{4,12},{5,13},{6,14},{7,15},{8,0},{9,1},... | collective-permute-start | bytes 589832 | tf_op jit(solution)/shard_map/ppermute | solution.py:774
  617.3 16.8 %collective-permute-start.33 = (bf16[128,768]{1,0:T(8,128)(2,1)S(1)}, bf16[128,768]{1,0:T(8,128)(2,1)S(1)}, u32[]{:S(2)}, u32[]{:S(2)}) collective-permute-start(bf16[128,768]{1,0:T(8,128)(2,1)S(1)} %pad_maximum_fusion.10), channel_id=1, source_target_pairs={{0,16},{1,17},{2,18},{3,19},{4,20},{5,21},{6,22},{7,23},{8,24},{9,... | collective-permute-start | bytes 589832 | tf_op jit(solution)/shard_map/ppermute | solution.py:774
  619.4 14.7 %collective-permute-start.34 = (bf16[128,768]{1,0:T(8,128)(2,1)S(1)}, bf16[128,768]{1,0:T(8,128)(2,1)S(1)}, u32[]{:S(2)}, u32[]{:S(2)}) collective-permute-start(bf16[128,768]{1,0:T(8,128)(2,1)S(1)} %pad_maximum_fusion.11), channel_id=1, source_target_pairs={{0,24},{1,25},{2,26},{3,27},{4,28},{5,29},{6,30},{7,31},{8,16},{9,... | collective-permute-start | bytes 589832 | tf_op jit(solution)/shard_map/ppermute | solution.py:774
  634.9 6.6 %collective-permute-start.35 = (f32[27,32]{1,0:T(8,128)S(1)}, f32[27,32]{1,0:T(8,128)S(1)}, u32[]{:S(2)}, u32[]{:S(2)}) collective-permute-start(f32[27,32]{1,0:T(8,128)S(1)} %get-tuple-element.223), channel_id=1, source_target_pairs={{0,8},{1,9},{2,10},{3,11},{4,12},{5,13},{6,14},{7,15},{8,0},{9,1},... | collective-permute-start | bytes 10376 | tf_op jit(solution)/shard_map/ppermute | solution.py:774
  637.7 4.6 collective-permute-start.36
  638.5 5.5 collective-permute-start.37
Sparse Core Ops, SparseCore 0:
  11.4 109.4 all-gather.2
  123.8 113.4 all-gather.4

commit v5 on v3

--- a/solution.py
+++ b/solution.py
@@ -47,6 +47,14 @@
 
 def weight_step(model, width, at):
     return pl.BlockSpec((1, model, width), lambda o, *_: (o, 0, at))
+
+
+def weight_slices(packed, width, at):
+    outer, model, _ = packed.shape
+    return [
+        pl.BlockSpec((1, model, width), lambda *_, o=o: (o, 0, at), pipeline_mode=pl.Buffered(1))
+        for o in range(outer)
+    ]
 
 
 def weight_block(packed, width, at):
@@ -243,9 +251,11 @@
     causal, table_ref, q_ref, k_ref, v_ref, grad_ref, level_ref, own_ref, other_ref, *rest
 ):
     if causal:
-        out_ref, keys_t, values_t = rest
+        out_hbm, out_ref, keys_t, values_t, sems, pair_sems = rest
+        pair_hbm, pair_ref, shift = out_hbm, out_ref, HEADS * HEAD_DIM
     else:
-        out_ref, pair_ref, keys_t, values_t = rest
+        out_hbm, pair_hbm, out_ref, pair_ref, keys_t, values_t, sems, pair_sems = rest
+        shift = 0
     block_index = pl.program_id(0)
     group = pl.program_id(1)
     blocks = pl.num_programs(0)
@@ -294,13 +304,35 @@
         own_rows = pl.ds(pl.multiple_of(block_index * BLOCK, BLOCK), BLOCK)
         out_ref[own_rows, pl.ds(columns, width)] = grad_q
 
+    def query_copy(b, g):
+        spot = (
+            pl.ds(pl.multiple_of(b * BLOCK, BLOCK), BLOCK), pl.ds(pl.multiple_of(g * width, width), width)
+        )
+        return pltpu.make_async_copy(out_ref.at[spot], out_hbm.at[spot], sems.at[b, g])
+
+    def pair_copy(g, at):
+        spot = (
+            slice(None), pl.ds(pl.multiple_of(g * width + (shift + at * model), width), width)
+        )
+        return pltpu.make_async_copy(pair_ref.at[spot], pair_hbm.at[spot], pair_sems.at[g, at])
+
     for_window(table_ref, body)
-    pair_out, shift = (out_ref, model) if causal else (pair_ref, 0)
+    query_copy(block_index, group).start()
 
     @pl.when(block_index == blocks - 1)
     def _():
-        pair_out[:, pl.ds(columns + shift, width)] = keys_t[rows, :].astype(bf16).T
-        pair_out[:, pl.ds(columns + shift + model, width)] = values_t[rows, :].astype(bf16).T
+        pair_ref[:, pl.ds(columns + shift, width)] = keys_t[rows, :].astype(bf16).T
+        pair_ref[:, pl.ds(columns + shift + model, width)] = values_t[rows, :].astype(bf16).T
+        pair_copy(group, 0).start()
+        pair_copy(group, 1).start()
+
+    @pl.when((block_index == blocks - 1) & (group == pl.num_programs(1) - 1))
+    def _():
+        for g in range(model // width):
+            for b in range(out_ref.shape[0] // BLOCK):
+                query_copy(b, g).wait()
+            pair_copy(g, 0).wait()
+            pair_copy(g, 1).wait()
 
 
 def attend_back_call(
@@ -330,8 +362,11 @@
                 pl.BlockSpec((BLOCK, 1), lambda b, g, t: (b, 0)),
                 pl.BlockSpec((1, others), lambda b, g, t: (0, 0)),
             ],
-            out_specs=[whole(item.shape) for item in out_shape],
-            scratch_shapes=[pltpu.VMEM((model, others), f32), pltpu.VMEM((model, others), f32)],
+            out_specs=[pl.BlockSpec(memory_space=pl.ANY)] * len(out_shape),
+            scratch_shapes=[pltpu.VMEM(item.shape, bf16) for item in out_shape]
+            + [pltpu.VMEM((model, others), f32), pltpu.VMEM((model, others), f32)]
+            + [pltpu.SemaphoreType.DMA((tokens // BLOCK, HEADS // GROUP)),
+               pltpu.SemaphoreType.DMA((HEADS // GROUP, 2))],
         ),
         out_shape=out_shape,
         compiler_params=params(),
@@ -525,10 +560,11 @@
 
 
 def middle_back_kernel(
-    residual_ref, queries_grad_ref, normed_ref, rstd_ref, vec_ref, query_weight_ref, out_weight_ref,
-    start_ref, branch_grad_ref, mix_grad_ref, sums_ref,
+    outer, residual_ref, queries_grad_ref, normed_ref, rstd_ref, vec_ref, *rest
 ):
-    outer, _, width = out_weight_ref.shape
+    query_weights, out_weights = rest[:outer], rest[outer:2 * outer]
+    start_ref, branch_grad_ref, mix_grad_ref, sums_ref = rest[2 * outer:]
+    width = out_weights[0].shape[2]
 
     @pl.when(pl.program_id(0) == 0)
     def _():
@@ -537,7 +573,7 @@
     grad_first = 2.0 * residual_ref[...]
     for o in range(outer):
         grad_first = grad_first + mm_nt(
-            queries_grad_ref[:, o * width:(o + 1) * width], query_weight_ref[o]
+            queries_grad_ref[:, o * width:(o + 1) * width], query_weights[o][0]
         )
     normed = normed_ref[...]
     sums_ref[0:1, :] += column_sum(grad_first * normed)
@@ -546,10 +582,10 @@
     start_ref[...] = back
     branch_grad = back.astype(bf16)
     branch_grad_ref[...] = branch_grad
-    mix_grad = mm_nt(branch_grad[:, 0:width], out_weight_ref[0])
+    mix_grad = mm_nt(branch_grad[:, 0:width], out_weights[0][0])
     for o in range(1, outer):
         mix_grad = mix_grad + mm_nt(
-            branch_grad[:, o * width:(o + 1) * width], out_weight_ref[o]
+            branch_grad[:, o * width:(o + 1) * width], out_weights[o][0]
         )
     mix_grad_ref[...] = mix_grad.astype(bf16)
 
@@ -558,15 +594,16 @@
     tokens, model = residual.shape
     row = lambda r: (r, 0)
     blocked = pl.BlockSpec((BLOCK, model), row)
+    outer = packed.shape[0]
     return pl.pallas_call(
-        middle_back_kernel,
+        functools.partial(middle_back_kernel, outer),
         grid=(tokens // BLOCK,),
         in_specs=[
             blocked, blocked, blocked,
             pl.BlockSpec((BLOCK, 1), row),
             whole(vec.shape),
-            weight_block(packed, width, at_cross),
-            weight_block(packed, width, at_self),
+            *weight_slices(packed, width, at_cross),
+            *weight_slices(packed, width, at_self),
         ],
         out_specs=[blocked, blocked, blocked, pl.BlockSpec((8, model), lambda r: (0, 0))],
         out_shape=[
@@ -578,12 +615,20 @@
         compiler_params=params(),
         cost_estimate=cost(4 * tokens * model * model, 22 * MIB),
         name="middle_back",
-    )(residual, queries_grad, normed, rstd, vec, packed, packed)
+    )(residual, queries_grad, normed, rstd, vec, *[packed] * (2 * outer))
+
+
+def column_copy(source, held, sems, at):
+    width = held.shape[2]
+    columns = pl.ds(pl.multiple_of(at * width, width), width)
+    return pltpu.make_async_copy(source.at[:, columns], held.at[at], sems.at[at])
 
 
 def half_kernel(count, first, table_ref, *refs):
     lefts, rights = refs[:count], refs[count:2 * count]
-    out_ref, held, sems = refs[2 * count], refs[2 * count + 1:-1], refs[-1]
+    out_ref, held = refs[2 * count], refs[2 * count + 1:3 * count + 1]
+    held_rights = refs[3 * count + 1:4 * count + 1]
+    sems, right_sems = refs[4 * count + 1], refs[4 * count + 2:]
     part, _, piece, _ = out_ref.shape
     step = pl.program_id(0)
 
@@ -599,6 +644,10 @@
         for at in range(count):
             for row in range(part):
                 copy(at, row).start()
+            column_copy(rights[at], held_rights[at], right_sems[at], 0).start()
+        for o in range(1, held_rights[0].shape[0]):
+            for at in range(count):
+                column_copy(rights[at], held_rights[at], right_sems[at], o).start()
 
     lo = 0
     for at in range(count):
@@ -607,8 +656,9 @@
             for row in range(part):
                 copy(at, row).wait()
 
-        width = rights[at].shape[1]
-        product = mm(held[at][...], rights[at][...]).astype(bf16)
+        column_copy(rights[at], held_rights[at], right_sems[at], step).wait()
+        width = held_rights[at].shape[2]
+        product = mm(held[at][...], held_rights[at][step]).astype(bf16)
         out_ref[:, 0, :, lo:lo + width] = product.reshape(part, piece, width)
         lo += width
 
@@ -623,15 +673,14 @@
         grid_spec=pltpu.PrefetchScalarGridSpec(
             num_scalar_prefetch=1,
             grid=(outer,),
-            in_specs=[pl.BlockSpec(memory_space=pl.ANY)] * len(lefts) + [
-                pl.BlockSpec((right.shape[0], width), lambda o, table: (0, o))
-                for right, width in zip(rights, widths)
-            ],
+            in_specs=[pl.BlockSpec(memory_space=pl.ANY)] * (len(lefts) + len(rights)),
             out_specs=pl.BlockSpec(
                 (part, 1, piece, sum(widths)), lambda o, table: (0, table[inner + o], 0, 0)
             ),
             scratch_shapes=[pltpu.VMEM((part * piece, left.shape[1]), bf16) for left in lefts]
-            + [pltpu.SemaphoreType.DMA((len(lefts), part))],
+            + [pltpu.VMEM((outer, right.shape[0], width), bf16) for right, width in zip(rights, widths)]
+            + [pltpu.SemaphoreType.DMA((len(lefts), part))]
+            + [pltpu.SemaphoreType.DMA((outer,))] * len(rights),
         ),
         out_shape=jax.ShapeDtypeStruct((part, outer, piece, sum(widths)), bf16),
         compiler_params=params(),
@@ -640,21 +689,36 @@
     )(table, *lefts, *rights)
 
 
-def feed_in_kernel(left_ref, right_ref, *rest):
-    out_ref = rest[-1]
+def next_columns(right_hbm, held, sems):
+    step = pl.program_id(0)
+
+    @pl.when(step == 0)
+    def _():
+        for o in range(held.shape[0]):
+            column_copy(right_hbm, held, sems, o).start()
+
+    column_copy(right_hbm, held, sems, step).wait()
+    return held[step]
+
+
+def feed_in_kernel(left_ref, right_hbm, *rest):
+    out_ref, held, sems = rest[-3:]
     _, inner, piece, width = out_ref.shape
-    product = mm(left_ref[...], right_ref[...]).astype(bf16)
+    product = mm(left_ref[...], next_columns(right_hbm, held, sems)).astype(bf16)
     out_ref[0] = product.reshape(inner, piece, width)
 
 
-def feed_out_kernel(left_ref, right_ref, out_ref):
+def feed_out_kernel(left_ref, right_hbm, out_ref, held, sems):
     _, inner, piece, width = out_ref.shape
-    product = mm(left_ref[...], right_ref[...]).astype(bf16)
+    product = mm(left_ref[...], next_columns(right_hbm, held, sems)).astype(bf16)
     for i in range(inner):
         for b in range(width // piece):
             out_ref[0, i, :, b * piece:(b + 1) * piece] = product[
                 b * piece:(b + 1) * piece, i * piece:(i + 1) * piece
             ]
+
+
+in_place = pl.BlockSpec(memory_space=pl.ANY)
 
 
 def feed_rows_kernel(left_ref, right_ref, out_ref):
@@ -673,6 +737,10 @@
     return pl.pallas_call(
         kernel,
         grid=(outer,),
+        scratch_shapes=[
+            pltpu.VMEM((outer, right.shape[0], right.shape[1] // outer), bf16),
+            pltpu.SemaphoreType.DMA((outer,)),
+        ] if right_spec is in_place else [],
         in_specs=specs,
         out_specs=pl.BlockSpec((1, inner, piece, width), lambda o: (o, 0, 0, at)),
         out_shape=jax.ShapeDtypeStruct((outer, inner, piece, total), bf16),
@@ -684,11 +752,11 @@
 
 
 def entry_back_kernel(
-    start_ref, triple_ref, pairs_ref, weight_ref, pairs_weight_ref, token_t_ref,
-    out_ref, memory_ref, lang_ref,
+    outer, start_ref, triple_ref, pairs_ref, token_t_ref, *rest
 ):
-    outer, _, width = weight_ref.shape
-    pair_width = pairs_weight_ref.shape[2]
+    weights, pairs_weights = rest[:outer], rest[outer:2 * outer]
+    out_ref, memory_ref, lang_ref = rest[2 * outer:]
+    width, pair_width = weights[0].shape[2], pairs_weights[0].shape[2]
 
     @pl.when(pl.program_id(0) == 0)
     def _():
@@ -696,7 +764,7 @@
 
     grad = 2.0 * start_ref[...]
     for o in range(outer):
-        grad = grad + mm_nt(triple_ref[:, o * width:(o + 1) * width], weight_ref[o])
+        grad = grad + mm_nt(triple_ref[:, o * width:(o + 1) * width], weights[o][0])
     out_ref[...] = grad
     high = grad.astype(bf16)
     rest = grad - high.astype(f32)
@@ -704,10 +772,10 @@
     low = (rest - mid.astype(f32)).astype(bf16)
     token_t = token_t_ref[...]
     lang_ref[...] += mm(token_t, high) + mm(token_t, mid) + mm(token_t, low)
-    memory_grad = mm_nt(pairs_ref[:, 0:pair_width], pairs_weight_ref[0])
+    memory_grad = mm_nt(pairs_ref[:, 0:pair_width], pairs_weights[0][0])
     for o in range(1, outer):
         memory_grad = memory_grad + mm_nt(
-            pairs_ref[:, o * pair_width:(o + 1) * pair_width], pairs_weight_ref[o]
+            pairs_ref[:, o * pair_width:(o + 1) * pair_width], pairs_weights[o][0]
         )
     memory_ref[...] = memory_grad
 
@@ -719,15 +787,15 @@
     memory_block = pairs_grad.shape[0] // steps
     row = lambda r: (r, 0)
     return pl.pallas_call(
-        entry_back_kernel,
+        functools.partial(entry_back_kernel, outer),
         grid=(steps,),
         in_specs=[
             pl.BlockSpec((BLOCK, model), row),
             pl.BlockSpec((BLOCK, outer * width), row),
             pl.BlockSpec((memory_block, outer * pairs_width), row),
-            weight_block(packed, width, 0),
-            weight_block(pairs_packed, pairs_width, at),
             pl.BlockSpec((token_t.shape[0], BLOCK), lambda r: (0, r)),
+            *weight_slices(packed, width, 0),
+            *weight_slices(pairs_packed, pairs_width, at),
         ],
         out_specs=[
             pl.BlockSpec((BLOCK, model), row),
@@ -742,7 +810,7 @@
         compiler_params=params(),
         cost_estimate=cost(2 * tokens * model * outer * (width + pairs_width // 2), 40 * MIB),
         name="entry_back",
-    )(start_grad, triple_grad, pairs_grad, packed, pairs_packed, token_t)
+    )(start_grad, triple_grad, pairs_grad, token_t, *[packed] * outer, *[pairs_packed] * outer)
 
 
 def gather(shard, outer):
@@ -944,18 +1012,18 @@
     hidden_step = pl.BlockSpec((tokens, w4), lambda o: (0, o))
     if together:
         ffn_grads = feed_weight_grad(
-            feed_out_kernel, branch_grad_t, whole(branch_grad_t.shape), act, hidden_step,
+            feed_out_kernel, branch_grad_t, whole(branch_grad_t.shape), act, in_place,
             outer, inner, rows, model, 1, 2 * w4,
         )
         ffn_grads = [feed_weight_grad(
-            feed_in_kernel, ffn_entry_t, whole(ffn_entry_t.shape), pre_grad, hidden_step,
+            feed_in_kernel, ffn_entry_t, whole(ffn_entry_t.shape), pre_grad, in_place,
             outer, inner, rows, w4, 0, 2 * w4, ffn_grads,
         )]
     else:
         branch_grad = branch_grad_t.T
         ffn_grads = [
             feed_weight_grad(
-                feed_in_kernel, ffn_entry_t, whole(ffn_entry_t.shape), pre_grad, hidden_step,
+                feed_in_kernel, ffn_entry_t, whole(ffn_entry_t.shape), pre_grad, in_place,
                 outer, inner, rows, w4, 0, w4,
             ),
             feed_weight_grad(

time: 634 us -> 635 us (level)
  transfers between devices with their start and end apart: 33 -> 33, of which waited for: 18 -> 18; matrix products, arithmetic and copies ran while one was open for 10% -> 10% of each run, Pallas kernels for 38% -> 37%
where the time goes in v5:
time: 635 us; the launch traced here: 631 us
  Pallas kernels  324 us (51%)
  waiting for transfers between devices  180 us (28%)
  other arithmetic  41.4 us (7%)
  starting transfers between devices  39.7 us (6%)
  local copies, waits for them, and re-layouts  31.3 us (5%)
  between operations  14.5 us (2%)
    ppermute x30, waiting for transfers between devices, swap(): lax.ppermute(value, both, [(d, d ^ distance) for d in range(devices)])  176 us
    pallas_call x2, Pallas kernels, attend_back_call(): pl.pallas_call(functools.partial(attend_back_kernel, causal), grid_spec=p...  76.2 us
    pallas_call x1, Pallas kernels, feed_call(): pl.pallas_call(functools.partial(feed_kernel, at_cross, at_in, at_out), g...  58.1 us
    pallas_call x2, Pallas kernels, attend_call(): pl.pallas_call(functools.partial(attend_kernel, causal), grid_spec=pltpu....  51.2 us
    pallas_call x4, Pallas kernels, half_weight_grads(): pl.pallas_call(functools.partial(half_kernel, len(lefts), first), grid_sp...  47.8 us
    ppermute x30, starting transfers between devices, swap(): lax.ppermute(value, both, [(d, d ^ distance) for d in range(devices)])  39.6 us
    pallas_call x2, Pallas kernels, feed_weight_grad(): pl.pallas_call(kernel, grid=(outer,), scratch_shapes=[pltpu.VMEM((outer,...  29.5 us
    pallas_call x1, Pallas kernels, entry_back_call(): pl.pallas_call(functools.partial(entry_back_kernel, outer), grid=(steps,)...  20.4 us
  transfers between devices with their start and end apart: 33, of which 18 were waited for; matrix products, arithmetic and copies ran while one was open for 10% of the time, Pallas kernels for 37%

profile of v5, /device:TPU:0, one launch (start us, length us, event | category | flops | bytes accessed | tf_op | source)
XLA Modules:
  0.0 630.7 jit_solution(1510388419844200397)
XLA Ops:
  8.0 1.5 concatenate.54
  9.5 1.6 fusion.10
  14.7 3.0 collective-permute-start
  17.7 2.6 collective-permute-start.1
  21.3 13.9 %collective-permute-done = bf16[128,1280]{1,0:T(8,128)(2,1)S(1)} collective-permute-done((bf16[128,1280]{1,0:T(8,128)(2,1)S(1)}, bf16[128,1280]{1,0:T(8,128)(2,1)S(1)}, u32[]{:S(2)}, u32[]{:S(2)}) %collective-permute-start) | collective-permute-done | bytes 327712 | tf_op jit(solution)/shard_map/ppermute | solution.py:822
  35.2 12.8 %collective-permute-done.1 = bf16[128,1280]{1,0:T(8,128)(2,1)S(1)} collective-permute-done((bf16[128,1280]{1,0:T(8,128)(2,1)S(1)}, bf16[128,1280]{1,0:T(8,128)(2,1)S(1)}, u32[]{:S(2)}, u32[]{:S(2)}) %collective-permute-start.1) | collective-permute-done | bytes 327712 | tf_op jit(solution)/shard_map/ppermute | solution.py:822
  48.1 1.7 collective-permute-start.3
  49.9 1.5 collective-permute-start.4
  51.7 39.1 %collective-permute-done.3 = bf16[4,128,1280]{2,1,0:T(8,128)(2,1)S(1)} collective-permute-done((bf16[4,128,1280]{2,1,0:T(8,128)(2,1)S(1)}, bf16[4,128,1280]{2,1,0:T(8,128)(2,1)S(1)}, u32[]{:S(2)}, u32[]{:S(2)}) %collective-permute-start.3) | collective-permute-done | bytes 1310752 | tf_op jit(solution)/shard_map/ppermute | solution.py:822
  90.7 33.8 %collective-permute-done.5 = bf16[4,128,1280]{2,1,0:T(8,128)(2,1)} collective-permute-done((bf16[4,128,1280]{2,1,0:T(8,128)(2,1)S(1)}, bf16[4,128,1280]{2,1,0:T(8,128)(2,1)}, u32[]{:S(2)}, u32[]{:S(2)}) %collective-permute-start.5) | collective-permute-done | bytes 1310752 | tf_op jit(solution)/shard_map/ppermute | solution.py:822
  124.6 2.9 broadcast_in_dim.99
  127.5 1.2 bitcast_dynamic-update-slice_fusion.3
  128.6 1.1 bitcast_dynamic-update-slice_fusion.2
  129.8 2.6 bitcast_dynamic-update-slice_fusion.1
  132.4 2.5 bitcast_dynamic-update-slice_fusion
  138.8 1.3 slice.355
  142.0 12.3 %triple.1 = (bf16[1024,3072]{1,0:T(8,128)(2,1)}, bf16[1024,1024]{1,0:T(8,128)(2,1)}) custom-call(bf16[1024,1024]{1,0:T(8,128)(2,1)} %target_ref.3, bf16[1024,128]{1,0:T(8,128)(2,1)} %fusion.4.token_ref, bf16[128,1024]{1,0:T(8,128)(2,1)} %pad.15.lang_ref, bf16[4,1024,896]{2,1,0:T(8,128)(2,1)} %bitcast.129), custom_call_target="tpu_custom_call" | custom-call | flops 100663296 | bytes 262144 | tf_op jit(solution)/shard_map/triple/pallas_call | solution.py:97
  154.9 10.1 %bitcast_select_fusion.out_weight_ref.query_weight_ref.weight_ref.cross_hbm.rest_0_.rest_1_.rest_2_.rest_3_.rest_4_.rest_5_.rest_6_.rest_7_ = bf16[4,1024,1280]{2,1,0:T(8,128)(2,1)} fusion(pred[1024]{0:T(1024)(128)(4,1)S(1)} %broadcast_in_dim.105, bf16[4,4,128,1280]{3,2,1,0:T(8,128)(2,1)} %collective-permute-done.6, ...), kind=kLoop, calls=%fused_computation.1 | loop fusion | flops 5242880 | bytes 20972544 | tf_op jit(solution)/shard_map/jit(_where)/select_n | solution.py:922
  165.0 6.4 %pairs.1 = (bf16[512,2048]{1,0:T(8,128)(2,1)}, bf16[1024,512]{1,0:T(8,128)(2,1)}) custom-call(bf16[512,1024]{1,0:T(8,128)(2,1)} %memory_ref.1, bf16[4,1024,1280]{2,1,0:T(8,128)(2,1)} %bitcast_select_fusion.out_weight_ref.query_weight_ref.weight_ref.cross_hbm.rest_0_.rest_1_.rest_2_.rest_3_.rest_4_.rest_5_.rest_6_.rest_7_), custom_call_target="tpu_custom_call" | custom-call | flops 33554432 | bytes 131072 | tf_op jit(solution)/shard_map/pairs/pallas_call | solution.py:127
  171.4 26.2 %attend.2 = (bf16[1024,1024]{1,0:T(8,128)(2,1)}, bf16[1024,1024]{1,0:T(8,128)(2,1)}, f32[1024,128]{1,0:T(8,128)}) custom-call(s32[8]{0:T(128)} %pad_add_fusion.1.table_ref, bf16[1024,3072]{1,0:T(8,128)(2,1)} %get-tuple-element.108.q_ref.k_ref.v_ref, bf16[1024,3072]{1,0:T(8,128)(2,1)} %get-tuple-element.108.q_ref.k_ref.v_ref, ...), custom_call_target="tpu_custom_call" | custom-call | flops 187500000 | bytes 196608 | tf_op jit(solution)/shard_map/attend/pallas_call | solution.py:220
  197.6 10.8 %middle.1 = (f32[1024,1024]{1,0:T(8,128)}, f32[1024,1]{1,0:T(8,128)}, bf16[1024,1024]{1,0:T(8,128)(2,1)}, bf16[1024,1024]{1,0:T(8,128)(2,1)}) custom-call(bf16[1024,1024]{1,0:T(8,128)(2,1)} %get-tuple-element.109.mix_ref, bf16[1024,1024]{1,0:T(8,128)(2,1)} %target_ref.3, bf16[1024,128]{1,0:T(8,128)(2,1)} %fusion.4.token_ref, ...), custom_call_target="tpu_custom_call" | custom-call | flops 67108864 | bytes 262144 | tf_op jit(solution)/shard_map/middle/pallas_call | solution.py:398
  208.4 25.0 %attend.3 = (bf16[1024,1024]{1,0:T(8,128)(2,1)}, bf16[1024,1024]{1,0:T(8,128)(2,1)}, f32[1024,128]{1,0:T(8,128)}) custom-call(s32[8]{0:T(128)} %pad_add_fusion.table_ref, bf16[1024,1024]{1,0:T(8,128)(2,1)} %get-tuple-element.111.q_ref, bf16[512,2048]{1,0:T(8,128)(2,1)} %get-tuple-element.112.k_ref.v_ref, bf16[512,2048]{1,0:T(8,128)(2,1)} %get-tuple-element.112.k_ref.v_ref, ...), custom_call_target="tpu_custom_call" | custom-call | flops 187500000 | bytes 196608 | tf_op jit(solution)/shard_map/attend/pallas_call | solution.py:220
  233.4 4.0 all-gather.5.cloned.1.call-done
  237.4 58.1 %feed.1 = (bf16[1024,1024]{1,0:T(8,128)(2,1)}, bf16[1024,1024]{1,0:T(8,128)(2,1)}, bf16[1024,4096]{1,0:T(8,128)(2,1)}, bf16[1024,1024]{1,0:T(8,128)(2,1)}, bf16[...) custom-call(bf16[1024,1024]{1,0:T(8,128)(2,1)} %get-tuple-element.11, ...), custom_call_target="tpu_custom_call" | custom-call | flops 603979776 | bytes 983040 | tf_op jit(solution)/shard_map/feed/pallas_call | solution.py:530
  295.5 15.2 %feed_weight_grad.2.rest_0_ = bf16[4,8,128,2048]{3,2,1,0:T(8,128)(2,1)} custom-call(bf16[1024,1024]{1,0:T(8,128)(2,1)} %get-tuple-element.121.left_ref, bf16[1024,4096]{1,0:T(8,128)(2,1)} %get-tuple-element.122.right_hbm), custom_call_target="tpu_custom_call" | custom-call | flops 134217728 | bytes 393216 | tf_op jit(solution)/shard_map/feed_weight_grad/pallas_call | solution.py:737
  310.7 14.3 %feed_weight_grad.3 = bf16[4,8,128,2048]{3,2,1,0:T(8,128)(2,1)} custom-call(bf16[1024,1024]{1,0:T(8,128)(2,1)} %get-tuple-element.119.left_ref, bf16[1024,4096]{1,0:T(8,128)(2,1)} %get-tuple-element.120.right_hbm, bf16[4,8,128,2048]{3,2,1,0:T(8,128)(2,1)} %feed_weight_grad.2.rest_0_), custom_call_target="tpu_custom_call", output_to_operand_aliasing={{}: (2, {})} | custom-call | flops 134217728 | bytes 393216 | tf_op jit(solution)/shard_map/feed_weight_grad/pallas_call | solution.py:737
  326.3 35.0 %attend_back.2 = (bf16[1024,1024]{1,0:T(8,128)(2,1)}, bf16[512,2048]{1,0:T(8,128)(2,1)}) custom-call(s32[8]{0:T(128)} %pad_add_fusion.table_ref, bf16[1024,1024]{1,0:T(8,128)(2,1)} %get-tuple-element.111.q_ref, bf16[512,2048]{1,0:T(8,128)(2,1)} %get-tuple-element.112.k_ref.v_ref, bf16[512,2048]{1,0:T(8,128)(2,1)} %get-tuple-element.112.k_ref.v_ref, ...), custom_call_target="tpu_custom_call" | custom-call | flops 468750016 | bytes 262144 | tf_op jit(solution)/shard_map/attend_back/pallas_call | solution.py:351
  361.3 11.5 %middle_back.1 = (f32[1024,1024]{1,0:T(8,128)}, bf16[1024,1024]{1,0:T(8,128)(2,1)}, bf16[1024,1024]{1,0:T(8,128)(2,1)}, f32[8,1024]{1,0:T(8,128)}) custom-call(f32[1024,1024]{1,0:T(8,128)} %get-tuple-element.117.residual_ref, bf16[1024,1024]{1,0:T(8,128)(2,1)} %get-tuple-element.137.queries_grad_ref.refs_5_, f32[1024,1024]{1,0:T(8,128)} %get-tuple-element.114.normed_ref, ...), custom_call_target="tpu_custom_call" | custom-call | flops 67108864 | bytes 360448 | tf_op jit(solution)/shard_map/middle_back/pallas_call | solution.py:598
  372.8 15.6 %half_weight_grads.4 = bf16[4,4,128,1280]{3,2,1,0:T(8,128)(2,1)} custom-call(s32[12]{0:T(128)} %pad_add_fusion.2.table_ref, bf16[1024,512]{1,0:T(8,128)(2,1)} %get-tuple-element.129.refs_0_, bf16[1024,1024]{1,0:T(8,128)(2,1)} %get-tuple-element.130.refs_1_, bf16[1024,1024]{1,0:T(8,128)(2,1)} %get-tuple-element.131.refs_2_, ...), custom_call_target="tpu_custom_call" | custom-call | flops 67108864 | bytes 196608 | tf_op jit(solution)/shard_map/half_weight_grads/pallas_call | solution.py:671
  388.6 15.2 %half_weight_grads.5 = bf16[4,4,128,1280]{3,2,1,0:T(8,128)(2,1)} custom-call(s32[12]{0:T(128)} %pad_add_fusion.2.table_ref, bf16[1024,512]{1,0:T(8,128)(2,1)} %get-tuple-element.129.refs_0_, bf16[1024,1024]{1,0:T(8,128)(2,1)} %get-tuple-element.130.refs_1_, bf16[1024,1024]{1,0:T(8,128)(2,1)} %get-tuple-element.131.refs_2_, ...), custom_call_target="tpu_custom_call" | custom-call | flops 67108864 | bytes 196608 | tf_op jit(solution)/shard_map/half_weight_grads/pallas_call | solution.py:671
  403.9 5.9 add_convert_fusion
  409.7 1.3 collective-permute-start.9
  411.6 41.2 %attend_back.3.refs_1_.triple_ref = bf16[1024,3072]{1,0:T(8,128)(2,1)} custom-call(s32[8]{0:T(128)} %pad_add_fusion.1.table_ref, bf16[1024,3072]{1,0:T(8,128)(2,1)} %get-tuple-element.108.q_ref.k_ref.v_ref, bf16[1024,3072]{1,0:T(8,128)(2,1)} %get-tuple-element.108.q_ref.k_ref.v_ref, bf16[1024,3072]{1,0:T(8,128)(2,1)} %get-tuple-element.108.q_ref.k_ref.v_ref, ...), custom_call_target="tpu_custom_call" | custom-call | flops 468750016 | bytes 262144 | tf_op jit(solution)/shard_map/attend_back/pallas_call | solution.py:351
  453.4 1.6 fusion.3
  455.0 15.8 %collective-permute-done.8 = bf16[2,4,128,640]{3,2,1,0:T(8,128)(2,1)} collective-permute-done((bf16[2,4,128,640]{3,2,1,0:T(8,128)(2,1)}, bf16[2,4,128,640]{3,2,1,0:T(8,128)(2,1)}, u32[]{:S(2)}, u32[]{:S(2)}) %collective-permute-start.8) | collective-permute-done | bytes 1310752 | tf_op jit(solution)/shard_map/ppermute | solution.py:822
  470.8 2.5 fusion.1
  473.3 8.3 %half_weight_grads.6 = bf16[4,4,128,768]{3,2,1,0:T(8,128)(2,1)} custom-call(s32[12]{0:T(128)} %pad_add_fusion.2.table_ref, bf16[1024,1024]{1,0:T(8,128)(2,1)} %get-tuple-element.148.refs_0_, bf16[1024,3072]{1,0:T(8,128)(2,1)} %attend_back.3.refs_1_.triple_ref), custom_call_target="tpu_custom_call" | custom-call | flops 50331648 | bytes 196608 | tf_op jit(solution)/shard_map/half_weight_grads/pallas_call | solution.py:671
  481.7 2.9 collective-permute-start.11
  486.0 8.6 %half_weight_grads.7 = bf16[4,4,128,768]{3,2,1,0:T(8,128)(2,1)} custom-call(s32[12]{0:T(128)} %pad_add_fusion.2.table_ref, bf16[1024,1024]{1,0:T(8,128)(2,1)} %get-tuple-element.148.refs_0_, bf16[1024,3072]{1,0:T(8,128)(2,1)} %attend_back.3.refs_1_.triple_ref), custom_call_target="tpu_custom_call" | custom-call | flops 50331648 | bytes 196608 | tf_op jit(solution)/shard_map/half_weight_grads/pallas_call | solution.py:671
  494.5 12.5 %collective-permute-done.11 = bf16[4,128,640]{2,1,0:T(8,128)(2,1)S(1)} collective-permute-done((bf16[4,128,640]{2,1,0:T(8,128)(2,1)}, bf16[4,128,640]{2,1,0:T(8,128)(2,1)S(1)}, u32[]{:S(2)}, u32[]{:S(2)}) %collective-permute-start.11) | collective-permute-done | bytes 655392 | tf_op jit(solution)/shard_map/ppermute | solution.py:822
  507.3 8.8 %collective-permute-done.12 = bf16[4,128,640]{2,1,0:T(8,128)(2,1)S(1)} collective-permute-done((bf16[4,128,640]{2,1,0:T(8,128)(2,1)S(1)}, bf16[4,128,640]{2,1,0:T(8,128)(2,1)S(1)}, u32[]{:S(2)}, u32[]{:S(2)}) %collective-permute-start.12) | collective-permute-done | bytes 655392 | tf_op jit(solution)/shard_map/ppermute | solution.py:822
  517.1 3.7 add_convert_fusion.4
  520.8 2.8 collective-permute-start.15
  523.6 1.6 collective-permute-start.16
  526.2 5.0 collective-permute-start.14
  533.9 20.4 %entry_back.1 = (f32[1024,1024]{1,0:T(8,128)}, f32[512,1024]{1,0:T(8,128)}, f32[16,1024]{1,0:T(8,128)}) custom-call(f32[1024,1024]{1,0:T(8,128)} %get-tuple-element.127.start_ref, bf16[1024,3072]{1,0:T(8,128)(2,1)} %attend_back.3.refs_1_.triple_ref, bf16[512,2048]{1,0:T(8,128)(2,1)} %get-tuple-element.136.refs_4_.pairs_ref, ...), custom_call_target="tpu_custom_call" | custom-call | flops 134217728 | bytes 655360 | tf_op jit(solution)/shard_map/entry_back/pallas_call | solution.py:789
  554.3 3.2 collective-permute-done.17
  557.5 1.3 convert_add_fusion
  558.9 2.1 fusion.9
  561.0 9.0 %collective-permute-done.13 = bf16[2,4,128,384]{3,2,1,0:T(8,128)(2,1)} collective-permute-done((bf16[2,4,128,384]{3,2,1,0:T(8,128)(2,1)S(1)}, bf16[2,4,128,384]{3,2,1,0:T(8,128)(2,1)}, u32[]{:S(2)}, u32[]{:S(2)}) %collective-permute-start.13) | collective-permute-done | bytes 786464 | tf_op jit(solution)/shard_map/ppermute | solution.py:822
  570.0 1.3 fusion.7
  571.3 1.9 collective-permute-start.19
  575.4 1.4 collective-permute-done.18
  576.8 3.9 collective-permute-done.19
  581.8 5.0 collective-permute-done.20
  587.3 1.4 collective-permute-start.22
  588.8 1.8 collective-permute-start.23
  592.3 2.7 collective-permute-start.26
  595.0 4.0 collective-permute-done.24
  599.0 9.5 %collective-permute-done.25 = bf16[128,768]{1,0:T(8,128)(2,1)S(1)} collective-permute-done((bf16[128,768]{1,0:T(8,128)(2,1)S(1)}, bf16[128,768]{1,0:T(8,128)(2,1)S(1)}, u32[]{:S(2)}, u32[]{:S(2)}) %collective-permute-start.25) | collective-permute-done | bytes 196640 | tf_op jit(solution)/shard_map/ppermute | solution.py:822
  609.4 2.8 collective-permute-start.27
  612.8 1.7 collective-permute-start.29
  616.8 1.6 collective-permute-done.29
  620.7 1.1 convert_element_type.604
  (145 shorter events, 34.9 us)
Async XLA Ops:
  7.2 13.3 %copy-start.4 = (bf16[128,1024]{1,0:T(8,128)(2,1)S(1)}, bf16[128,1024]{1,0:T(8,128)(2,1)}, u32[]{:S(2)}) copy-start(bf16[128,1024]{1,0:T(8,128)(2,1)} %param.31) | copy-start | bytes 786436
  7.2 13.3 %copy-start.3 = (bf16[128,1024]{1,0:T(8,128)(2,1)S(1)}, bf16[128,1024]{1,0:T(8,128)(2,1)}, u32[]{:S(2)}) copy-start(bf16[128,1024]{1,0:T(8,128)(2,1)} %param.33) | copy-start | bytes 786436
  7.2 117.4 %all-gather.3.cloned.1.call-start = ((), (), s32[]{:S(2)}) async-start(), calls=%async_computation.1 | async-start | bytes 7569408 | tf_op jit(solution)/shard_map/all_gather | solution.py:817
  11.2 226.2 %all-gather.5.cloned.1.call-start = ((), (), s32[]{:S(2)}) async-start(), calls=%async_computation.2 | async-start | bytes 17301504 | tf_op jit(solution)/shard_map/all_gather | solution.py:817
  14.7 20.5 %collective-permute-start = (bf16[128,1280]{1,0:T(8,128)(2,1)S(1)}, bf16[128,1280]{1,0:T(8,128)(2,1)S(1)}, u32[]{:S(2)}, u32[]{:S(2)}) collective-permute-start(bf16[128,1280]{1,0:T(8,128)(2,1)S(1)} %constant_dynamic-update-slice_fusion), channel_id=1, source_target_pairs={{0,8},{1,9},{2,10},{3,11},{4,12},{5,13},{6,14},{7,15},{8,0},{9,1},... | collective-permute-start | bytes 983048 | tf_op jit(solution)/shard_map/ppermute | solution.py:822
  17.7 30.3 %collective-permute-start.1 = (bf16[128,1280]{1,0:T(8,128)(2,1)S(1)}, bf16[128,1280]{1,0:T(8,128)(2,1)S(1)}, u32[]{:S(2)}, u32[]{:S(2)}) collective-permute-start(bf16[128,1280]{1,0:T(8,128)(2,1)S(1)} %constant_dynamic-update-slice_fusion), channel_id=1, source_target_pairs={{0,16},{1,17},{2,18},{3,19},{4,20},{5,21},{6,22},{7,23},{8,24},{9,... | collective-permute-start | bytes 983048 | tf_op jit(solution)/shard_map/ppermute | solution.py:822
  20.3 27.7 %collective-permute-start.2 = (bf16[128,1280]{1,0:T(8,128)(2,1)S(1)}, bf16[128,1280]{1,0:T(8,128)(2,1)S(1)}, u32[]{:S(2)}, u32[]{:S(2)}) collective-permute-start(bf16[128,1280]{1,0:T(8,128)(2,1)S(1)} %constant_dynamic-update-slice_fusion), channel_id=1, source_target_pairs={{0,24},{1,25},{2,26},{3,27},{4,28},{5,29},{6,30},{7,31},{8,16},{9,... | collective-permute-start | bytes 983048 | tf_op jit(solution)/shard_map/ppermute | solution.py:822
  48.1 572.6 %reduce-scatter.2.cloned.1.call-start = ((), (), s32[]{:S(2)}) async-start(), calls=%async_computation.3 | async-start | bytes 17301504 | tf_op jit(solution)/shard_map/reduce_scatter | solution.py:854
  48.1 42.6 %collective-permute-start.3 = (bf16[4,128,1280]{2,1,0:T(8,128)(2,1)S(1)}, bf16[4,128,1280]{2,1,0:T(8,128)(2,1)S(1)}, u32[]{:S(2)}, u32[]{:S(2)}) collective-permute-start(bf16[4,128,1280]{2,1,0:T(8,128)(2,1)S(1)} %bitcast_dynamic-update-slice_fusion.4), channel_id=1, source_target_pairs={{0,2},{1,3},{2,0},{3,1},{4,6},{5,7},{6,4},{7,5},{8,10},{9,11},{10,... | collective-permute-start | bytes 3932168 | tf_op jit(solution)/shard_map/ppermute | solution.py:822
  49.9 40.9 %collective-permute-start.4 = (bf16[4,128,1280]{2,1,0:T(8,128)(2,1)S(1)}, bf16[4,128,1280]{2,1,0:T(8,128)(2,1)}, u32[]{:S(2)}, u32[]{:S(2)}) collective-permute-start(bf16[4,128,1280]{2,1,0:T(8,128)(2,1)S(1)} %bitcast_dynamic-update-slice_fusion.4), channel_id=1, source_target_pairs={{0,4},{1,5},{2,6},{3,7},{4,0},{5,1},{6,2},{7,3},{8,12},{9,13},{10,... | collective-permute-start | bytes 3932168 | tf_op jit(solution)/shard_map/ppermute | solution.py:822
  51.4 73.2 %collective-permute-start.5 = (bf16[4,128,1280]{2,1,0:T(8,128)(2,1)S(1)}, bf16[4,128,1280]{2,1,0:T(8,128)(2,1)}, u32[]{:S(2)}, u32[]{:S(2)}) collective-permute-start(bf16[4,128,1280]{2,1,0:T(8,128)(2,1)S(1)} %bitcast_dynamic-update-slice_fusion.4), channel_id=1, source_target_pairs={{0,6},{1,7},{2,4},{3,5},{4,2},{5,3},{6,0},{7,1},{8,14},{9,15},{10,... | collective-permute-start | bytes 3932168 | tf_op jit(solution)/shard_map/ppermute | solution.py:822
  129.8 5.1 copy-start.5
  132.4 4.0 copy-start.7
  132.4 5.5 copy-start.10
  134.9 20.0 %collective-permute-start.6 = (bf16[4,4,128,1280]{3,2,1,0:T(8,128)(2,1)}, bf16[4,4,128,1280]{3,2,1,0:T(8,128)(2,1)}, u32[]{:S(2)}, u32[]{:S(2)}) collective-permute-start(bf16[4,4,128,1280]{3,2,1,0:T(8,128)(2,1)} %bitcast_dynamic-update-slice_fusion), channel_id=1, source_target_pairs={{0,1},{1,0},{2,3},{3,2},{4,5},{5,4},{6,7},{7,6},{8,9},{9,8},{10,11... | collective-permute-start | bytes 15728648 | tf_op jit(solution)/shard_map/ppermute | solution.py:822
  325.1 0.7 copy-start.11
  388.5 15.4 %collective-permute-start.7 = (bf16[4,4,128,1280]{3,2,1,0:T(8,128)(2,1)}, bf16[4,4,128,1280]{3,2,1,0:T(8,128)(2,1)}, u32[]{:S(2)}, u32[]{:S(2)}) collective-permute-start(bf16[4,4,128,1280]{3,2,1,0:T(8,128)(2,1)} %half_weight_grads.4), channel_id=1, source_target_pairs={{0,1},{1,0},{2,3},{3,2},{4,5},{5,4},{6,7},{7,6},{8,9},{9,8},{10,11... | collective-permute-start | bytes 15728648 | tf_op jit(solution)/shard_map/ppermute | solution.py:822
  409.7 43.7 %collective-permute-start.9 = (bf16[2,4,128,640]{3,2,1,0:T(8,128)(2,1)S(1)}, bf16[2,4,128,640]{3,2,1,0:T(8,128)(2,1)}, u32[]{:S(2)}, u32[]{:S(2)}) collective-permute-start(bf16[2,4,128,640]{3,2,1,0:T(8,128)(2,1)S(1)} %get-tuple-element.146), channel_id=1, source_target_pairs={{0,4},{1,5},{2,6},{3,7},{4,0},{5,1},{6,2},{7,3},{8,12},{9,13},{10,... | collective-permute-start | bytes 3932168 | tf_op jit(solution)/shard_map/ppermute | solution.py:822
  411.0 59.8 %collective-permute-start.8 = (bf16[2,4,128,640]{3,2,1,0:T(8,128)(2,1)}, bf16[2,4,128,640]{3,2,1,0:T(8,128)(2,1)}, u32[]{:S(2)}, u32[]{:S(2)}) collective-permute-start(bf16[2,4,128,640]{3,2,1,0:T(8,128)(2,1)} %get-tuple-element.144), channel_id=1, source_target_pairs={{0,2},{1,3},{2,0},{3,1},{4,6},{5,7},{6,4},{7,5},{8,10},{9,11},{10,... | collective-permute-start | bytes 3932168 | tf_op jit(solution)/shard_map/ppermute | solution.py:822
  481.6 35.4 %collective-permute-start.10 = (bf16[4,4,128,768]{3,2,1,0:T(8,128)(2,1)}, bf16[4,4,128,768]{3,2,1,0:T(8,128)(2,1)}, u32[]{:S(2)}, u32[]{:S(2)}) collective-permute-start(bf16[4,4,128,768]{3,2,1,0:T(8,128)(2,1)} %half_weight_grads.6), channel_id=1, source_target_pairs={{0,1},{1,0},{2,3},{3,2},{4,5},{5,4},{6,7},{7,6},{8,9},{9,8},{10,11... | collective-permute-start | bytes 9437192 | tf_op jit(solution)/shard_map/ppermute | solution.py:822
  481.7 25.4 %collective-permute-start.11 = (bf16[4,128,640]{2,1,0:T(8,128)(2,1)}, bf16[4,128,640]{2,1,0:T(8,128)(2,1)S(1)}, u32[]{:S(2)}, u32[]{:S(2)}) collective-permute-start(bf16[4,128,640]{2,1,0:T(8,128)(2,1)} %get-tuple-element.152), channel_id=1, source_target_pairs={{0,4},{1,5},{2,6},{3,7},{4,0},{5,1},{6,2},{7,3},{8,12},{9,13},{10,... | collective-permute-start | bytes 1966088 | tf_op jit(solution)/shard_map/ppermute | solution.py:822
  484.6 31.4 %collective-permute-start.12 = (bf16[4,128,640]{2,1,0:T(8,128)(2,1)S(1)}, bf16[4,128,640]{2,1,0:T(8,128)(2,1)S(1)}, u32[]{:S(2)}, u32[]{:S(2)}) collective-permute-start(bf16[4,128,640]{2,1,0:T(8,128)(2,1)S(1)} %get-tuple-element.154), channel_id=1, source_target_pairs={{0,2},{1,3},{2,0},{3,1},{4,6},{5,7},{6,4},{7,5},{8,10},{9,11},{10,... | collective-permute-start | bytes 1966088 | tf_op jit(solution)/shard_map/ppermute | solution.py:822
  507.3 9.8 %copy-start = (bf16[4,4,128,768]{3,2,1,0:T(8,128)(2,1)S(1)}, bf16[4,4,128,768]{3,2,1,0:T(8,128)(2,1)}, u32[]{:S(2)}) copy-start(bf16[4,4,128,768]{3,2,1,0:T(8,128)(2,1)} %half_weight_grads.7) | copy-start | bytes 9437188
  517.0 14.9 %copy-start.9 = (f32[8,1024]{1,0:T(8,128)S(1)}, f32[8,1024]{1,0:T(8,128)}, u32[]{:S(2)}) copy-start(f32[8,1024]{1,0:T(8,128)} %get-tuple-element.169) | copy-start | bytes 98308
  517.0 15.5 %copy-start.8 = (f32[1,4096]{1,0:T(1,128)S(1)}, f32[1,4096]{1,0:T(1,128)}, u32[]{:S(2)}) copy-start(f32[1,4096]{1,0:T(1,128)} %get-tuple-element.170) | copy-start | bytes 49156
  520.8 33.5 %collective-permute-start.15 = (bf16[128,1280]{1,0:T(8,128)(2,1)}, bf16[128,1280]{1,0:T(8,128)(2,1)}, u32[]{:S(2)}, u32[]{:S(2)}) collective-permute-start(bf16[128,1280]{1,0:T(8,128)(2,1)} %pad_maximum_fusion.3), channel_id=1, source_target_pairs={{0,8},{1,9},{2,10},{3,11},{4,12},{5,13},{6,14},{7,15},{8,0},{9,1},... | collective-permute-start | bytes 983048 | tf_op jit(solution)/shard_map/ppermute | solution.py:822
  523.6 30.8 %collective-permute-start.16 = (bf16[128,1280]{1,0:T(8,128)(2,1)S(1)}, bf16[128,1280]{1,0:T(8,128)(2,1)}, u32[]{:S(2)}, u32[]{:S(2)}) collective-permute-start(bf16[128,1280]{1,0:T(8,128)(2,1)S(1)} %pad_maximum_fusion.4), channel_id=1, source_target_pairs={{0,16},{1,17},{2,18},{3,19},{4,20},{5,21},{6,22},{7,23},{8,24},{9,... | collective-permute-start | bytes 983048 | tf_op jit(solution)/shard_map/ppermute | solution.py:822
  525.1 32.4 %collective-permute-start.17 = (bf16[128,1280]{1,0:T(8,128)(2,1)S(1)}, bf16[128,1280]{1,0:T(8,128)(2,1)}, u32[]{:S(2)}, u32[]{:S(2)}) collective-permute-start(bf16[128,1280]{1,0:T(8,128)(2,1)S(1)} %pad_maximum_fusion.5), channel_id=1, source_target_pairs={{0,24},{1,25},{2,26},{3,27},{4,28},{5,29},{6,30},{7,31},{8,16},{9,... | collective-permute-start | bytes 983048 | tf_op jit(solution)/shard_map/ppermute | solution.py:822
  526.2 32.7 %collective-permute-start.14 = (bf16[2,4,128,384]{3,2,1,0:T(8,128)(2,1)}, bf16[2,4,128,384]{3,2,1,0:T(8,128)(2,1)}, u32[]{:S(2)}, u32[]{:S(2)}) collective-permute-start(bf16[2,4,128,384]{3,2,1,0:T(8,128)(2,1)} %get-tuple-element.162), channel_id=1, source_target_pairs={{0,4},{1,5},{2,6},{3,7},{4,0},{5,1},{6,2},{7,3},{8,12},{9,13},{10,... | collective-permute-start | bytes 2359304 | tf_op jit(solution)/shard_map/ppermute | solution.py:822
  533.9 36.1 %collective-permute-start.13 = (bf16[2,4,128,384]{3,2,1,0:T(8,128)(2,1)S(1)}, bf16[2,4,128,384]{3,2,1,0:T(8,128)(2,1)}, u32[]{:S(2)}, u32[]{:S(2)}) collective-permute-start(bf16[2,4,128,384]{3,2,1,0:T(8,128)(2,1)S(1)} %get-tuple-element.160), channel_id=1, source_target_pairs={{0,2},{1,3},{2,0},{3,1},{4,6},{5,7},{6,4},{7,5},{8,10},{9,11},{10,... | collective-permute-start | bytes 2359304 | tf_op jit(solution)/shard_map/ppermute | solution.py:822
  558.9 14.4 %copy-start.6 = (f32[16,1024]{1,0:T(8,128)S(1)}, f32[16,1024]{1,0:T(8,128)}, u32[]{:S(2)}) copy-start(f32[16,1024]{1,0:T(8,128)} %get-tuple-element.167) | copy-start | bytes 196612
  571.3 4.0 copy-start.2
  571.3 9.4 %collective-permute-start.19 = (bf16[4,128,384]{2,1,0:T(8,128)(2,1)S(1)}, bf16[4,128,384]{2,1,0:T(8,128)(2,1)}, u32[]{:S(2)}, u32[]{:S(2)}) collective-permute-start(bf16[4,128,384]{2,1,0:T(8,128)(2,1)S(1)} %get-tuple-element.172), channel_id=1, source_target_pairs={{0,4},{1,5},{2,6},{3,7},{4,0},{5,1},{6,2},{7,3},{8,12},{9,13},{10,... | collective-permute-start | bytes 1179656 | tf_op jit(solution)/shard_map/ppermute | solution.py:822
  575.2 1.6 collective-permute-start.18
  575.3 11.5 %collective-permute-start.20 = (bf16[4,128,384]{2,1,0:T(8,128)(2,1)S(1)}, bf16[4,128,384]{2,1,0:T(8,128)(2,1)S(1)}, u32[]{:S(2)}, u32[]{:S(2)}) collective-permute-start(bf16[4,128,384]{2,1,0:T(8,128)(2,1)S(1)} %copy-done.2), channel_id=1, source_target_pairs={{0,2},{1,3},{2,0},{3,1},{4,6},{5,7},{6,4},{7,5},{8,10},{9,11},{10,... | collective-permute-start | bytes 1179656 | tf_op jit(solution)/shard_map/ppermute | solution.py:822
  587.0 5.3 collective-permute-start.21
  587.3 7.6 %collective-permute-start.22 = (f32[4,27,32]{2,1,0:T(8,128)S(1)}, f32[4,27,32]{2,1,0:T(8,128)S(1)}, u32[]{:S(2)}, u32[]{:S(2)}) collective-permute-start(f32[4,27,32]{2,1,0:T(8,128)S(1)} %get-tuple-element.177), channel_id=1, source_target_pairs={{0,4},{1,5},{2,6},{3,7},{4,0},{5,1},{6,2},{7,3},{8,12},{9,13},{10,... | collective-permute-start | bytes 41480 | tf_op jit(solution)/shard_map/ppermute | solution.py:822
  588.8 6.2 collective-permute-start.23
  590.6 8.4 %collective-permute-start.24 = (bf16[128,768]{1,0:T(8,128)(2,1)S(1)}, bf16[128,768]{1,0:T(8,128)(2,1)S(1)}, u32[]{:S(2)}, u32[]{:S(2)}) collective-permute-start(bf16[128,768]{1,0:T(8,128)(2,1)S(1)} %pad_maximum_fusion.7), channel_id=1, source_target_pairs={{0,8},{1,9},{2,10},{3,11},{4,12},{5,13},{6,14},{7,15},{8,0},{9,1},... | collective-permute-start | bytes 589832 | tf_op jit(solution)/shard_map/ppermute | solution.py:822
  591.6 16.9 %collective-permute-start.25 = (bf16[128,768]{1,0:T(8,128)(2,1)S(1)}, bf16[128,768]{1,0:T(8,128)(2,1)S(1)}, u32[]{:S(2)}, u32[]{:S(2)}) collective-permute-start(bf16[128,768]{1,0:T(8,128)(2,1)S(1)} %pad_maximum_fusion.8), channel_id=1, source_target_pairs={{0,16},{1,17},{2,18},{3,19},{4,20},{5,21},{6,22},{7,23},{8,24},{9,... | collective-permute-start | bytes 589832 | tf_op jit(solution)/shard_map/ppermute | solution.py:822
  592.3 16.2 %collective-permute-start.26 = (bf16[128,768]{1,0:T(8,128)(2,1)S(1)}, bf16[128,768]{1,0:T(8,128)(2,1)S(1)}, u32[]{:S(2)}, u32[]{:S(2)}) collective-permute-start(bf16[128,768]{1,0:T(8,128)(2,1)S(1)} %pad_maximum_fusion.9), channel_id=1, source_target_pairs={{0,24},{1,25},{2,26},{3,27},{4,28},{5,29},{6,30},{7,31},{8,16},{9,... | collective-permute-start | bytes 589832 | tf_op jit(solution)/shard_map/ppermute | solution.py:822
  609.4 6.6 %collective-permute-start.27 = (f32[27,32]{1,0:T(8,128)S(1)}, f32[27,32]{1,0:T(8,128)S(1)}, u32[]{:S(2)}, u32[]{:S(2)}) collective-permute-start(f32[27,32]{1,0:T(8,128)S(1)} %get-tuple-element.184), channel_id=1, source_target_pairs={{0,8},{1,9},{2,10},{3,11},{4,12},{5,13},{6,14},{7,15},{8,0},{9,1},... | collective-permute-start | bytes 10376 | tf_op jit(solution)/shard_map/ppermute | solution.py:822
  612.1 4.6 collective-permute-start.28
  612.8 5.5 collective-permute-start.29
  621.8 1.3 copy-start.1
Sparse Core Ops, SparseCore 0:
  11.4 109.4 all-gather.2
  123.8 113.5 all-gather.4
  325.2 244.3 reduce-scatter.1
